TPU v7x, 32 devices: a whole 2x2x4 slice. The times are simulated.
32 devices in a mesh: groups: 2 (over y), cuts: 4 (over z), rep: 2 (over x), sub: 2 (over core).
Axes of the slice: x: 2, y: 2, z: 4, core: 2. Of those that a mesh axis runs over, the one named last changes fastest.
Arguments:
- features: bfloat16 [4096, 4096], P(('groups', 'rep', 'sub'), 'cuts'), parts along dimension 0, may hold values from -6 to 6
- w_self1: bfloat16 [4096, 512], P('cuts'), may hold values from -0.09375 to 0.09375
- w_neigh1: bfloat16 [4096, 512], P('cuts'), may hold values from -0.09375 to 0.09375
- bias1: float32 [512], replicated, may hold values from -3 to 3
- w_self2: bfloat16 [512, 512], replicated, may hold values from -0.25 to 0.25
- w_neigh2: bfloat16 [512, 512], replicated, may hold values from -0.25 to 0.25
- bias2: float32 [512], replicated, may hold values from -3 to 3
- degree: int32 [8, 512], P(('groups', 'rep', 'sub')), parts along dimension 0, may hold values from 16 to 159
- neighbor_owners: int32 [8, 4, 3], P(('groups', 'rep', 'sub')), parts along dimension 0, may hold values from 0 to 3, as said below
- neighbor_count: int32 [8, 4], P(('groups', 'rep', 'sub')), parts along dimension 0, may hold values from 1 to 3, as said below
- boundary_rows: int32 [8, 4, 3, 32], P(('groups', 'rep', 'sub')), parts along dimension 0, may hold values from 0 to 127, as said below
- boundary_count: int32 [8, 4, 3], P(('groups', 'rep', 'sub')), parts along dimension 0, may hold values from 16 to 32, as said below
- edge_weight: bfloat16 [8, 4, 3, 32, 128], P(('groups', 'rep', 'sub')), parts along dimension 0, may hold values from 0.5 to 1.5
- node_id: int32 [8, 512], P(('groups', 'rep', 'sub'), 'cuts'), parts along dimension 0, may hold values from 0 to 2047, as said below
Outputs:
- embeddings: bfloat16 [4096, 512], P(('groups', 'cuts', 'rep', 'sub')), parts along dimension 0
There are 2 independent parts, one for each index of `groups`. A program takes and returns all parts, laid end to end along the dimension named above; an argument that names none is the same for every part. Nothing has to cross between parts.
Inputs may be any that keep to these rules, and one draw needn't show every extreme that they name: `neighbor_owners`: each list holds 3 distinct owners. `neighbor_count`: every block has an owner whose count is 3. `boundary_rows`: distinct within each list. `boundary_count`: every block has a list whose count is 32. `node_id`: A permutation. Call block b's nodes u * 128 to (u + 1) * 128 - 1 owner (b,u) and ids d * 128 to (d + 1) * 128 - 1 range d; owner (b,u) holds exactly 16 id of each range d with d mod 2 = b mod 2, and none of others.
All inputs are finite; a program needn't handle non-finite values.
Results may differ from a plain program's by a relative error of at most 0.0045.
Values may be sent and summed in bfloat16 or wider, within the bound.
No kernel may reach another device: no remote copies, remote signals or barrier semaphores. Data moves between devices by JAX's collectives and lax.ppermute only.
A program may use at most 64 MiB of HBM per device.

v0:
```python
import jax
import jax.numpy as jnp
from jax import lax
from jax.sharding import PartitionSpec as P


def masked_weights(edge_weights, owner_counts, row_counts):
    neigh_total = edge_weights.shape[1]
    slot_total = edge_weights.shape[2]
    owner_mask = jnp.arange(neigh_total)[None, :] < owner_counts[:, None]
    slot_mask = jnp.arange(slot_total)[None, None, :] < row_counts[:, :, None]
    full_mask = owner_mask[:, :, None] & slot_mask
    return edge_weights * full_mask[:, :, :, None].astype(edge_weights.dtype)


def body(
    features,
    w_self1,
    w_neigh1,
    bias1,
    w_self2,
    w_neigh2,
    bias2,
    degree,
    neighbor_owners,
    neighbor_count,
    boundary_rows,
    boundary_count,
    edge_weight,
    node_id,
):
    cut_count = lax.axis_size("cuts")
    rep_count = lax.axis_size("rep")
    sub_count = lax.axis_size("sub")
    owner_index = lax.axis_index("cuts")
    owner_lists = neighbor_owners[0]
    row_lists = boundary_rows[0]
    edge_weights = edge_weight[0]
    degrees_block = degree[0].astype(jnp.float32)
    feat_width = features.shape[1]
    rows_dev = edge_weights.shape[3]
    slot_cap = edge_weights.shape[2]
    units = w_self1.shape[1]
    live_weights = masked_weights(edge_weights, neighbor_count[0], boundary_count[0])
    send_hits = (owner_lists == owner_index).astype(jnp.int32)
    send_index = jnp.sum(send_hits[:, :, None] * row_lists, axis=1)
    mine_live = lax.dynamic_index_in_dim(live_weights, owner_index, 0, keepdims=False)
    mine_owners = lax.dynamic_index_in_dim(owner_lists, owner_index, 0, keepdims=False)
    owner_onehot = (mine_owners[:, None] == jnp.arange(cut_count)[None, :]).astype(jnp.bfloat16)
    spread = jnp.einsum("ksi,ko->ios", mine_live, owner_onehot, preferred_element_type=jnp.float32)
    spread = spread.reshape(rows_dev, cut_count * slot_cap)
    my_degrees = lax.dynamic_slice_in_dim(degrees_block, owner_index * rows_dev, rows_dev)
    feature_table = features.reshape(cut_count, rows_dev, feat_width)
    picked = feature_table[owner_lists[:, :, None], row_lists]
    summed = jnp.einsum("uksi,uksw->uiw", live_weights, picked, preferred_element_type=jnp.float32)
    summed = summed.reshape(cut_count * rows_dev, feat_width)
    agg_one = summed / degrees_block[:, None]
    own_rows = lax.all_to_all(features, "cuts", split_axis=0, concat_axis=1, tiled=True)
    near_rows = lax.all_to_all(
        agg_one.astype(jnp.bfloat16), "cuts", split_axis=0, concat_axis=1, tiled=True
    ).astype(agg_one.dtype)
    running = jnp.dot(
        own_rows,
        lax.all_gather(w_self1, "cuts", axis=0, tiled=True),
        preferred_element_type=jnp.float32,
    )
    projected = running + jnp.dot(
        near_rows,
        lax.all_gather(w_neigh1, "cuts", axis=0, tiled=True).astype(jnp.float32),
        precision=lax.Precision.HIGHEST,
    )
    layer_one = jnp.maximum(projected + bias1, 0.0).astype(jnp.bfloat16)
    payload = layer_one[send_index]
    received = lax.all_to_all(payload, "cuts", split_axis=0, concat_axis=0, tiled=True)
    spread_half = spread.astype(jnp.bfloat16)
    gathered_sum = jnp.dot(
        spread_half,
        received.reshape(cut_count * slot_cap, units),
        preferred_element_type=jnp.float32,
    )
    agg_two = (gathered_sum / my_degrees[:, None]).astype(jnp.bfloat16)
    z_value = jnp.dot(layer_one, w_self2, preferred_element_type=jnp.float32)
    z_value = z_value + jnp.dot(agg_two, w_neigh2, preferred_element_type=jnp.float32) + bias2
    scale = lax.rsqrt(jnp.mean(z_value * z_value, axis=1, keepdims=True) + 1e-05)
    normalized = (z_value * scale).astype(jnp.bfloat16)
    my_ids = node_id[0]
    dest_device = my_ids // rows_dev
    dest_cut = dest_device // (rep_count * sub_count)
    dest_rep = dest_device // sub_count % rep_count
    dest_peer = dest_cut * rep_count + dest_rep
    sort_order = jnp.argsort(dest_peer, stable=True)
    sorted_rows = normalized[sort_order]
    sorted_ids = my_ids[sort_order]
    peer_total = cut_count * rep_count
    per_peer = rows_dev // peer_total
    arrived_rows, arrived_ids = (
        lax.all_to_all(
            sorted_rows.reshape(peer_total, per_peer, units),
            ("cuts", "rep"),
            split_axis=0,
            concat_axis=0,
            tiled=True,
        ),
        lax.all_to_all(
            sorted_ids.reshape(peer_total, per_peer),
            ("cuts", "rep"),
            split_axis=0,
            concat_axis=0,
            tiled=True,
        ),
    )
    arrived_rows = arrived_rows.reshape(rows_dev, units)
    local_slot = arrived_ids.reshape(rows_dev) % rows_dev
    placement_order = jnp.argsort(local_slot)
    return arrived_rows[placement_order]


def solution(mesh):
    placed = (
        P(("groups", "rep", "sub"), "cuts"),
        P("cuts", None),
        P("cuts", None),
        P(),
        P(),
        P(),
        P(),
        P(("groups", "rep", "sub"), None),
        P(("groups", "rep", "sub"), None, None),
        P(("groups", "rep", "sub"), None),
        P(("groups", "rep", "sub"), None, None, None),
        P(("groups", "rep", "sub"), None, None),
        P(("groups", "rep", "sub"), None, None, None, None),
        P(("groups", "rep", "sub"), "cuts"),
    )
    return jax.shard_map(
        body,
        mesh=mesh,
        in_specs=placed,
        out_specs=P(("groups", "cuts", "rep", "sub"), None),
        check_vma=False,
    )
```

profile of v0, /device:TPU:0, one launch (start us, length us, event | category | flops | bytes accessed | tf_op | source)
XLA Modules:
  0.0 253.5 jit_solution(10137682749723714053)
XLA Ops:
  6.6 0.7 all-gather.3.cloned.1.call-update
  7.3 0.7 all-gather.5.cloned.1.call-update
  8.0 0.7 fusion.25
  8.7 2.5 %sort.34 = (s32[128]{0:T(128)}, s32[128]{0:T(128)S(1)}) sort(s32[128]{0:T(128)S(1)} %fusion.25, s32[128]{0:T(128)S(1)} %iota.24), dimensions={0}, to_apply=%region_2.3 | sort | flops 896 | bytes 2048 | tf_op jit(solution)/shard_map/jit(argsort)/sort | solution.py:91
  11.3 1.6 gather_fusion.3
  12.9 15.2 %all_to_all.54 = s32[8,1,16]{2,1,0:T(1,128)S(1)} all-to-all(s32[8,1,16]{2,1,0:T(1,128)S(1)} %bitcast.78), channel_id=1, replica_groups=mesh['groups'=2,'cuts'=4,'rep'=2,'sub'=2] {'cuts','rep'}, dimensions={0} | all-to-all | bytes 1024 | tf_op jit(solution)/shard_map/all_to_all | solution.py:104
  28.2 3.6 %all-to-all-start = ((bf16[4,128,1024]{2,1,0:T(8,128)(2,1)}), bf16[4,128,1024]{2,1,0:T(8,128)(2,1)S(1)}, u32[]{:S(2)}, u32[]{:S(2)}) async-start(bf16[4,128,1024]{2,1,0:T(8,128)(2,1)} %bitcast.70), calls=%async_computation | async-start | bytes 2097152 | tf_op jit(solution)/shard_map/all_to_all | solution.py:58
  32.3 5.2 %gather_fusion = bf16[384,1024]{1,0:T(8,128)(2,1)S(1)} fusion(bf16[4,128,1024]{2,1,0:T(8,128)(2,1)S(1)} %bitcast.71, s32[384]{0:T(512)S(1)} %reshape.158), kind=kCustom, calls=%fused_computation | custom fusion | bytes 1575936 | tf_op jit(solution)/shard_map/gather | solution.py:54
  37.7 1.0 bitcast_multiply_fusion
  38.7 1.5 fusion
  40.2 45.2 %all-to-all-done = bf16[4,128,1024]{2,1,0:T(8,128)(2,1)S(1)} async-done(((bf16[4,128,1024]{2,1,0:T(8,128)(2,1)}), bf16[4,128,1024]{2,1,0:T(8,128)(2,1)S(1)}, u32[]{:S(2)}, u32[]{:S(2)}) %all-to-all-start) | async-done | bytes 1048608 | tf_op jit(solution)/shard_map/all_to_all | solution.py:58
  85.3 5.5 %all-to-all-start.1 = ((bf16[4,128,1024]{2,1,0:T(8,128)(2,1)}), bf16[4,128,1024]{2,1,0:T(8,128)(2,1)S(1)}, u32[]{:S(2)}, u32[]{:S(2)}) async-start(bf16[4,128,1024]{2,1,0:T(8,128)(2,1)} %fusion), calls=%async_computation.1 | async-start | bytes 2097152 | tf_op jit(solution)/shard_map/all_to_all | solution.py:59
  91.1 0.2 dynamic-slice_reduce_fusion
  91.5 0.5 broadcast.164
  92.0 0.7 reduce.5
  92.8 2.5 %sort.35 = (s32[128]{0:T(128)}, s32[128]{0:T(128)S(1)}) sort(s32[128]{0:T(128)S(1)} %and_select_fusion, s32[128]{0:T(128)S(1)} %iota.25), dimensions={0}, to_apply=%region_3.4 | sort | flops 896 | bytes 2048 | tf_op jit(solution)/shard_map/jit(argsort)/sort | solution.py:114
  95.3 1.4 copy.26
  96.7 36.7 %all-to-all-done.1 = bf16[4,128,1024]{2,1,0:T(8,128)(2,1)S(1)} async-done(((bf16[4,128,1024]{2,1,0:T(8,128)(2,1)}), bf16[4,128,1024]{2,1,0:T(8,128)(2,1)S(1)}, u32[]{:S(2)}, u32[]{:S(2)}) %all-to-all-start.1) | async-done | bytes 1048608 | tf_op jit(solution)/shard_map/all_to_all | solution.py:59
  133.4 0.7 copy.31
  134.0 3.1 %all-gather.3.cloned.1.call-done = bf16[4096,512]{1,0:T(8,128)(2,1)} async-done(((bf16[1024,512]{1,0:T(8,128)(2,1)}), bf16[4096,512]{1,0:T(8,128)(2,1)}) %all-gather.3.cloned.1.call-update) | async-done | bytes 4194320 | tf_op jit(solution)/shard_map/all_gather | solution.py:64
  137.2 3.3 %fusion.31 = f32[128,512]{1,0:T(8,128)S(1)} fusion(bf16[128,4096]{0,1:T(8,128)(2,1)} %bitcast.76, bf16[4096,512]{1,0:T(8,128)(2,1)} %all-gather.3.cloned.1.call-done), kind=kOutput, calls=%fused_computation.74 | convolution fusion | flops 536870912 | bytes 5505024 | tf_op jit(solution)/shard_map/dot_general | solution.py:62
  140.4 77.5 %all-gather.5.cloned.1.call-done = bf16[4096,512]{1,0:T(8,128)(2,1)} async-done(((bf16[1024,512]{1,0:T(8,128)(2,1)}), bf16[4096,512]{1,0:T(8,128)(2,1)}) %all-gather.5.cloned.1.call-update) | async-done | bytes 4194320 | tf_op jit(solution)/shard_map/all_gather | solution.py:69
  217.9 2.9 %fusion.4 = bf16[128,512]{1,0:T(8,128)(2,1)S(1)} fusion(f32[128,512]{1,0:T(8,128)S(1)} %fusion.31, bf16[128,4096]{0,1:T(8,128)(2,1)S(1)} %bitcast.73, bf16[4096,512]{1,0:T(8,128)(2,1)} %all-gather.5.cloned.1.call-done, f32[512]{0:T(512)S(1)} %copy-done.5), kind=kOutput, calls=%fused_computation.13 | convolution fusion | flops 537133056 | bytes 5638144 | tf_op jit(solution)/shard_map/dot_general | solution.py:67
  220.9 1.5 gather_fusion.1
  222.4 3.3 %all-to-all-start.2 = ((bf16[4,32,512]{2,1,0:T(8,128)(2,1)}), bf16[4,32,512]{2,1,0:T(8,128)(2,1)S(1)}, u32[]{:S(2)}, u32[]{:S(2)}) async-start(bf16[4,32,512]{2,1,0:T(8,128)(2,1)} %bitcast.19), calls=%async_computation.2 | async-start | bytes 262144 | tf_op jit(solution)/shard_map/all_to_all | solution.py:74
  225.7 0.2 fusion.32
  226.0 5.9 %all-to-all-done.2 = bf16[4,32,512]{2,1,0:T(8,128)(2,1)S(1)} async-done(((bf16[4,32,512]{2,1,0:T(8,128)(2,1)}), bf16[4,32,512]{2,1,0:T(8,128)(2,1)S(1)}, u32[]{:S(2)}, u32[]{:S(2)}) %all-to-all-start.2) | async-done | bytes 131104 | tf_op jit(solution)/shard_map/all_to_all | solution.py:74
  231.9 0.5 multiply_reduce_fusion
  232.5 1.5 gather_fusion.2
  234.0 3.8 %all-to-all-start.3 = ((bf16[8,16,512]{2,1,0:T(8,128)(2,1)}), bf16[8,16,512]{2,1,0:T(8,128)(2,1)S(1)}, u32[]{:S(2)}, u32[]{:S(2)}) async-start(bf16[8,16,512]{2,1,0:T(8,128)(2,1)} %bitcast.23), calls=%async_computation.3 | async-start | bytes 262144 | tf_op jit(solution)/shard_map/all_to_all | solution.py:97
  237.8 7.3 %all-to-all-done.3 = bf16[8,16,512]{2,1,0:T(8,128)(2,1)S(1)} async-done(((bf16[8,16,512]{2,1,0:T(8,128)(2,1)}), bf16[8,16,512]{2,1,0:T(8,128)(2,1)S(1)}, u32[]{:S(2)}, u32[]{:S(2)}) %all-to-all-start.3) | async-done | bytes 131104 | tf_op jit(solution)/shard_map/all_to_all | solution.py:97
  245.1 1.5 gather_fusion.4
  (52 shorter events, 1.5 us)
Async XLA Ops:
  6.5 225.4 %copy-start = (bf16[512,512]{1,0:T(8,128)(2,1)S(1)}, bf16[512,512]{1,0:T(8,128)(2,1)}, u32[]{:S(2)}) copy-start(bf16[512,512]{1,0:T(8,128)(2,1)} %param.19) | copy-start | bytes 1572868
  6.5 25.8 %copy-start.1 = (bf16[512,1024]{1,0:T(8,128)(2,1)S(1)}, bf16[512,1024]{1,0:T(8,128)(2,1)}, u32[]{:S(2)}) copy-start(bf16[512,1024]{1,0:T(8,128)(2,1)} %param.14) | copy-start | bytes 3145732
  6.5 25.3 %copy-start.7 = (s32[1,4,3]{1,0,2:T(1,128)S(1)}, s32[1,4,3]{1,0,2:T(1,128)}, u32[]{:S(2)}) copy-start(s32[1,4,3]{1,0,2:T(1,128)} %param.25) | copy-start | bytes 148
  6.5 25.4 %copy-start.4 = (s32[1,4,3]{1,0,2:T(1,128)S(1)}, s32[1,4,3]{1,0,2:T(1,128)}, u32[]{:S(2)}) copy-start(s32[1,4,3]{1,0,2:T(1,128)} %param.22) | copy-start | bytes 148
  6.5 25.6 %copy-start.3 = (s32[1,4,3,32]{3,1,2,0:T(4,128)S(1)}, s32[1,4,3,32]{3,1,2,0:T(4,128)}, u32[]{:S(2)}) copy-start(s32[1,4,3,32]{3,1,2,0:T(4,128)} %param.24) | copy-start | bytes 4612
  6.5 130.6 %all-gather.3.cloned.1.call-start = ((), (), s32[]{:S(2)}) async-start(), calls=%async_computation.5 | async-start | bytes 5242880 | tf_op jit(solution)/shard_map/all_gather | solution.py:64
  7.3 210.6 %all-gather.5.cloned.1.call-start = ((), (), s32[]{:S(2)}) async-start(), calls=%async_computation.6 | async-start | bytes 5242880 | tf_op jit(solution)/shard_map/all_gather | solution.py:69
  28.2 9.3 %copy-start.6 = (s32[1,512]{1,0:T(1,128)S(1)}, s32[1,512]{1,0:T(1,128)}, u32[]{:S(2)}) copy-start(s32[1,512]{1,0:T(1,128)} %param.21) | copy-start | bytes 6148
  28.2 9.3 %copy-start.9 = (s32[1,4]{1,0:T(1,128)S(1)}, s32[1,4]{1,0:T(1,128)}, u32[]{:S(2)}) copy-start(s32[1,4]{1,0:T(1,128)} %param.23) | copy-start | bytes 52
  28.2 57.1 %all-to-all-start = ((bf16[4,128,1024]{2,1,0:T(8,128)(2,1)}), bf16[4,128,1024]{2,1,0:T(8,128)(2,1)S(1)}, u32[]{:S(2)}, u32[]{:S(2)}) async-start(bf16[4,128,1024]{2,1,0:T(8,128)(2,1)} %bitcast.70), calls=%async_computation | async-start | bytes 2097152 | tf_op jit(solution)/shard_map/all_to_all | solution.py:58
  85.3 48.1 %all-to-all-start.1 = ((bf16[4,128,1024]{2,1,0:T(8,128)(2,1)}), bf16[4,128,1024]{2,1,0:T(8,128)(2,1)S(1)}, u32[]{:S(2)}, u32[]{:S(2)}) async-start(bf16[4,128,1024]{2,1,0:T(8,128)(2,1)} %fusion), calls=%async_computation.1 | async-start | bytes 2097152 | tf_op jit(solution)/shard_map/all_to_all | solution.py:59
  96.7 121.2 %copy-start.5 = (f32[512]{0:T(512)S(1)}, f32[512]{0:T(512)}, u32[]{:S(2)}) copy-start(f32[512]{0:T(512)} %param.17) | copy-start | bytes 6148
  140.4 85.3 %copy-start.2 = (bf16[512,512]{1,0:T(8,128)(2,1)S(1)}, bf16[512,512]{1,0:T(8,128)(2,1)}, u32[]{:S(2)}) copy-start(bf16[512,512]{1,0:T(8,128)(2,1)} %param.18) | copy-start | bytes 1572868
  140.4 91.5 %copy-start.8 = (f32[512]{0:T(512)S(1)}, f32[512]{0:T(512)}, u32[]{:S(2)}) copy-start(f32[512]{0:T(512)} %param.20) | copy-start | bytes 6148
  222.4 9.5 %all-to-all-start.2 = ((bf16[4,32,512]{2,1,0:T(8,128)(2,1)}), bf16[4,32,512]{2,1,0:T(8,128)(2,1)S(1)}, u32[]{:S(2)}, u32[]{:S(2)}) async-start(bf16[4,32,512]{2,1,0:T(8,128)(2,1)} %bitcast.19), calls=%async_computation.2 | async-start | bytes 262144 | tf_op jit(solution)/shard_map/all_to_all | solution.py:74
  234.0 11.1 %all-to-all-start.3 = ((bf16[8,16,512]{2,1,0:T(8,128)(2,1)}), bf16[8,16,512]{2,1,0:T(8,128)(2,1)S(1)}, u32[]{:S(2)}, u32[]{:S(2)}) async-start(bf16[8,16,512]{2,1,0:T(8,128)(2,1)} %bitcast.23), calls=%async_computation.3 | async-start | bytes 262144 | tf_op jit(solution)/shard_map/all_to_all | solution.py:97
Sparse Core Ops, SparseCore 0:
  9.0 128.1 all-gather.2
  138.7 79.1 all-gather.4
where the time goes:
time: 254 us; the launch traced here: 253 us
  waiting for transfers between devices  177 us (70%)
  starting transfers between devices  16.4 us (6%)
  blocking collectives  15.2 us (6%)
  local copies, waits for them, and re-layouts  14.8 us (6%)
  between operations  13.6 us (5%)
  matrix products  8.49 us (3%)
  other arithmetic  7.9 us (3%)
    all_gather x1, waiting for transfers between devices, body(): lax.all_gather(w_neigh1, 'cuts', axis=0, tiled=True).astype(jnp.float32)  77.5 us
    all_to_all x1, waiting for transfers between devices, body(): lax.all_to_all(features, 'cuts', split_axis=0, concat_axis=1, tiled=True)  45.2 us
    all_to_all x1, waiting for transfers between devices, body(): lax.all_to_all(agg_one.astype(jnp.bfloat16), 'cuts', split_axis=0, concat...  36.7 us
    all_to_all x1, blocking collectives, body(): lax.all_to_all(sorted_ids.reshape(peer_total, per_peer), ('cuts', 'rep'),...  15.2 us
    all_to_all x1, waiting for transfers between devices, body(): lax.all_to_all(sorted_rows.reshape(peer_total, per_peer, units), ('cuts',...  7.32 us
    all_to_all x1, waiting for transfers between devices, body(): lax.all_to_all(payload, 'cuts', split_axis=0, concat_axis=0, tiled=True)  5.93 us
    all_to_all x1, starting transfers between devices, body(): lax.all_to_all(agg_one.astype(jnp.bfloat16), 'cuts', split_axis=0, concat...  5.51 us
    gather x1, local copies, waits for them, and re-layouts, body(): picked = feature_table[owner_lists[:, :, None], row_lists]  5.18 us
  transfers between devices with their start and end apart: 6, of which 6 were waited for; matrix products, arithmetic and copies ran while one was open for 9% of the time, Pallas kernels for 0%

commit v1 on v0

v1 whole, which is shorter than its diff:
```python
import functools

import jax
import jax.numpy as jnp
from jax import lax
from jax.experimental import pallas as pl
from jax.experimental.pallas import tpu as pltpu
from jax.sharding import PartitionSpec as P

F32 = jnp.float32
BF16 = jnp.bfloat16
VMEM = pltpu.VMEM
SMEM = pltpu.SMEM


def partner(index, step, total):
    if total & (total - 1) == 0:
        return index ^ step
    return lax.rem(step - index + 2 * total, total)


def partner_pairs(step, total):
    if total & (total - 1) == 0:
        return [(i, i ^ step) for i in range(total)]
    return [(i, (step - i) % total) for i in range(total)]


def as_column(row):
    n = row.shape[1]
    eye = lax.broadcasted_iota(jnp.int32, (n, n), 0) == lax.broadcasted_iota(jnp.int32, (n, n), 1)
    return jnp.sum(jnp.where(eye, jnp.broadcast_to(row, (n, n)), 0.0), axis=1, keepdims=True)


def live_limit(count_ref, bcount_ref, owner, k):
    return jnp.where(k < count_ref[0, owner], bcount_ref[0, owner, k], 0)


def live_tile(ew_ref, count_ref, bcount_ref, owner):
    _, _, neigh, cap, rows = ew_ref.shape
    slot = lax.broadcasted_iota(jnp.int32, (cap, rows), 0)
    tiles = []
    for k in range(neigh):
        live = slot < live_limit(count_ref, bcount_ref, owner, k)
        tiles.append(jnp.where(live, ew_ref[0, owner, k].astype(F32), 0.0).astype(BF16))
    return jnp.concatenate(tiles, axis=0)


def contract_first(a, b):
    return lax.dot_general(a, b, (((0,), (0,)), ((), ())), preferred_element_type=F32)


def contract_last(a, b):
    return lax.dot_general(a, b, (((1,), (1,)), ((), ())), preferred_element_type=F32)


def first_layer_kernel(
    cuts, owners_ref, count_ref, bcount_ref, x_hbm, wn_hbm, ws_hbm, deg_ref, brow_ref, ew_ref, *rest
):
    outs = rest[:cuts]
    x_v, wn_v, ws_v, pick_v, y_v, s_v, sb_v, sems = rest[cuts:]
    copies = [
        pltpu.make_async_copy(src, dst, sems.at[i])
        for i, (src, dst) in enumerate(((x_hbm, x_v), (wn_hbm, wn_v), (ws_hbm, ws_v)))
    ]
    for copy in copies:
        copy.start()
    _, _, neigh, cap, rows = ew_ref.shape
    total = cuts * rows
    me = lax.axis_index("cuts")
    lane = lax.broadcasted_iota(jnp.int32, (cap, total), 1)
    eye = (
        lax.broadcasted_iota(jnp.int32, (cap, cap), 0) == lax.broadcasted_iota(jnp.int32, (cap, cap), 1)
    ).astype(F32)
    for u in range(cuts):
        columns = contract_last(eye, brow_ref[0, u].astype(F32)).astype(jnp.int32)
        for k in range(neigh):
            target = columns[:, k : k + 1] + owners_ref[0, u, k] * rows
            pick_v[u, k * cap : (k + 1) * cap, :] = (lane == target).astype(F32).astype(BF16)
    copies[0].wait()
    copies[1].wait()
    y_v[...] = jnp.dot(x_v[...], wn_v[...], preferred_element_type=F32).astype(BF16)
    copies[2].wait()
    s_v[...] = jnp.dot(x_v[...], ws_v[...], preferred_element_type=F32)
    for u in range(cuts):
        at = slice(u * rows, (u + 1) * rows)
        picked = jnp.dot(pick_v[u], y_v[...], preferred_element_type=F32).astype(BF16)
        summed = contract_first(live_tile(ew_ref, count_ref, bcount_ref, u), picked)
        scale = as_column(1.0 / deg_ref[:, at].astype(F32))
        sb_v[at, :] = (s_v[at, :] + summed * scale).astype(BF16)
    for step in range(cuts):
        u = partner(me, step, cuts)
        outs[step][:rows, :] = sb_v[pl.ds(pl.multiple_of(u * rows, rows), rows), :]
        outs[step][rows:, :] = jnp.dot(pick_v[u], sb_v[...], preferred_element_type=F32).astype(BF16)


def second_layer_kernel(cuts, reps, subs, count_ref, bcount_ref, *rest):
    slabs = rest[:cuts]
    b1_ref, ws_ref, wn_ref, b2_ref, deg_ref, ew_ref, id_ref, out_ref = rest[cuts:]
    rows = ew_ref.shape[4]
    units = ws_ref.shape[0]
    me = lax.axis_index("cuts")
    total = slabs[0][...].astype(F32)
    for slab in slabs[1:]:
        total = total + slab[...].astype(F32)
    hidden = jnp.maximum(total + b1_ref[...], 0.0).astype(BF16)
    own, border = hidden[:rows], hidden[rows:]
    summed = contract_first(live_tile(ew_ref, count_ref, bcount_ref, me), border)
    degrees = deg_ref[:, pl.ds(pl.multiple_of(me * rows, rows), rows)].astype(F32)
    mean = (summed * as_column(1.0 / degrees)).astype(BF16)
    z = jnp.dot(own, ws_ref[...], preferred_element_type=F32)
    z = z + jnp.dot(mean, wn_ref[...], preferred_element_type=F32) + b2_ref[...]
    scale = lax.rsqrt(jnp.mean(z * z, axis=1, keepdims=True) + 1e-05)
    normalized = (z * scale).astype(BF16)
    ids = id_ref[...]
    device = ids // rows
    peer = (device // (reps * subs)) * reps + (device // subs) % reps
    slot = (ids - device * rows).astype(F32)
    peer_f = peer.astype(F32)
    down = lax.broadcasted_iota(jnp.int32, (rows, rows), 0)
    across = lax.broadcasted_iota(jnp.int32, (rows, rows), 1)
    earlier = (as_column(peer_f) == peer_f) & (down < across)
    rank = jnp.sum(earlier.astype(F32), axis=0, keepdims=True).astype(jnp.int32)
    place = peer * (rows // (cuts * reps)) + rank
    chosen = down == place
    out_ref[:, :units] = jnp.dot(chosen.astype(F32).astype(BF16), normalized, preferred_element_type=F32).astype(BF16)
    slots = jnp.sum(jnp.where(chosen, slot, 0.0), axis=1, keepdims=True)
    out_ref[:, units:] = jnp.broadcast_to(slots, (rows, rows)).astype(BF16)


def placing_kernel(in_ref, out_ref):
    rows, units = out_ref.shape
    across = lax.broadcasted_iota(jnp.int32, (rows, rows), 1)
    chosen = in_ref[:, units:].astype(F32).astype(jnp.int32) == across
    out_ref[...] = contract_first(chosen.astype(F32).astype(BF16), in_ref[:, :units]).astype(BF16)


def body(
    features,
    w_self1,
    w_neigh1,
    bias1,
    w_self2,
    w_neigh2,
    bias2,
    degree,
    neighbor_owners,
    neighbor_count,
    boundary_rows,
    boundary_count,
    edge_weight,
    node_id,
):
    cuts, reps, subs = (lax.axis_size(a) for a in ("cuts", "rep", "sub"))
    total, width = features.shape
    units = w_self1.shape[1]
    _, _, neigh, cap, rows = edge_weight.shape
    border = neigh * cap
    smem = pl.BlockSpec(memory_space=SMEM)
    vmem = pl.BlockSpec(memory_space=VMEM)
    hbm = pl.BlockSpec(memory_space=pl.ANY)
    slab = jax.ShapeDtypeStruct((rows + border, units), BF16)
    held = 2 * (total * width + 2 * width * units + cuts * border * total + 4 * total * units)
    held += 2 * cuts * (rows + border) * units + 8 * total * units
    slabs = pl.pallas_call(
        functools.partial(first_layer_kernel, cuts),
        out_shape=[slab] * cuts,
        in_specs=[smem] * 3 + [hbm] * 3 + [vmem] * 3,
        out_specs=[vmem] * cuts,
        scratch_shapes=[
            pltpu.VMEM((total, width), BF16),
            pltpu.VMEM((width, units), BF16),
            pltpu.VMEM((width, units), BF16),
            pltpu.VMEM((cuts, border, total), BF16),
            pltpu.VMEM((total, units), BF16),
            pltpu.VMEM((total, units), F32),
            pltpu.VMEM((total, units), BF16),
            pltpu.SemaphoreType.DMA((3,)),
        ],
        compiler_params=pltpu.CompilerParams(vmem_limit_bytes=held + (8 << 20)),
        name="first_layer",
    )(neighbor_owners, neighbor_count, boundary_count, features, w_neigh1, w_self1, degree, boundary_rows, edge_weight)
    arrived = [slabs[0]]
    order = sorted(range(1, cuts), key=lambda s: (-(s & (s - 1)) if s > 1 else 1, s))
    got = {s: lax.ppermute(slabs[s], "cuts", partner_pairs(s, cuts)) for s in order}
    arrived += [got[s] for s in range(1, cuts)]
    payload = pl.pallas_call(
        functools.partial(second_layer_kernel, cuts, reps, subs),
        out_shape=jax.ShapeDtypeStruct((rows, units + rows), BF16),
        in_specs=[smem] * 2 + [vmem] * (cuts + 7),
        out_specs=vmem,
        compiler_params=pltpu.CompilerParams(vmem_limit_bytes=24 << 20),
        name="second_layer",
    )(
        neighbor_count,
        boundary_count,
        *arrived,
        bias1.reshape(1, units),
        w_self2,
        w_neigh2,
        bias2.reshape(1, units),
        degree,
        edge_weight,
        node_id,
    )
    peers = cuts * reps
    moved = lax.all_to_all(
        payload.reshape(peers, rows // peers, units + rows), ("cuts", "rep"), split_axis=0, concat_axis=0, tiled=True
    )
    return pl.pallas_call(
        placing_kernel,
        out_shape=jax.ShapeDtypeStruct((rows, units), BF16),
        in_specs=[vmem],
        out_specs=vmem,
        name="placing",
    )(moved.reshape(rows, units + rows))


def solution(mesh):
    block = ("groups", "rep", "sub")
    placed = (
        P(block, "cuts"),
        P("cuts", None),
        P("cuts", None),
        P(),
        P(),
        P(),
        P(),
        P(block, None),
        P(block, None, None),
        P(block, None),
        P(block, None, None, None),
        P(block, None, None),
        P(block, None, None, None, None),
        P(block, "cuts"),
    )
    return jax.shard_map(
        body,
        mesh=mesh,
        in_specs=placed,
        out_specs=P(("groups", "cuts", "rep", "sub"), None),
        check_vma=False,
    )
```

time: 254 us -> 52 us (0.20)
  waiting for transfers between devices: 177 us -> 16.7 us
  between operations: 13.6 us -> 0.07 us
  starting transfers between devices: 16.4 us -> 5.68 us
  matrix products: 8.49 us -> 0 us
  other arithmetic: 7.9 us -> 0 us
  local copies, waits for them, and re-layouts: 14.8 us -> 7.47 us
  Pallas kernels: 0 us -> 6.98 us
    all_to_all x4 -> x0, waiting for transfers between devices: 95.1 us -> none  [the longest x1 45.2 us: body(): lax.all_to_all(features, 'cuts', split_axis=0, concat_axis=1, tiled=True)]
    all_gather x2 -> x0, waiting for transfers between devices: 80.6 us -> none  [the longest x1 77.5 us: body(): lax.all_gather(w_neigh1, 'cuts', axis=0, tiled=True).astype(jnp.float32)]
    ppermute x0 -> x3, waiting for transfers between devices: none -> 16.7 us  [body(): lax.ppermute(slabs[s], 'cuts', partner_pairs(s, cuts))]
    all_to_all x4 -> x0, starting transfers between devices: 16.3 us -> none  [the longest x1 5.51 us: body(): lax.all_to_all(agg_one.astype(jnp.bfloat16), 'cuts', split_axis=0, concat...]
    gather x5 -> x0, local copies, waits for them, and re-layouts: 11.3 us -> none  [the longest x1 5.18 us: body(): picked = feature_table[owner_lists[:, :, None], row_lists]]
    dot_general x6 -> x0, matrix products: 8.49 us -> none  [the longest x1 3.26 us: body(): jnp.dot(own_rows, lax.all_gather(w_self1, 'cuts', axis=0, tiled=True), pr...]
    unnamed x22 -> x29, local copies, waits for them, and re-layouts: 0.23 us -> 7.47 us
    pallas_call x0 -> x3, Pallas kernels: none -> 6.98 us  [the longest x1 3.91 us: body(): pl.pallas_call(functools.partial(first_layer_kernel, cuts), out_shape=[sl...]
  transfers between devices with their start and end apart: 6 -> 3, of which waited for: 6 -> 2; matrix products, arithmetic and copies ran while one was open for 9% -> 0% of each run, Pallas kernels for 0% -> 0%
where the time goes in v1:
time: 52 us; the launch traced here: 51.6 us
  waiting for transfers between devices  16.7 us (32%)
  blocking collectives  14.7 us (28%)
  local copies, waits for them, and re-layouts  7.47 us (14%)
  Pallas kernels  6.98 us (13%)
  starting transfers between devices  5.68 us (11%)
    ppermute x3, waiting for transfers between devices, body(): lax.ppermute(slabs[s], 'cuts', partner_pairs(s, cuts))  16.7 us
    all_to_all x1, blocking collectives, body(): lax.all_to_all(payload.reshape(peers, rows // peers, units + rows), ('cut...  14.7 us
    unnamed x29, local copies, waits for them, and re-layouts  7.47 us
    ppermute x3, starting transfers between devices, body(): lax.ppermute(slabs[s], 'cuts', partner_pairs(s, cuts))  5.68 us
    pallas_call x1, Pallas kernels, body(): pl.pallas_call(functools.partial(first_layer_kernel, cuts), out_shape=[sl...  3.91 us
    pallas_call x1, Pallas kernels, body(): pl.pallas_call(placing_kernel, out_shape=jax.ShapeDtypeStruct((rows, unit...  1.78 us
    pallas_call x1, Pallas kernels, body(): pl.pallas_call(functools.partial(second_layer_kernel, cuts, reps, subs),...  1.29 us
  transfers between devices with their start and end apart: 3, of which 2 were waited for; matrix products, arithmetic and copies ran while one was open for 0% of the time, Pallas kernels for 0%

profile of v1, /device:TPU:0, one launch (start us, length us, event | category | flops | bytes accessed | tf_op | source)
XLA Modules:
  0.0 51.6 jit_solution(9394528013584718959)
XLA Ops:
  0.0 0.0 copy-start.12
  0.0 0.8 %copy.18.bcount_ref = s32[1,4,3]{2,1,0:T(4,128)S(1)} copy(s32[1,4,3]{1,0,2:T(1,128)} %param.25) | data formatting | bytes 96 | tf_op args[11]
  0.8 0.8 %copy.15.owners_ref = s32[1,4,3]{2,1,0:T(4,128)S(1)} copy(s32[1,4,3]{1,0,2:T(1,128)} %param.22) | data formatting | bytes 96 | tf_op args[8]
  1.5 0.0 copy-done.12
  1.6 0.0 copy-start.7
  1.6 0.0 copy-start.10
  1.6 0.7 %copy-done.7 = s32[1,512]{1,0:T(1,128)S(1)} copy-done((s32[1,512]{1,0:T(1,128)S(1)}, s32[1,512]{1,0:T(1,128)}, u32[]{:S(2)}) %copy-start.7) | copy-done | bytes 2072
  2.2 0.0 copy-done.10
  2.2 0.0 copy-start
  2.2 1.2 %copy-done = bf16[512,1024]{1,0:T(8,128)(2,1)S(1)} copy-done((bf16[512,1024]{1,0:T(8,128)(2,1)S(1)}, bf16[512,1024]{1,0:T(8,128)(2,1)}, u32[]{:S(2)}) %copy-start) | copy-done | bytes 1048600
  3.5 0.0 copy-start.1
  3.5 1.2 %copy-done.1 = bf16[1024,512]{1,0:T(8,128)(2,1)S(1)} copy-done((bf16[1024,512]{1,0:T(8,128)(2,1)S(1)}, bf16[1024,512]{1,0:T(8,128)(2,1)}, u32[]{:S(2)}) %copy-start.1) | copy-done | bytes 1048600
  4.7 0.0 copy-start.2
  4.7 1.2 %copy-done.2 = bf16[1024,512]{1,0:T(8,128)(2,1)S(1)} copy-done((bf16[1024,512]{1,0:T(8,128)(2,1)S(1)}, bf16[1024,512]{1,0:T(8,128)(2,1)}, u32[]{:S(2)}) %copy-start.2) | copy-done | bytes 1048600
  5.9 0.0 copy-start.5
  5.9 0.9 %copy-done.5 = bf16[1,4,3,32,128]{4,3,2,1,0:T(8,128)(2,1)S(1)} copy-done((bf16[1,4,3,32,128]{4,3,2,1,0:T(8,128)(2,1)S(1)}, bf16[1,4,3,32,128]{4,3,2,1,0:T(8,128)(2,1)}, u32[]{:S(2)}) %copy-start.5) | copy-done | bytes 98328
  6.8 3.9 %first_layer.1 = (bf16[224,512]{1,0:T(8,128)(2,1)S(1)}, bf16[224,512]{1,0:T(8,128)(2,1)S(1)}, bf16[224,512]{1,0:T(8,128)(2,1)S(1)}, bf16[224,512]{1,0:T(8,128)(2,1)S(1)}) custom-call(s32[1,4,3]{2,1,0:T(4,128)S(1)} %copy.15.owners_ref, s32[1,4]{1,0:T(1,128)S(1)} %copy-done.10, s32[1,4,3]{2,1,0:T(4,128)S(1)} %copy.18.bcount_ref, ...), custom_call_target="tpu_custom_call" | custom-call | tf_op jit(solution)/shard_map/first_layer/pallas_call | solution.py:164
  10.7 3.1 %collective-permute-start = (bf16[224,512]{1,0:T(8,128)(2,1)S(1)}, bf16[224,512]{1,0:T(8,128)(2,1)S(1)}, u32[]{:S(2)}, u32[]{:S(2)}) collective-permute-start(bf16[224,512]{1,0:T(8,128)(2,1)S(1)} %get-tuple-element.10), channel_id=1, source_target_pairs={{0,4},{4,0},{8,12},{12,8},{1,5},{5,1},{9,13},{13,9},{2,6},{6,2},{1... | collective-permute-start | bytes 688136 | tf_op jit(solution)/shard_map/ppermute | solution.py:184
  13.8 2.6 %collective-permute-start.1 = (bf16[224,512]{1,0:T(8,128)(2,1)S(1)}, bf16[224,512]{1,0:T(8,128)(2,1)S(1)}, u32[]{:S(2)}, u32[]{:S(2)}) collective-permute-start(bf16[224,512]{1,0:T(8,128)(2,1)S(1)} %get-tuple-element.11), channel_id=1, source_target_pairs={{0,8},{4,12},{8,0},{12,4},{1,9},{5,13},{9,1},{13,5},{2,10},{6,14},... | collective-permute-start | bytes 688136 | tf_op jit(solution)/shard_map/ppermute | solution.py:184
  16.4 0.0 collective-permute-start.2
  16.4 7.2 %collective-permute-done.rest_1_ = bf16[224,512]{1,0:T(8,128)(2,1)S(1)} collective-permute-done((bf16[224,512]{1,0:T(8,128)(2,1)S(1)}, bf16[224,512]{1,0:T(8,128)(2,1)S(1)}, u32[]{:S(2)}, u32[]{:S(2)}) %collective-permute-start) | collective-permute-done | bytes 229408 | tf_op jit(solution)/shard_map/ppermute | solution.py:184
  23.6 9.5 %collective-permute-done.1.rest_2_ = bf16[224,512]{1,0:T(8,128)(2,1)S(1)} collective-permute-done((bf16[224,512]{1,0:T(8,128)(2,1)S(1)}, bf16[224,512]{1,0:T(8,128)(2,1)S(1)}, u32[]{:S(2)}, u32[]{:S(2)}) %collective-permute-start.1) | collective-permute-done | bytes 229408 | tf_op jit(solution)/shard_map/ppermute | solution.py:184
  33.1 0.0 collective-permute-done.2.rest_3_
  33.1 0.0 copy-done.3
  33.1 0.0 copy-done.4
  33.1 0.0 copy-done.6
  33.1 0.6 %copy-done.9 = f32[512]{0:T(512)S(1)} copy-done((f32[512]{0:T(512)S(1)}, f32[512]{0:T(512)}, u32[]{:S(2)}) %copy-start.9) | copy-done | bytes 2072
  33.8 0.0 copy-done.8
  33.8 0.0 copy-done.11
  33.8 1.3 %second_layer.1 = bf16[128,640]{1,0:T(8,128)(2,1)S(1)} custom-call(s32[1,4]{1,0:T(1,128)S(1)} %copy-done.10, s32[1,4,3]{2,1,0:T(4,128)S(1)} %copy.18.bcount_ref, bf16[224,512]{1,0:T(8,128)(2,1)S(1)} %get-tuple-element.9.rest_0_, bf16[224,512]{1,0:T(8,128)(2,1)S(1)} %collective-permute-done.rest_1_, bf16[224,512]{1,0:T(8,128)(2,1)S(1)} %collective-permute-done.1.rest_2_, ...), custom_call_target="tpu_custom_call" | custom-call | tf_op jit(solution)/shard_map/second_layer/pallas_call | solution.py:186
  35.1 14.7 %all_to_all.5 = bf16[8,16,640]{2,1,0:T(8,128)(2,1)} all-to-all(bf16[8,16,640]{2,1,0:T(8,128)(2,1)S(1)} %bitcast.4), channel_id=1, replica_groups=mesh['groups'=2,'cuts'=4,'rep'=2,'sub'=2] {'cuts','rep'}, dimensions={0} | all-to-all | bytes 327680 | tf_op jit(solution)/shard_map/all_to_all | solution.py:206
  49.8 1.8 %placing.1 = bf16[128,512]{1,0:T(8,128)(2,1)} custom-call(bf16[128,640]{1,0:T(8,128)(2,1)} %bitcast.7), custom_call_target="tpu_custom_call" | custom-call | tf_op jit(solution)/shard_map/placing/pallas_call | solution.py:209
  (7 shorter events, 0.0 us)
Async XLA Ops:
  0.0 1.6 %copy-start.12 = (s32[1,4,3,32]{3,1,2,0:T(4,128)S(1)}, s32[1,4,3,32]{3,1,2,0:T(4,128)}, u32[]{:S(2)}) copy-start(s32[1,4,3,32]{3,1,2,0:T(4,128)} %param.24) | copy-start | bytes 4612
  1.6 0.7 %copy-start.7 = (s32[1,512]{1,0:T(1,128)S(1)}, s32[1,512]{1,0:T(1,128)}, u32[]{:S(2)}) copy-start(s32[1,512]{1,0:T(1,128)} %rest_8_.1) | copy-start | bytes 6148
  1.6 0.7 %copy-start.10 = (s32[1,4]{1,0:T(1,128)S(1)}, s32[1,4]{1,0:T(1,128)}, u32[]{:S(2)}) copy-start(s32[1,4]{1,0:T(1,128)} %count_ref.3) | copy-start | bytes 52
  2.2 1.2 %copy-start = (bf16[512,1024]{1,0:T(8,128)(2,1)S(1)}, bf16[512,1024]{1,0:T(8,128)(2,1)}, u32[]{:S(2)}) copy-start(bf16[512,1024]{1,0:T(8,128)(2,1)} %x_hbm.1) | copy-start | bytes 3145732
  3.5 1.2 %copy-start.1 = (bf16[1024,512]{1,0:T(8,128)(2,1)S(1)}, bf16[1024,512]{1,0:T(8,128)(2,1)}, u32[]{:S(2)}) copy-start(bf16[1024,512]{1,0:T(8,128)(2,1)} %wn_hbm.1) | copy-start | bytes 3145732
  4.7 1.2 %copy-start.2 = (bf16[1024,512]{1,0:T(8,128)(2,1)S(1)}, bf16[1024,512]{1,0:T(8,128)(2,1)}, u32[]{:S(2)}) copy-start(bf16[1024,512]{1,0:T(8,128)(2,1)} %ws_hbm.1) | copy-start | bytes 3145732
  5.9 0.9 %copy-start.5 = (bf16[1,4,3,32,128]{4,3,2,1,0:T(8,128)(2,1)S(1)}, bf16[1,4,3,32,128]{4,3,2,1,0:T(8,128)(2,1)}, u32[]{:S(2)}) copy-start(bf16[1,4,3,32,128]{4,3,2,1,0:T(8,128)(2,1)} %rest_9_.1) | copy-start | bytes 294916
  6.8 26.3 %copy-start.3 = (bf16[512,512]{1,0:T(8,128)(2,1)S(1)}, bf16[512,512]{1,0:T(8,128)(2,1)}, u32[]{:S(2)}) copy-start(bf16[512,512]{1,0:T(8,128)(2,1)} %rest_5_.1) | copy-start | bytes 1572868
  6.8 26.3 %copy-start.4 = (bf16[512,512]{1,0:T(8,128)(2,1)S(1)}, bf16[512,512]{1,0:T(8,128)(2,1)}, u32[]{:S(2)}) copy-start(bf16[512,512]{1,0:T(8,128)(2,1)} %rest_6_.1) | copy-start | bytes 1572868
  6.8 26.3 %copy-start.6 = (bf16[1,4,3,32,128]{4,3,2,1,0:T(8,128)(2,1)S(1)}, bf16[1,4,3,32,128]{4,3,2,1,0:T(8,128)(2,1)}, u32[]{:S(2)}) copy-start(bf16[1,4,3,32,128]{4,3,2,1,0:T(8,128)(2,1)} %rest_9_.1) | copy-start | bytes 294916
  10.7 12.8 %collective-permute-start = (bf16[224,512]{1,0:T(8,128)(2,1)S(1)}, bf16[224,512]{1,0:T(8,128)(2,1)S(1)}, u32[]{:S(2)}, u32[]{:S(2)}) collective-permute-start(bf16[224,512]{1,0:T(8,128)(2,1)S(1)} %get-tuple-element.10), channel_id=1, source_target_pairs={{0,4},{4,0},{8,12},{12,8},{1,5},{5,1},{9,13},{13,9},{2,6},{6,2},{1... | collective-permute-start | bytes 688136 | tf_op jit(solution)/shard_map/ppermute | solution.py:184
  13.8 19.3 %collective-permute-start.1 = (bf16[224,512]{1,0:T(8,128)(2,1)S(1)}, bf16[224,512]{1,0:T(8,128)(2,1)S(1)}, u32[]{:S(2)}, u32[]{:S(2)}) collective-permute-start(bf16[224,512]{1,0:T(8,128)(2,1)S(1)} %get-tuple-element.11), channel_id=1, source_target_pairs={{0,8},{4,12},{8,0},{12,4},{1,9},{5,13},{9,1},{13,5},{2,10},{6,14},... | collective-permute-start | bytes 688136 | tf_op jit(solution)/shard_map/ppermute | solution.py:184
  16.4 16.7 %collective-permute-start.2 = (bf16[224,512]{1,0:T(8,128)(2,1)S(1)}, bf16[224,512]{1,0:T(8,128)(2,1)S(1)}, u32[]{:S(2)}, u32[]{:S(2)}) collective-permute-start(bf16[224,512]{1,0:T(8,128)(2,1)S(1)} %get-tuple-element.12), channel_id=1, source_target_pairs={{0,12},{4,8},{8,4},{12,0},{1,13},{5,9},{9,5},{13,1},{2,14},{6,10},... | collective-permute-start | bytes 688136 | tf_op jit(solution)/shard_map/ppermute | solution.py:184
  33.1 0.7 %copy-start.9 = (f32[512]{0:T(512)S(1)}, f32[512]{0:T(512)}, u32[]{:S(2)}) copy-start(f32[512]{0:T(512)} %param.20) | copy-start | bytes 6148
  33.1 0.7 %copy-start.8 = (f32[512]{0:T(512)S(1)}, f32[512]{0:T(512)}, u32[]{:S(2)}) copy-start(f32[512]{0:T(512)} %param.17) | copy-start | bytes 6148
  33.1 0.7 %copy-start.11 = (s32[1,128]{1,0:T(1,128)S(1)}, s32[1,128]{1,0:T(1,128)}, u32[]{:S(2)}) copy-start(s32[1,128]{1,0:T(1,128)} %rest_10_.1) | copy-start | bytes 1540

commit v2 on v1

v2 whole, which is shorter than its diff:
```python
import functools

import jax
import jax.numpy as jnp
from jax import lax
from jax.experimental import pallas as pl
from jax.experimental.pallas import tpu as pltpu
from jax.sharding import PartitionSpec as P

F32 = jnp.float32
BF16 = jnp.bfloat16
VMEM = pltpu.VMEM
SMEM = pltpu.SMEM


def partner(index, step, total):
    if total & (total - 1) == 0:
        return index ^ step
    return lax.rem(step - index + 2 * total, total)


def partner_pairs(step, total):
    if total & (total - 1) == 0:
        return [(i, i ^ step) for i in range(total)]
    return [(i, (step - i) % total) for i in range(total)]


def as_column(row):
    n = row.shape[1]
    eye = lax.broadcasted_iota(jnp.int32, (n, n), 0) == lax.broadcasted_iota(jnp.int32, (n, n), 1)
    return jnp.sum(jnp.where(eye, jnp.broadcast_to(row, (n, n)), 0.0), axis=1, keepdims=True)


def live_limit(count_ref, bcount_ref, owner, k):
    return jnp.where(k < count_ref[0, owner], bcount_ref[k, 0, owner], 0)


def live_tile(tile, count_ref, bcount_ref, owner):
    neigh, cap, rows = tile.shape
    slot = lax.broadcasted_iota(jnp.int32, (cap, rows), 0)
    tiles = []
    for k in range(neigh):
        live = slot < live_limit(count_ref, bcount_ref, owner, k)
        tiles.append(jnp.where(live, tile[k].astype(F32), 0.0).astype(BF16))
    return jnp.concatenate(tiles, axis=0)


def contract_first(a, b):
    return lax.dot_general(a, b, (((0,), (0,)), ((), ())), preferred_element_type=F32)


def contract_last(a, b):
    return lax.dot_general(a, b, (((1,), (1,)), ((), ())), preferred_element_type=F32)


def in_hbm(*arrays):
    return [pltpu.with_memory_space_constraint(a, pltpu.HBM) for a in arrays]


def start_all(pairs, sems):
    copies = [pltpu.make_async_copy(src, dst, sems.at[i]) for i, (src, dst) in enumerate(pairs)]
    for copy in copies:
        copy.start()
    return copies


def fill_slab(out_ref, sums_ref, pick_ref, owner, rows):
    out_ref[:rows, :] = sums_ref[pl.ds(pl.multiple_of(owner * rows, rows), rows), :]
    out_ref[rows:, :] = jnp.dot(pick_ref[owner], sums_ref[...], preferred_element_type=F32).astype(BF16)


def first_layer_kernel(
    cuts, far, owners_hbm, count_hbm, bcount_hbm, x_hbm, wn_hbm, ws_hbm, deg_hbm, brow_hbm, ew_hbm, *rest
):
    outs, (sums_ref, pick_ref) = rest[: len(far)], rest[len(far) : len(far) + 2]
    owners_ref, count_ref, bcount_ref, brow_v, deg_v, x_v, wn_v, ws_v, ew_v, y_v, s_v, sems = rest[len(far) + 2 :]
    pairs = (
        (brow_hbm, brow_v),
        (owners_hbm, owners_ref),
        (x_hbm, x_v),
        (wn_hbm, wn_v),
        (count_hbm, count_ref),
        (bcount_hbm, bcount_ref),
        (deg_hbm, deg_v),
        (ws_hbm, ws_v),
        (ew_hbm, ew_v),
    )
    brow_in, owners_in, x_in, wn_in, *counts_in, deg_in, ws_in, ew_in = start_all(pairs, sems)
    _, _, neigh, cap, rows = ew_v.shape
    total = cuts * rows
    me = lax.axis_index("cuts")
    lane = lax.broadcasted_iota(jnp.int32, (cap, total), 1)
    eye = (
        lax.broadcasted_iota(jnp.int32, (cap, cap), 0) == lax.broadcasted_iota(jnp.int32, (cap, cap), 1)
    ).astype(F32)
    brow_in.wait()
    owners_in.wait()
    for k in range(neigh):
        columns = contract_last(eye, brow_v[0, k].astype(F32)).astype(jnp.int32)
        for u in range(cuts):
            target = columns[:, u : u + 1] + owners_ref[k, 0, u] * rows
            pick_ref[u, k * cap : (k + 1) * cap, :] = (lane == target).astype(F32).astype(BF16)
    x_in.wait()
    wn_in.wait()
    y_v[...] = jnp.dot(x_v[...], wn_v[...], preferred_element_type=F32).astype(BF16)
    ws_in.wait()
    s_v[...] = jnp.dot(x_v[...], ws_v[...], preferred_element_type=F32)
    for copy in (*counts_in, deg_in, ew_in):
        copy.wait()
    for u in range(cuts):
        at = slice(u * rows, (u + 1) * rows)
        picked = jnp.dot(pick_ref[u], y_v[...], preferred_element_type=F32).astype(BF16)
        summed = contract_first(live_tile(ew_v[0, u], count_ref, bcount_ref, u), picked)
        scale = as_column(1.0 / deg_v[:, at].astype(F32))
        sums_ref[at, :] = (s_v[at, :] + summed * scale).astype(BF16)
    for step, out_ref in zip(far, outs):
        fill_slab(out_ref, sums_ref, pick_ref, partner(me, step, cuts), rows)


def near_kernel(
    cuts,
    reps,
    subs,
    near,
    sums_ref,
    pick_ref,
    count_hbm,
    bcount_hbm,
    ws_hbm,
    wn_hbm,
    b1_hbm,
    b2_hbm,
    deg_hbm,
    ew_hbm,
    id_hbm,
    *rest,
):
    outs, rest = rest[: len(near)], rest[len(near) :]
    w_ref, b1_ref, b2_ref, live_ref, scale_ref, chosen_ref, slots_ref = rest[:7]
    count_ref, bcount_ref, deg_v, ew_v, id_v, sems = rest[7:]
    units = ws_hbm.shape[0]
    rows = ew_v.shape[2]
    me = lax.axis_index("cuts")
    pairs = (
        (count_hbm, count_ref),
        (bcount_hbm, bcount_ref),
        (deg_hbm, deg_v),
        (id_hbm, id_v),
        (ew_hbm.at[0, me], ew_v),
        (b1_hbm, b1_ref),
        (b2_hbm, b2_ref),
        (ws_hbm, w_ref.at[pl.ds(0, units)]),
        (wn_hbm, w_ref.at[pl.ds(units, units)]),
    )
    copies = start_all(pairs, sems)
    for step, out_ref in zip(near, outs):
        fill_slab(out_ref, sums_ref, pick_ref, partner(me, step, cuts), rows)
    for copy in copies[:5]:
        copy.wait()
    live_ref[...] = live_tile(ew_v[...], count_ref, bcount_ref, me)
    degrees = deg_v[:, pl.ds(pl.multiple_of(me * rows, rows), rows)].astype(F32)
    scale_ref[...] = jnp.broadcast_to(as_column(1.0 / degrees), (rows, rows))
    ids = id_v[...]
    device = ids // rows
    peer = (device // (reps * subs)) * reps + (device // subs) % reps
    slot = (ids - device * rows).astype(F32)
    peer_f = peer.astype(F32)
    down = lax.broadcasted_iota(jnp.int32, (rows, rows), 0)
    across = lax.broadcasted_iota(jnp.int32, (rows, rows), 1)
    earlier = (as_column(peer_f) == peer_f) & (down < across)
    rank = jnp.sum(earlier.astype(F32), axis=0, keepdims=True).astype(jnp.int32)
    place = peer * (rows // (cuts * reps)) + rank
    chosen = down == place
    chosen_ref[...] = chosen.astype(F32).astype(BF16)
    slots = jnp.sum(jnp.where(chosen, slot, 0.0), axis=1, keepdims=True)
    slots_ref[...] = jnp.broadcast_to(slots, (rows, rows)).astype(BF16)
    for copy in copies[5:]:
        copy.wait()


def second_layer_kernel(cuts, *rest):
    slabs = rest[:cuts]
    w_ref, b1_ref, b2_ref, live_ref, scale_ref, chosen_ref, slots_ref, out_ref = rest[cuts:]
    rows = chosen_ref.shape[0]
    units = w_ref.shape[1]
    total = slabs[0][...].astype(F32)
    for slab in slabs[1:]:
        total = total + slab[...].astype(F32)
    hidden = jnp.maximum(total + b1_ref[...], 0.0).astype(BF16)
    own, border = hidden[:rows], hidden[rows:]
    summed = contract_first(live_ref[...], border)
    mean = (summed * scale_ref[:, :1]).astype(BF16)
    z = jnp.dot(jnp.concatenate([own, mean], axis=1), w_ref[...], preferred_element_type=F32) + b2_ref[...]
    scale = lax.rsqrt(jnp.mean(z * z, axis=1, keepdims=True) + 1e-05)
    normalized = (z * scale).astype(BF16)
    out_ref[:, :units] = jnp.dot(chosen_ref[...], normalized, preferred_element_type=F32).astype(BF16)
    out_ref[:, units:] = slots_ref[...]


def placing_kernel(in_ref, out_ref):
    rows, units = out_ref.shape
    across = lax.broadcasted_iota(jnp.int32, (rows, rows), 1)
    chosen = in_ref[:, units:].astype(F32).astype(jnp.int32) == across
    out_ref[...] = contract_first(chosen.astype(F32).astype(BF16), in_ref[:, :units]).astype(BF16)


def body(
    features,
    w_self1,
    w_neigh1,
    bias1,
    w_self2,
    w_neigh2,
    bias2,
    degree,
    neighbor_owners,
    neighbor_count,
    boundary_rows,
    boundary_count,
    edge_weight,
    node_id,
):
    cuts, reps, subs = (lax.axis_size(a) for a in ("cuts", "rep", "sub"))
    total, width = features.shape
    units = w_self1.shape[1]
    _, _, neigh, cap, rows = edge_weight.shape
    border = neigh * cap
    vmem = pl.BlockSpec(memory_space=VMEM)
    hbm = pl.BlockSpec(memory_space=pltpu.HBM)
    shape = jax.ShapeDtypeStruct
    slab = shape((rows + border, units), BF16)
    near, far = list(range(min(2, cuts))), list(range(2, cuts))
    owners = neighbor_owners.transpose(2, 0, 1)
    bcounts = boundary_count.transpose(2, 0, 1)
    brows = boundary_rows.transpose(0, 2, 1, 3)
    counts_held = [SMEM(a.shape, jnp.int32) for a in (owners, neighbor_count, bcounts)]
    held = 2 * (total * width + 2 * width * units + cuts * border * total + 4 * total * units)
    held += 2 * cuts * (rows + border) * units + 8 * total * units + 2 * cuts * border * rows
    *sent_far, sums, pick = pl.pallas_call(
        functools.partial(first_layer_kernel, cuts, far),
        out_shape=[slab] * len(far) + [shape((total, units), BF16), shape((cuts, border, total), BF16)],
        in_specs=[hbm] * 9,
        out_specs=[vmem] * (len(far) + 2),
        scratch_shapes=[
            *counts_held,
            pltpu.VMEM(brows.shape, jnp.int32),
            pltpu.VMEM(degree.shape, jnp.int32),
            pltpu.VMEM((total, width), BF16),
            pltpu.VMEM((width, units), BF16),
            pltpu.VMEM((width, units), BF16),
            pltpu.VMEM(edge_weight.shape, BF16),
            pltpu.VMEM((total, units), BF16),
            pltpu.VMEM((total, units), F32),
            pltpu.SemaphoreType.DMA((9,)),
        ],
        compiler_params=pltpu.CompilerParams(vmem_limit_bytes=held + (8 << 20)),
        name="first_layer",
    )(*in_hbm(owners, neighbor_count, bcounts, features, w_neigh1, w_self1, degree, brows, edge_weight))
    *sent_near, weights, b1, b2, live, scale, chosen, slots = pl.pallas_call(
        functools.partial(near_kernel, cuts, reps, subs, near),
        out_shape=[slab] * len(near)
        + [
            shape((2 * units, units), BF16),
            shape((1, units), F32),
            shape((1, units), F32),
            shape((border, rows), BF16),
            shape((rows, rows), F32),
            shape((rows, rows), BF16),
            shape((rows, rows), BF16),
        ],
        in_specs=[vmem] * 2 + [hbm] * 9,
        out_specs=[vmem] * (len(near) + 7),
        scratch_shapes=[
            *counts_held[1:],
            pltpu.VMEM(degree.shape, jnp.int32),
            pltpu.VMEM(edge_weight.shape[2:], BF16),
            pltpu.VMEM(node_id.shape, jnp.int32),
            pltpu.SemaphoreType.DMA((9,)),
        ],
        compiler_params=pltpu.CompilerParams(vmem_limit_bytes=held + (8 << 20)),
        cost_estimate=pl.CostEstimate(flops=2 * border * total * units, bytes_accessed=4 * units * units, transcendentals=0),
        name="near_slabs",
    )(
        sums,
        pick,
        *in_hbm(neighbor_count, bcounts, w_self2, w_neigh2, bias1.reshape(1, units), bias2.reshape(1, units)),
        *in_hbm(degree, edge_weight, node_id),
    )
    sent = dict(zip(near + far, sent_near + sent_far))
    arrived = [sent[s] if s == 0 else lax.ppermute(sent[s], "cuts", partner_pairs(s, cuts)) for s in range(cuts)]
    payload = pl.pallas_call(
        functools.partial(second_layer_kernel, cuts),
        out_shape=shape((rows, units + rows), BF16),
        in_specs=[vmem] * (cuts + 7),
        out_specs=vmem,
        compiler_params=pltpu.CompilerParams(vmem_limit_bytes=24 << 20),
        name="second_layer",
    )(*arrived, weights, b1, b2, live, scale, chosen, slots)
    peers = cuts * reps
    moved = lax.all_to_all(
        payload.reshape(peers, rows // peers, units + rows), ("cuts", "rep"), split_axis=0, concat_axis=0, tiled=True
    )
    return pl.pallas_call(
        placing_kernel,
        out_shape=shape((rows, units), BF16),
        in_specs=[vmem],
        out_specs=vmem,
        name="placing",
    )(moved.reshape(rows, units + rows))


def solution(mesh):
    block = ("groups", "rep", "sub")
    placed = (
        P(block, "cuts"),
        P("cuts", None),
        P("cuts", None),
        P(),
        P(),
        P(),
        P(),
        P(block, None),
        P(block, None, None),
        P(block, None),
        P(block, None, None, None),
        P(block, None, None),
        P(block, None, None, None, None),
        P(block, "cuts"),
    )
    return jax.shard_map(
        body,
        mesh=mesh,
        in_specs=placed,
        out_specs=P(("groups", "cuts", "rep", "sub"), None),
        check_vma=False,
    )
```

time: 52 us -> 44 us (0.85)
  local copies, waits for them, and re-layouts: 7.47 us -> 0 us
  waiting for transfers between devices: 16.7 us -> 15.2 us
  Pallas kernels: 6.98 us -> 8.3 us
    unnamed x29 -> x0, local copies, waits for them, and re-layouts: 7.47 us -> none
    ppermute x3, waiting for transfers between devices: 16.7 us -> 15.2 us  [body(): lax.ppermute(sent[s], 'cuts', partner_pairs(s, cuts))]
    pallas_call x3 -> x4, Pallas kernels: 6.98 us -> 8.3 us  [the longest x1 4.43 us: body(): pl.pallas_call(functools.partial(first_layer_kernel, cuts, far), out_shap...]
  transfers between devices with their start and end apart: 3 -> 3, of which waited for: 2 -> 2; matrix products, arithmetic and copies ran while one was open for 0% -> 0% of each run, Pallas kernels for 0% -> 3%
where the time goes in v2:
time: 44 us; the launch traced here: 43.7 us
  waiting for transfers between devices  15.2 us (35%)
  blocking collectives  14.5 us (33%)
  Pallas kernels  8.3 us (19%)
  starting transfers between devices  5.74 us (13%)
    ppermute x3, waiting for transfers between devices, body(): lax.ppermute(sent[s], 'cuts', partner_pairs(s, cuts))  15.2 us
    all_to_all x1, blocking collectives, body(): lax.all_to_all(payload.reshape(peers, rows // peers, units + rows), ('cut...  14.5 us
    ppermute x3, starting transfers between devices, body(): lax.ppermute(sent[s], 'cuts', partner_pairs(s, cuts))  5.74 us
    pallas_call x1, Pallas kernels, body(): pl.pallas_call(functools.partial(first_layer_kernel, cuts, far), out_shap...  4.43 us
    pallas_call x1, Pallas kernels, body(): pl.pallas_call(placing_kernel, out_shape=shape((rows, units), BF16), in_s...  1.79 us
    pallas_call x1, Pallas kernels, body(): pl.pallas_call(functools.partial(near_kernel, cuts, reps, subs, near), ou...  1.46 us
  transfers between devices with their start and end apart: 3, of which 2 were waited for; matrix products, arithmetic and copies ran while one was open for 0% of the time, Pallas kernels for 3%

profile of v2, /device:TPU:0, one launch (start us, length us, event | category | flops | bytes accessed | tf_op | source)
XLA Modules:
  0.0 43.7 jit_solution(16783948969342026855)
XLA Ops:
  0.0 4.4 %first_layer.1 = (bf16[224,512]{1,0:T(8,128)(2,1)S(1)}, bf16[224,512]{1,0:T(8,128)(2,1)S(1)}, bf16[512,512]{1,0:T(8,128)(2,1)S(1)}, bf16[4,96,512]{2,1,0:T(8,128)(2,1)S(1)}) custom-call(s32[3,1,4]{2,1,0:T(1,128)} %bitcast.14, s32[1,4]{1,0:T(1,128)} %count_hbm.3, s32[3,1,4]{2,1,0:T(1,128)} %bitcast.9, bf16[512,1024]{1,0:T(8,128)(2,1)} %x_hbm.1, ...), custom_call_target="tpu_custom_call" | custom-call | tf_op jit(solution)/shard_map/first_layer/pallas_call | solution.py:239
  4.4 4.1 %collective-permute-start.1 = (bf16[224,512]{1,0:T(8,128)(2,1)S(1)}, bf16[224,512]{1,0:T(8,128)(2,1)S(1)}, u32[]{:S(2)}, u32[]{:S(2)}) collective-permute-start(bf16[224,512]{1,0:T(8,128)(2,1)S(1)} %get-tuple-element.22), channel_id=1, source_target_pairs={{0,8},{4,12},{8,0},{12,4},{1,9},{5,13},{9,1},{13,5},{2,10},{6,14},... | collective-permute-start | bytes 688136 | tf_op jit(solution)/shard_map/ppermute | solution.py:290
  8.5 1.3 %collective-permute-start.2 = (bf16[224,512]{1,0:T(8,128)(2,1)S(1)}, bf16[224,512]{1,0:T(8,128)(2,1)S(1)}, u32[]{:S(2)}, u32[]{:S(2)}) collective-permute-start(bf16[224,512]{1,0:T(8,128)(2,1)S(1)} %get-tuple-element.23), channel_id=1, source_target_pairs={{0,12},{4,8},{8,4},{12,0},{1,13},{5,9},{9,5},{13,1},{2,14},{6,10},... | collective-permute-start | bytes 688136 | tf_op jit(solution)/shard_map/ppermute | solution.py:290
  9.9 1.5 %near_slabs.1 = (bf16[224,512]{1,0:T(8,128)(2,1)S(1)}, bf16[224,512]{1,0:T(8,128)(2,1)S(1)}, bf16[1024,512]{1,0:T(8,128)(2,1)S(1)}, f32[1,512]{1,0:T(1,128)S(1)}...) custom-call(bf16[512,512]{1,0:T(8,128)(2,1)S(1)} %get-tuple-element., ...), custom_call_target="tpu_custom_call" | custom-call | flops 50331648 | bytes 1048576 | tf_op jit(solution)/shard_map/near_slabs/pallas_call | solution.py:259
  11.3 0.3 collective-permute-start
  11.6 13.2 %collective-permute-done.1.rest_2_ = bf16[224,512]{1,0:T(8,128)(2,1)S(1)} collective-permute-done((bf16[224,512]{1,0:T(8,128)(2,1)S(1)}, bf16[224,512]{1,0:T(8,128)(2,1)S(1)}, u32[]{:S(2)}, u32[]{:S(2)}) %collective-permute-start.1) | collective-permute-done | bytes 229408 | tf_op jit(solution)/shard_map/ppermute | solution.py:290
  24.8 0.0 collective-permute-done.2.rest_3_
  24.8 2.0 %collective-permute-done.rest_1_ = bf16[224,512]{1,0:T(8,128)(2,1)S(1)} collective-permute-done((bf16[224,512]{1,0:T(8,128)(2,1)S(1)}, bf16[224,512]{1,0:T(8,128)(2,1)S(1)}, u32[]{:S(2)}, u32[]{:S(2)}) %collective-permute-start) | collective-permute-done | bytes 229408 | tf_op jit(solution)/shard_map/ppermute | solution.py:290
  26.9 0.6 %second_layer.1 = bf16[128,640]{1,0:T(8,128)(2,1)S(1)} custom-call(bf16[224,512]{1,0:T(8,128)(2,1)S(1)} %get-tuple-element.20.rest_0_, bf16[224,512]{1,0:T(8,128)(2,1)S(1)} %collective-permute-done.rest_1_, bf16[224,512]{1,0:T(8,128)(2,1)S(1)} %collective-permute-done.1.rest_2_, bf16[224,512]{1,0:T(8,128)(2,1)S(1)} %collective-permute-done.2.rest_3_, ...), custom_call_target="tpu_custom_call" | custom-call | tf_op jit(solution)/shard_map/second_layer/pallas_call | solution.py:291
  27.5 14.5 %all_to_all.5 = bf16[8,16,640]{2,1,0:T(8,128)(2,1)} all-to-all(bf16[8,16,640]{2,1,0:T(8,128)(2,1)S(1)} %bitcast.7), channel_id=1, replica_groups=mesh['groups'=2,'cuts'=4,'rep'=2,'sub'=2] {'cuts','rep'}, dimensions={0} | all-to-all | bytes 327680 | tf_op jit(solution)/shard_map/all_to_all | solution.py:300
  42.0 1.8 %placing.1 = bf16[128,512]{1,0:T(8,128)(2,1)} custom-call(bf16[128,640]{1,0:T(8,128)(2,1)} %bitcast.8), custom_call_target="tpu_custom_call" | custom-call | tf_op jit(solution)/shard_map/placing/pallas_call | solution.py:303
Async XLA Ops:
  4.4 20.4 %collective-permute-start.1 = (bf16[224,512]{1,0:T(8,128)(2,1)S(1)}, bf16[224,512]{1,0:T(8,128)(2,1)S(1)}, u32[]{:S(2)}, u32[]{:S(2)}) collective-permute-start(bf16[224,512]{1,0:T(8,128)(2,1)S(1)} %get-tuple-element.22), channel_id=1, source_target_pairs={{0,8},{4,12},{8,0},{12,4},{1,9},{5,13},{9,1},{13,5},{2,10},{6,14},... | collective-permute-start | bytes 688136 | tf_op jit(solution)/shard_map/ppermute | solution.py:290
  8.5 16.3 %collective-permute-start.2 = (bf16[224,512]{1,0:T(8,128)(2,1)S(1)}, bf16[224,512]{1,0:T(8,128)(2,1)S(1)}, u32[]{:S(2)}, u32[]{:S(2)}) collective-permute-start(bf16[224,512]{1,0:T(8,128)(2,1)S(1)} %get-tuple-element.23), channel_id=1, source_target_pairs={{0,12},{4,8},{8,4},{12,0},{1,13},{5,9},{9,5},{13,1},{2,14},{6,10},... | collective-permute-start | bytes 688136 | tf_op jit(solution)/shard_map/ppermute | solution.py:290
  11.3 15.5 %collective-permute-start = (bf16[224,512]{1,0:T(8,128)(2,1)S(1)}, bf16[224,512]{1,0:T(8,128)(2,1)S(1)}, u32[]{:S(2)}, u32[]{:S(2)}) collective-permute-start(bf16[224,512]{1,0:T(8,128)(2,1)S(1)} %get-tuple-element.21), channel_id=1, source_target_pairs={{0,4},{4,0},{8,12},{12,8},{1,5},{5,1},{9,13},{13,9},{2,6},{6,2},{1... | collective-permute-start | bytes 688136 | tf_op jit(solution)/shard_map/ppermute | solution.py:290

commit v3 on v2

--- a/solution.py
+++ b/solution.py
@@ -13,16 +13,8 @@
 SMEM = pltpu.SMEM
 
 
-def partner(index, step, total):
-    if total & (total - 1) == 0:
-        return index ^ step
-    return lax.rem(step - index + 2 * total, total)
-
-
 def partner_pairs(step, total):
-    if total & (total - 1) == 0:
-        return [(i, i ^ step) for i in range(total)]
-    return [(i, (step - i) % total) for i in range(total)]
+    return [(i, i ^ step) for i in range(total)]
 
 
 def as_column(row):
@@ -64,16 +56,26 @@
     return copies
 
 
-def fill_slab(out_ref, sums_ref, pick_ref, owner, rows):
-    out_ref[:rows, :] = sums_ref[pl.ds(pl.multiple_of(owner * rows, rows), rows), :]
-    out_ref[rows:, :] = jnp.dot(pick_ref[owner], sums_ref[...], preferred_element_type=F32).astype(BF16)
+def own_part(sums_ref, owner, rows):
+    return sums_ref[pl.ds(pl.multiple_of(owner * rows, rows), rows), :]
+
+
+def border_part(sums_ref, pick_ref, owner):
+    return jnp.dot(pick_ref[owner], sums_ref[...], preferred_element_type=F32)
 
 
 def first_layer_kernel(
-    cuts, far, owners_hbm, count_hbm, bcount_hbm, x_hbm, wn_hbm, ws_hbm, deg_hbm, brow_hbm, ew_hbm, *rest
+    cuts, owners_hbm, count_hbm, bcount_hbm, x_hbm, wn_hbm, ws_hbm, deg_hbm, brow_hbm, ew_hbm, *rest
 ):
-    outs, (sums_ref, pick_ref) = rest[: len(far)], rest[len(far) : len(far) + 2]
-    owners_ref, count_ref, bcount_ref, brow_v, deg_v, x_v, wn_v, ws_v, ew_v, y_v, s_v, sems = rest[len(far) + 2 :]
+    near, far = min(2, cuts), cuts - min(2, cuts)
+    border_refs, own_refs, slab_refs, local_refs = (
+        rest[: far // 2],
+        rest[far // 2 : far // 2 + far],
+        rest[far // 2 + far : far // 2 + far + near],
+        rest[far // 2 + far + near : 2 * far + near],
+    )
+    rest = rest[2 * far + near :]
+    owners_ref, count_ref, bcount_ref, brow_v, deg_v, x_v, wn_v, ws_v, ew_v, pick_v, y_v, s_v, sums_v, sems = rest
     pairs = (
         (brow_hbm, brow_v),
         (owners_hbm, owners_ref),
@@ -99,7 +101,7 @@
         columns = contract_last(eye, brow_v[0, k].astype(F32)).astype(jnp.int32)
         for u in range(cuts):
             target = columns[:, u : u + 1] + owners_ref[k, 0, u] * rows
-            pick_ref[u, k * cap : (k + 1) * cap, :] = (lane == target).astype(F32).astype(BF16)
+            pick_v[u, k * cap : (k + 1) * cap, :] = (lane == target).astype(F32).astype(BF16)
     x_in.wait()
     wn_in.wait()
     y_v[...] = jnp.dot(x_v[...], wn_v[...], preferred_element_type=F32).astype(BF16)
@@ -109,36 +111,34 @@
         copy.wait()
     for u in range(cuts):
         at = slice(u * rows, (u + 1) * rows)
-        picked = jnp.dot(pick_ref[u], y_v[...], preferred_element_type=F32).astype(BF16)
+        picked = jnp.dot(pick_v[u], y_v[...], preferred_element_type=F32).astype(BF16)
         summed = contract_first(live_tile(ew_v[0, u], count_ref, bcount_ref, u), picked)
         scale = as_column(1.0 / deg_v[:, at].astype(F32))
-        sums_ref[at, :] = (s_v[at, :] + summed * scale).astype(BF16)
-    for step, out_ref in zip(far, outs):
-        fill_slab(out_ref, sums_ref, pick_ref, partner(me, step, cuts), rows)
-
-
-def near_kernel(
-    cuts,
-    reps,
-    subs,
-    near,
-    sums_ref,
-    pick_ref,
-    count_hbm,
-    bcount_hbm,
-    ws_hbm,
-    wn_hbm,
-    b1_hbm,
-    b2_hbm,
-    deg_hbm,
-    ew_hbm,
-    id_hbm,
-    *rest,
-):
-    outs, rest = rest[: len(near)], rest[len(near) :]
-    w_ref, b1_ref, b2_ref, live_ref, scale_ref, chosen_ref, slots_ref = rest[:7]
-    count_ref, bcount_ref, deg_v, ew_v, id_v, sems = rest[7:]
-    units = ws_hbm.shape[0]
+        sums_v[at, :] = (s_v[at, :] + summed * scale).astype(BF16)
+    for i, out_ref in enumerate(border_refs):
+        out_ref[...] = border_part(sums_v, pick_v, me ^ (2 * i + 3)).astype(BF16)
+    for i, out_ref in enumerate(own_refs):
+        out_ref[...] = own_part(sums_v, me ^ (i + 2), rows)
+    for step, out_ref in enumerate(slab_refs):
+        out_ref[:rows, :] = own_part(sums_v, me ^ step, rows)
+        out_ref[rows:, :] = border_part(sums_v, pick_v, me ^ step).astype(BF16)
+    for i, out_ref in enumerate(local_refs):
+        out_ref[...] = border_part(sums_v, pick_v, me ^ (2 * i + 2))
+
+
+def hidden_rows(parts, b1_ref):
+    total = parts[0].astype(F32)
+    for part in parts[1:]:
+        total = total + part.astype(F32)
+    return jnp.maximum(total + b1_ref[...], 0.0).astype(BF16)
+
+
+def own_rows_kernel(cuts, reps, subs, *rest):
+    near, far = min(2, cuts), cuts - min(2, cuts)
+    slab_refs, own_refs, rest = rest[:near], rest[near : near + far], rest[near + far :]
+    count_hbm, bcount_hbm, ws_hbm, wn_hbm, b1_hbm, b2_hbm, deg_hbm, ew_hbm, id_hbm = rest[:9]
+    z_ref, wn_ref, b1_ref, live_ref, scale_ref, chosen_ref, slots_ref = rest[9:16]
+    ws_v, b2_v, count_ref, bcount_ref, deg_v, ew_v, id_v, sems = rest[16:]
     rows = ew_v.shape[2]
     me = lax.axis_index("cuts")
     pairs = (
@@ -148,13 +148,11 @@
         (id_hbm, id_v),
         (ew_hbm.at[0, me], ew_v),
         (b1_hbm, b1_ref),
-        (b2_hbm, b2_ref),
-        (ws_hbm, w_ref.at[pl.ds(0, units)]),
-        (wn_hbm, w_ref.at[pl.ds(units, units)]),
+        (b2_hbm, b2_v),
+        (ws_hbm, ws_v),
+        (wn_hbm, wn_ref),
     )
     copies = start_all(pairs, sems)
-    for step, out_ref in zip(near, outs):
-        fill_slab(out_ref, sums_ref, pick_ref, partner(me, step, cuts), rows)
     for copy in copies[:5]:
         copy.wait()
     live_ref[...] = live_tile(ew_v[...], count_ref, bcount_ref, me)
@@ -176,21 +174,20 @@
     slots_ref[...] = jnp.broadcast_to(slots, (rows, rows)).astype(BF16)
     for copy in copies[5:]:
         copy.wait()
-
-
-def second_layer_kernel(cuts, *rest):
-    slabs = rest[:cuts]
-    w_ref, b1_ref, b2_ref, live_ref, scale_ref, chosen_ref, slots_ref, out_ref = rest[cuts:]
+    own = hidden_rows([slab[:rows, :] for slab in slab_refs] + [part[...] for part in own_refs], b1_ref)
+    z_ref[...] = jnp.dot(own, ws_v[...], preferred_element_type=F32) + b2_v[...]
+
+
+def border_rows_kernel(cuts, *rest):
+    near, far = min(2, cuts), cuts - min(2, cuts)
+    slab_refs, border_refs, rest = rest[:near], rest[near : near + far // 2], rest[near + far // 2 :]
+    z_ref, wn_ref, b1_ref, live_ref, scale_ref, chosen_ref, slots_ref, out_ref = rest
     rows = chosen_ref.shape[0]
-    units = w_ref.shape[1]
-    total = slabs[0][...].astype(F32)
-    for slab in slabs[1:]:
-        total = total + slab[...].astype(F32)
-    hidden = jnp.maximum(total + b1_ref[...], 0.0).astype(BF16)
-    own, border = hidden[:rows], hidden[rows:]
+    units = wn_ref.shape[1]
+    border = hidden_rows([slab[rows:, :] for slab in slab_refs] + [part[...] for part in border_refs], b1_ref)
     summed = contract_first(live_ref[...], border)
     mean = (summed * scale_ref[:, :1]).astype(BF16)
-    z = jnp.dot(jnp.concatenate([own, mean], axis=1), w_ref[...], preferred_element_type=F32) + b2_ref[...]
+    z = z_ref[...] + jnp.dot(mean, wn_ref[...], preferred_element_type=F32)
     scale = lax.rsqrt(jnp.mean(z * z, axis=1, keepdims=True) + 1e-05)
     normalized = (z * scale).astype(BF16)
     out_ref[:, :units] = jnp.dot(chosen_ref[...], normalized, preferred_element_type=F32).astype(BF16)
@@ -229,18 +226,22 @@
     hbm = pl.BlockSpec(memory_space=pltpu.HBM)
     shape = jax.ShapeDtypeStruct
     slab = shape((rows + border, units), BF16)
-    near, far = list(range(min(2, cuts))), list(range(2, cuts))
+    own_slab, border_slab = shape((rows, units), BF16), shape((border, units), BF16)
+    near, far = min(2, cuts), cuts - min(2, cuts)
     owners = neighbor_owners.transpose(2, 0, 1)
     bcounts = boundary_count.transpose(2, 0, 1)
     brows = boundary_rows.transpose(0, 2, 1, 3)
     counts_held = [SMEM(a.shape, jnp.int32) for a in (owners, neighbor_count, bcounts)]
     held = 2 * (total * width + 2 * width * units + cuts * border * total + 4 * total * units)
     held += 2 * cuts * (rows + border) * units + 8 * total * units + 2 * cuts * border * rows
-    *sent_far, sums, pick = pl.pallas_call(
-        functools.partial(first_layer_kernel, cuts, far),
-        out_shape=[slab] * len(far) + [shape((total, units), BF16), shape((cuts, border, total), BF16)],
+    sent = pl.pallas_call(
+        functools.partial(first_layer_kernel, cuts),
+        out_shape=[border_slab] * (far // 2)
+        + [own_slab] * far
+        + [slab] * near
+        + [shape((border, units), F32)] * (far // 2),
         in_specs=[hbm] * 9,
-        out_specs=[vmem] * (len(far) + 2),
+        out_specs=[vmem] * (2 * far + near),
         scratch_shapes=[
             *counts_held,
             pltpu.VMEM(brows.shape, jnp.int32),
@@ -249,53 +250,67 @@
             pltpu.VMEM((width, units), BF16),
             pltpu.VMEM((width, units), BF16),
             pltpu.VMEM(edge_weight.shape, BF16),
+            pltpu.VMEM((cuts, border, total), BF16),
             pltpu.VMEM((total, units), BF16),
             pltpu.VMEM((total, units), F32),
+            pltpu.VMEM((total, units), BF16),
             pltpu.SemaphoreType.DMA((9,)),
         ],
         compiler_params=pltpu.CompilerParams(vmem_limit_bytes=held + (8 << 20)),
         name="first_layer",
     )(*in_hbm(owners, neighbor_count, bcounts, features, w_neigh1, w_self1, degree, brows, edge_weight))
-    *sent_near, weights, b1, b2, live, scale, chosen, slots = pl.pallas_call(
-        functools.partial(near_kernel, cuts, reps, subs, near),
-        out_shape=[slab] * len(near)
-        + [
-            shape((2 * units, units), BF16),
-            shape((1, units), F32),
+    sent = list(sent)
+    pairs, owns, slabs, local = (
+        sent[: far // 2],
+        sent[far // 2 : far // 2 + far],
+        sent[far // 2 + far : far // 2 + far + near],
+        sent[far // 2 + far + near :],
+    )
+    trade = lambda a, step: lax.ppermute(a, "cuts", partner_pairs(step, cuts))
+    pairs = [trade(a, 1) for a in pairs]
+    owns = [trade(a, i + 2) for i, a in enumerate(owns)]
+    slabs = slabs[:1] + [trade(a, 1) for a in slabs[1:]]
+    paired = [(a + b.astype(F32)).astype(BF16) for a, b in zip(local, pairs)]
+    borders = [trade(a, 2 * i + 2) for i, a in enumerate(paired)]
+    prepared = pl.pallas_call(
+        functools.partial(own_rows_kernel, cuts, reps, subs),
+        out_shape=[
+            shape((rows, units), F32),
+            shape((units, units), BF16),
             shape((1, units), F32),
             shape((border, rows), BF16),
             shape((rows, rows), F32),
             shape((rows, rows), BF16),
             shape((rows, rows), BF16),
         ],
-        in_specs=[vmem] * 2 + [hbm] * 9,
-        out_specs=[vmem] * (len(near) + 7),
+        in_specs=[vmem] * cuts + [hbm] * 9,
+        out_specs=[vmem] * 7,
         scratch_shapes=[
+            pltpu.VMEM((units, units), BF16),
+            pltpu.VMEM((1, units), F32),
             *counts_held[1:],
             pltpu.VMEM(degree.shape, jnp.int32),
             pltpu.VMEM(edge_weight.shape[2:], BF16),
             pltpu.VMEM(node_id.shape, jnp.int32),
             pltpu.SemaphoreType.DMA((9,)),
         ],
-        compiler_params=pltpu.CompilerParams(vmem_limit_bytes=held + (8 << 20)),
-        cost_estimate=pl.CostEstimate(flops=2 * border * total * units, bytes_accessed=4 * units * units, transcendentals=0),
-        name="near_slabs",
+        compiler_params=pltpu.CompilerParams(vmem_limit_bytes=24 << 20),
+        cost_estimate=pl.CostEstimate(flops=2 * rows * units * units, bytes_accessed=4 * units * units, transcendentals=0),
+        name="own_rows",
     )(
-        sums,
-        pick,
+        *slabs,
+        *owns,
         *in_hbm(neighbor_count, bcounts, w_self2, w_neigh2, bias1.reshape(1, units), bias2.reshape(1, units)),
         *in_hbm(degree, edge_weight, node_id),
     )
-    sent = dict(zip(near + far, sent_near + sent_far))
-    arrived = [sent[s] if s == 0 else lax.ppermute(sent[s], "cuts", partner_pairs(s, cuts)) for s in range(cuts)]
     payload = pl.pallas_call(
-        functools.partial(second_layer_kernel, cuts),
+        functools.partial(border_rows_kernel, cuts),
         out_shape=shape((rows, units + rows), BF16),
-        in_specs=[vmem] * (cuts + 7),
+        in_specs=[vmem] * (near + far // 2 + 7),
         out_specs=vmem,
         compiler_params=pltpu.CompilerParams(vmem_limit_bytes=24 << 20),
-        name="second_layer",
-    )(*arrived, weights, b1, b2, live, scale, chosen, slots)
+        name="border_rows",
+    )(*slabs, *borders, *prepared)
     peers = cuts * reps
     moved = lax.all_to_all(
         payload.reshape(peers, rows // peers, units + rows), ("cuts", "rep"), split_axis=0, concat_axis=0, tiled=True

time: 44 us -> 41 us (0.932)
  waiting for transfers between devices: 15.2 us -> 9.81 us
  starting transfers between devices: 5.74 us -> 10.1 us
  blocking collectives: 14.5 us -> 12.1 us
    ppermute x3 -> x5, waiting for transfers between devices: 15.2 us -> 9.81 us  [body(): trade = lambda a, step: lax.ppermute(a, 'cuts', partner_pairs(step, cuts))]
    ppermute x3 -> x5, starting transfers between devices: 5.74 us -> 10.1 us  [body(): trade = lambda a, step: lax.ppermute(a, 'cuts', partner_pairs(step, cuts))]
    all_to_all x1, blocking collectives: 14.5 us -> 12.1 us  [body(): lax.all_to_all(payload.reshape(peers, rows // peers, units + rows), ('cut...]
  transfers between devices with their start and end apart: 3 -> 5, of which waited for: 2 -> 3; matrix products, arithmetic and copies ran while one was open for 0% -> 0% of each run, Pallas kernels for 3% -> 4%
where the time goes in v3:
time: 41 us; the launch traced here: 40.8 us
  blocking collectives  12.1 us (30%)
  starting transfers between devices  10.1 us (25%)
  waiting for transfers between devices  9.81 us (24%)
  Pallas kernels  8.63 us (21%)
    all_to_all x1, blocking collectives, body(): lax.all_to_all(payload.reshape(peers, rows // peers, units + rows), ('cut...  12.1 us
    ppermute x5, starting transfers between devices, body(): trade = lambda a, step: lax.ppermute(a, 'cuts', partner_pairs(step, cuts))  10.1 us
    ppermute x5, waiting for transfers between devices, body(): trade = lambda a, step: lax.ppermute(a, 'cuts', partner_pairs(step, cuts))  9.81 us
    pallas_call x1, Pallas kernels, body(): pl.pallas_call(functools.partial(first_layer_kernel, cuts), out_shape=[bo...  4.61 us
    pallas_call x1, Pallas kernels, body(): pl.pallas_call(placing_kernel, out_shape=shape((rows, units), BF16), in_s...  1.79 us
    pallas_call x1, Pallas kernels, body(): pl.pallas_call(functools.partial(own_rows_kernel, cuts, reps, subs), out_...  1.61 us
  transfers between devices with their start and end apart: 5, of which 3 were waited for; matrix products, arithmetic and copies ran while one was open for 0% of the time, Pallas kernels for 4%

profile of v3, /device:TPU:0, one launch (start us, length us, event | category | flops | bytes accessed | tf_op | source)
XLA Modules:
  0.0 40.8 jit_solution(7507747799343462006)
XLA Ops:
  0.0 4.6 %first_layer.1 = (bf16[96,512]{1,0:T(8,128)(2,1)S(1)}, bf16[128,512]{1,0:T(8,128)(2,1)S(1)}, bf16[128,512]{1,0:T(8,128)(2,1)S(1)}, bf16[224,512]{1,0:T(8,128)(2,...) custom-call(s32[3,1,4]{2,1,0:T(1,128)} %bitcast.14, s32[1,4]{1,0:T(1,128)} %rest_4_.1, s32[3,1,4]{2,1,0:T(1,128)} %bitcast.9, ...), custom_call_target="tpu_custom_call" | custom-call | tf_op jit(solution)/shard_map/first_layer/pallas_call | solution.py:237
  4.6 3.1 %collective-permute-start.1 = (bf16[96,512]{1,0:T(8,128)(2,1)S(1)}, bf16[96,512]{1,0:T(8,128)(2,1)S(1)}, u32[]{:S(2)}, u32[]{:S(2)}) collective-permute-start(bf16[96,512]{1,0:T(8,128)(2,1)S(1)} %get-tuple-element.21), channel_id=1, source_target_pairs={{0,4},{4,0},{8,12},{12,8},{1,5},{5,1},{9,13},{13,9},{2,6},{6,2},{1... | collective-permute-start | bytes 294920 | tf_op jit(solution)/shard_map/ppermute | solution.py:269
  7.7 2.6 %collective-permute-start.3 = (bf16[128,512]{1,0:T(8,128)(2,1)S(1)}, bf16[128,512]{1,0:T(8,128)(2,1)S(1)}, u32[]{:S(2)}, u32[]{:S(2)}) collective-permute-start(bf16[128,512]{1,0:T(8,128)(2,1)S(1)} %get-tuple-element.22), channel_id=1, source_target_pairs={{0,8},{4,12},{8,0},{12,4},{1,9},{5,13},{9,1},{13,5},{2,10},{6,14},... | collective-permute-start | bytes 393224 | tf_op jit(solution)/shard_map/ppermute | solution.py:269
  10.3 0.0 collective-permute-start.4
  10.3 0.9 %collective-permute-start = (bf16[224,512]{1,0:T(8,128)(2,1)S(1)}, bf16[224,512]{1,0:T(8,128)(2,1)S(1)}, u32[]{:S(2)}, u32[]{:S(2)}) collective-permute-start(bf16[224,512]{1,0:T(8,128)(2,1)S(1)} %get-tuple-element.19), channel_id=1, source_target_pairs={{0,4},{4,0},{8,12},{12,8},{1,5},{5,1},{9,13},{13,9},{2,6},{6,2},{1... | collective-permute-start | bytes 688136 | tf_op jit(solution)/shard_map/ppermute | solution.py:269
  11.2 0.0 collective-permute-done.1
  11.2 3.6 %collective-permute-start.2 = (bf16[96,512]{1,0:T(8,128)(2,1)S(1)}, bf16[96,512]{1,0:T(8,128)(2,1)S(1)}, u32[]{:S(2)}, u32[]{:S(2)}) collective-permute-start(bf16[96,512]{1,0:T(8,128)(2,1)S(1)} %add_convert_fusion), channel_id=1, source_target_pairs={{0,8},{4,12},{8,0},{12,4},{1,9},{5,13},{9,1},{13,5},{2,10},{6,14},... | collective-permute-start | bytes 294920 | tf_op jit(solution)/shard_map/ppermute | solution.py:269
  14.8 5.5 %collective-permute-done.3.rest_2_ = bf16[128,512]{1,0:T(8,128)(2,1)S(1)} collective-permute-done((bf16[128,512]{1,0:T(8,128)(2,1)S(1)}, bf16[128,512]{1,0:T(8,128)(2,1)S(1)}, u32[]{:S(2)}, u32[]{:S(2)}) %collective-permute-start.3) | collective-permute-done | bytes 131104 | tf_op jit(solution)/shard_map/ppermute | solution.py:269
  20.3 0.0 collective-permute-done.4.rest_3_
  20.3 1.9 %collective-permute-done.rest_1_ = bf16[224,512]{1,0:T(8,128)(2,1)S(1)} collective-permute-done((bf16[224,512]{1,0:T(8,128)(2,1)S(1)}, bf16[224,512]{1,0:T(8,128)(2,1)S(1)}, u32[]{:S(2)}, u32[]{:S(2)}) %collective-permute-start) | collective-permute-done | bytes 229408 | tf_op jit(solution)/shard_map/ppermute | solution.py:269
  22.3 1.6 %own_rows.1 = (f32[128,512]{1,0:T(8,128)S(1)}, bf16[512,512]{1,0:T(8,128)(2,1)S(1)}, f32[1,512]{1,0:T(1,128)S(1)}, bf16[96,128]{1,0:T(8,128)(2,1)S(1)}, f32[128,...) custom-call(bf16[224,512]{1,0:T(8,128)(2,1)S(1)} %get-tuple-element.18.rest_0_, ...), custom_call_target="tpu_custom_call" | custom-call | flops 67108864 | bytes 1048576 | tf_op jit(solution)/shard_map/own_rows/pallas_call | solution.py:275
  23.9 2.3 %collective-permute-done.2.rest_2_ = bf16[96,512]{1,0:T(8,128)(2,1)S(1)} collective-permute-done((bf16[96,512]{1,0:T(8,128)(2,1)S(1)}, bf16[96,512]{1,0:T(8,128)(2,1)S(1)}, u32[]{:S(2)}, u32[]{:S(2)}) %collective-permute-start.2) | collective-permute-done | bytes 98336 | tf_op jit(solution)/shard_map/ppermute | solution.py:269
  26.2 0.6 %border_rows.1 = bf16[128,640]{1,0:T(8,128)(2,1)S(1)} custom-call(bf16[224,512]{1,0:T(8,128)(2,1)S(1)} %get-tuple-element.18.rest_0_, bf16[224,512]{1,0:T(8,128)(2,1)S(1)} %collective-permute-done.rest_1_, bf16[96,512]{1,0:T(8,128)(2,1)S(1)} %collective-permute-done.2.rest_2_, f32[128,512]{1,0:T(8,128)S(1)} %get-tuple-element.24.rest_3_, ...), custom_call_target="tpu_custom_call" | custom-call | tf_op jit(solution)/shard_map/border_rows/pallas_call | solution.py:306
  26.8 12.1 %all_to_all.5 = bf16[8,16,640]{2,1,0:T(8,128)(2,1)} all-to-all(bf16[8,16,640]{2,1,0:T(8,128)(2,1)S(1)} %bitcast.7), channel_id=1, replica_groups=mesh['groups'=2,'cuts'=4,'rep'=2,'sub'=2] {'cuts','rep'}, dimensions={0} | all-to-all | bytes 327680 | tf_op jit(solution)/shard_map/all_to_all | solution.py:315
  39.0 1.8 %placing.1 = bf16[128,512]{1,0:T(8,128)(2,1)} custom-call(bf16[128,640]{1,0:T(8,128)(2,1)} %bitcast.8), custom_call_target="tpu_custom_call" | custom-call | tf_op jit(solution)/shard_map/placing/pallas_call | solution.py:318
  (1 shorter events, 0.0 us)
Async XLA Ops:
  4.6 6.6 %collective-permute-start.1 = (bf16[96,512]{1,0:T(8,128)(2,1)S(1)}, bf16[96,512]{1,0:T(8,128)(2,1)S(1)}, u32[]{:S(2)}, u32[]{:S(2)}) collective-permute-start(bf16[96,512]{1,0:T(8,128)(2,1)S(1)} %get-tuple-element.21), channel_id=1, source_target_pairs={{0,4},{4,0},{8,12},{12,8},{1,5},{5,1},{9,13},{13,9},{2,6},{6,2},{1... | collective-permute-start | bytes 294920 | tf_op jit(solution)/shard_map/ppermute | solution.py:269
  7.7 12.6 %collective-permute-start.3 = (bf16[128,512]{1,0:T(8,128)(2,1)S(1)}, bf16[128,512]{1,0:T(8,128)(2,1)S(1)}, u32[]{:S(2)}, u32[]{:S(2)}) collective-permute-start(bf16[128,512]{1,0:T(8,128)(2,1)S(1)} %get-tuple-element.22), channel_id=1, source_target_pairs={{0,8},{4,12},{8,0},{12,4},{1,9},{5,13},{9,1},{13,5},{2,10},{6,14},... | collective-permute-start | bytes 393224 | tf_op jit(solution)/shard_map/ppermute | solution.py:269
  10.3 10.0 %collective-permute-start.4 = (bf16[128,512]{1,0:T(8,128)(2,1)S(1)}, bf16[128,512]{1,0:T(8,128)(2,1)S(1)}, u32[]{:S(2)}, u32[]{:S(2)}) collective-permute-start(bf16[128,512]{1,0:T(8,128)(2,1)S(1)} %get-tuple-element.23), channel_id=1, source_target_pairs={{0,12},{4,8},{8,4},{12,0},{1,13},{5,9},{9,5},{13,1},{2,14},{6,10},... | collective-permute-start | bytes 393224 | tf_op jit(solution)/shard_map/ppermute | solution.py:269
  10.3 12.0 %collective-permute-start = (bf16[224,512]{1,0:T(8,128)(2,1)S(1)}, bf16[224,512]{1,0:T(8,128)(2,1)S(1)}, u32[]{:S(2)}, u32[]{:S(2)}) collective-permute-start(bf16[224,512]{1,0:T(8,128)(2,1)S(1)} %get-tuple-element.19), channel_id=1, source_target_pairs={{0,4},{4,0},{8,12},{12,8},{1,5},{5,1},{9,13},{13,9},{2,6},{6,2},{1... | collective-permute-start | bytes 688136 | tf_op jit(solution)/shard_map/ppermute | solution.py:269
  11.2 15.0 %collective-permute-start.2 = (bf16[96,512]{1,0:T(8,128)(2,1)S(1)}, bf16[96,512]{1,0:T(8,128)(2,1)S(1)}, u32[]{:S(2)}, u32[]{:S(2)}) collective-permute-start(bf16[96,512]{1,0:T(8,128)(2,1)S(1)} %add_convert_fusion), channel_id=1, source_target_pairs={{0,8},{4,12},{8,0},{12,4},{1,9},{5,13},{9,1},{13,5},{2,10},{6,14},... | collective-permute-start | bytes 294920 | tf_op jit(solution)/shard_map/ppermute | solution.py:269

commit v4 on v3

--- a/solution.py
+++ b/solution.py
@@ -56,12 +56,8 @@
     return copies
 
 
-def own_part(sums_ref, owner, rows):
-    return sums_ref[pl.ds(pl.multiple_of(owner * rows, rows), rows), :]
-
-
-def border_part(sums_ref, pick_ref, owner):
-    return jnp.dot(pick_ref[owner], sums_ref[...], preferred_element_type=F32)
+def part_of(ref, owner, size):
+    return ref[pl.ds(pl.multiple_of(owner * size, size), size), :]
 
 
 def first_layer_kernel(
@@ -75,19 +71,20 @@
         rest[far // 2 + far + near : 2 * far + near],
     )
     rest = rest[2 * far + near :]
-    owners_ref, count_ref, bcount_ref, brow_v, deg_v, x_v, wn_v, ws_v, ew_v, pick_v, y_v, s_v, sums_v, sems = rest
+    owners_ref, count_ref, bcount_ref, brow_v, deg_v, x_v, wn_v, ws_v, ew_v, pick_v, adj_v, *rest = rest
+    scale_v, y_v, sums_v, border_v, sems = rest
     pairs = (
         (brow_hbm, brow_v),
         (owners_hbm, owners_ref),
-        (x_hbm, x_v),
-        (wn_hbm, wn_v),
         (count_hbm, count_ref),
         (bcount_hbm, bcount_ref),
         (deg_hbm, deg_v),
+        (ew_hbm, ew_v),
+        (x_hbm, x_v),
+        (wn_hbm, wn_v),
         (ws_hbm, ws_v),
-        (ew_hbm, ew_v),
-    )
-    brow_in, owners_in, x_in, wn_in, *counts_in, deg_in, ws_in, ew_in = start_all(pairs, sems)
+    )
+    brow_in, owners_in, *counts_in, deg_in, ew_in, x_in, wn_in, ws_in = start_all(pairs, sems)
     _, _, neigh, cap, rows = ew_v.shape
     total = cuts * rows
     me = lax.axis_index("cuts")
@@ -95,35 +92,53 @@
     eye = (
         lax.broadcasted_iota(jnp.int32, (cap, cap), 0) == lax.broadcasted_iota(jnp.int32, (cap, cap), 1)
     ).astype(F32)
+    span = min(cuts, 4)
+
+    def fill_picks(first):
+        for k in range(neigh):
+            columns = contract_last(eye, brow_v[0, k].astype(F32)).astype(jnp.int32)
+            for u in range(span):
+                target = columns[:, first + u : first + u + 1] + owners_ref[k, 0, first + u] * rows
+                at = u * neigh * cap + k * cap
+                pick_v[at : at + cap, :] = (lane == target).astype(F32).astype(BF16)
+
     brow_in.wait()
     owners_in.wait()
-    for k in range(neigh):
-        columns = contract_last(eye, brow_v[0, k].astype(F32)).astype(jnp.int32)
-        for u in range(cuts):
-            target = columns[:, u : u + 1] + owners_ref[k, 0, u] * rows
-            pick_v[u, k * cap : (k + 1) * cap, :] = (lane == target).astype(F32).astype(BF16)
+    for first in range(0, cuts, span):
+        fill_picks(first)
+        if first == 0:
+            for copy in (*counts_in, deg_in, ew_in):
+                copy.wait()
+        for u in range(first, first + span):
+            at = slice(u * rows, (u + 1) * rows)
+            picks = pick_v[(u - first) * neigh * cap : (u - first + 1) * neigh * cap, :]
+            adj_v[at, :] = contract_first(live_tile(ew_v[0, u], count_ref, bcount_ref, u), picks).astype(BF16)
+            scale_v[at, :] = as_column(1.0 / deg_v[:, at].astype(F32))
     x_in.wait()
     wn_in.wait()
-    y_v[...] = jnp.dot(x_v[...], wn_v[...], preferred_element_type=F32).astype(BF16)
+    for first in range(0, cuts, span):
+        at = slice(first * rows, (first + span) * rows)
+        y_v[at, :] = jnp.dot(x_v[at, :], wn_v[...], preferred_element_type=F32).astype(BF16)
     ws_in.wait()
-    s_v[...] = jnp.dot(x_v[...], ws_v[...], preferred_element_type=F32)
-    for copy in (*counts_in, deg_in, ew_in):
-        copy.wait()
-    for u in range(cuts):
-        at = slice(u * rows, (u + 1) * rows)
-        picked = jnp.dot(pick_v[u], y_v[...], preferred_element_type=F32).astype(BF16)
-        summed = contract_first(live_tile(ew_v[0, u], count_ref, bcount_ref, u), picked)
-        scale = as_column(1.0 / deg_v[:, at].astype(F32))
-        sums_v[at, :] = (s_v[at, :] + summed * scale).astype(BF16)
+    for first in range(0, cuts, span):
+        at = slice(first * rows, (first + span) * rows)
+        selfs = jnp.dot(x_v[at, :], ws_v[...], preferred_element_type=F32)
+        summed = jnp.dot(adj_v[at, :], y_v[...], preferred_element_type=F32)
+        sums_v[at, :] = (selfs + summed * scale_v[at, :]).astype(BF16)
+    for first in range(0, cuts, span):
+        if span < cuts:
+            fill_picks(first)
+        at = slice(first * neigh * cap, (first + span) * neigh * cap)
+        border_v[at, :] = jnp.dot(pick_v[...], sums_v[...], preferred_element_type=F32).astype(BF16)
     for i, out_ref in enumerate(border_refs):
-        out_ref[...] = border_part(sums_v, pick_v, me ^ (2 * i + 3)).astype(BF16)
+        out_ref[...] = part_of(border_v, me ^ (2 * i + 3), neigh * cap)
     for i, out_ref in enumerate(own_refs):
-        out_ref[...] = own_part(sums_v, me ^ (i + 2), rows)
+        out_ref[...] = part_of(sums_v, me ^ (i + 2), rows)
     for step, out_ref in enumerate(slab_refs):
-        out_ref[:rows, :] = own_part(sums_v, me ^ step, rows)
-        out_ref[rows:, :] = border_part(sums_v, pick_v, me ^ step).astype(BF16)
+        out_ref[:rows, :] = part_of(sums_v, me ^ step, rows)
+        out_ref[rows:, :] = part_of(border_v, me ^ step, neigh * cap)
     for i, out_ref in enumerate(local_refs):
-        out_ref[...] = border_part(sums_v, pick_v, me ^ (2 * i + 2))
+        out_ref[...] = part_of(border_v, me ^ (2 * i + 2), neigh * cap)
 
 
 def hidden_rows(parts, b1_ref):
@@ -133,12 +148,11 @@
     return jnp.maximum(total + b1_ref[...], 0.0).astype(BF16)
 
 
-def own_rows_kernel(cuts, reps, subs, *rest):
-    near, far = min(2, cuts), cuts - min(2, cuts)
-    slab_refs, own_refs, rest = rest[:near], rest[near : near + far], rest[near + far :]
+def prepare_kernel(cuts, reps, subs, after_ref, *rest):
     count_hbm, bcount_hbm, ws_hbm, wn_hbm, b1_hbm, b2_hbm, deg_hbm, ew_hbm, id_hbm = rest[:9]
-    z_ref, wn_ref, b1_ref, live_ref, scale_ref, chosen_ref, slots_ref = rest[9:16]
-    ws_v, b2_v, count_ref, bcount_ref, deg_v, ew_v, id_v, sems = rest[16:]
+    w_ref, b1_ref, b2_ref, live_ref, scale_ref, chosen_ref, slots_ref = rest[9:16]
+    count_ref, bcount_ref, deg_v, ew_v, id_v, sems = rest[16:]
+    units = ws_hbm.shape[0]
     rows = ew_v.shape[2]
     me = lax.axis_index("cuts")
     pairs = (
@@ -148,9 +162,9 @@
         (id_hbm, id_v),
         (ew_hbm.at[0, me], ew_v),
         (b1_hbm, b1_ref),
-        (b2_hbm, b2_v),
-        (ws_hbm, ws_v),
-        (wn_hbm, wn_ref),
+        (b2_hbm, b2_ref),
+        (ws_hbm, w_ref.at[pl.ds(0, units)]),
+        (wn_hbm, w_ref.at[pl.ds(units, units)]),
     )
     copies = start_all(pairs, sems)
     for copy in copies[:5]:
@@ -174,20 +188,19 @@
     slots_ref[...] = jnp.broadcast_to(slots, (rows, rows)).astype(BF16)
     for copy in copies[5:]:
         copy.wait()
+
+
+def second_layer_kernel(cuts, *rest):
+    near, far = min(2, cuts), cuts - min(2, cuts)
+    slab_refs, own_refs, border_refs = rest[:near], rest[near : near + far], rest[near + far : near + far + far // 2]
+    w_ref, b1_ref, b2_ref, live_ref, scale_ref, chosen_ref, slots_ref, out_ref = rest[near + far + far // 2 :]
+    rows = chosen_ref.shape[0]
+    units = w_ref.shape[1]
     own = hidden_rows([slab[:rows, :] for slab in slab_refs] + [part[...] for part in own_refs], b1_ref)
-    z_ref[...] = jnp.dot(own, ws_v[...], preferred_element_type=F32) + b2_v[...]
-
-
-def border_rows_kernel(cuts, *rest):
-    near, far = min(2, cuts), cuts - min(2, cuts)
-    slab_refs, border_refs, rest = rest[:near], rest[near : near + far // 2], rest[near + far // 2 :]
-    z_ref, wn_ref, b1_ref, live_ref, scale_ref, chosen_ref, slots_ref, out_ref = rest
-    rows = chosen_ref.shape[0]
-    units = wn_ref.shape[1]
     border = hidden_rows([slab[rows:, :] for slab in slab_refs] + [part[...] for part in border_refs], b1_ref)
     summed = contract_first(live_ref[...], border)
     mean = (summed * scale_ref[:, :1]).astype(BF16)
-    z = z_ref[...] + jnp.dot(mean, wn_ref[...], preferred_element_type=F32)
+    z = jnp.dot(jnp.concatenate([own, mean], axis=1), w_ref[...], preferred_element_type=F32) + b2_ref[...]
     scale = lax.rsqrt(jnp.mean(z * z, axis=1, keepdims=True) + 1e-05)
     normalized = (z * scale).astype(BF16)
     out_ref[:, :units] = jnp.dot(chosen_ref[...], normalized, preferred_element_type=F32).astype(BF16)
@@ -232,14 +245,14 @@
     bcounts = boundary_count.transpose(2, 0, 1)
     brows = boundary_rows.transpose(0, 2, 1, 3)
     counts_held = [SMEM(a.shape, jnp.int32) for a in (owners, neighbor_count, bcounts)]
-    held = 2 * (total * width + 2 * width * units + cuts * border * total + 4 * total * units)
-    held += 2 * cuts * (rows + border) * units + 8 * total * units + 2 * cuts * border * rows
+    held = total * width + 2 * width * units + total * total + 2 * total * units + 256 * total
+    held += min(cuts, 4) * border * total + cuts * border * (units + rows) + units * (near * (rows + border) + far * (rows + border))
     sent = pl.pallas_call(
         functools.partial(first_layer_kernel, cuts),
         out_shape=[border_slab] * (far // 2)
         + [own_slab] * far
         + [slab] * near
-        + [shape((border, units), F32)] * (far // 2),
+        + [border_slab] * (far // 2),
         in_specs=[hbm] * 9,
         out_specs=[vmem] * (2 * far + near),
         scratch_shapes=[
@@ -250,13 +263,15 @@
             pltpu.VMEM((width, units), BF16),
             pltpu.VMEM((width, units), BF16),
             pltpu.VMEM(edge_weight.shape, BF16),
-            pltpu.VMEM((cuts, border, total), BF16),
+            pltpu.VMEM((min(cuts, 4) * border, total), BF16),
+            pltpu.VMEM((total, total), BF16),
+            pltpu.VMEM((total, 1), F32),
             pltpu.VMEM((total, units), BF16),
-            pltpu.VMEM((total, units), F32),
             pltpu.VMEM((total, units), BF16),
+            pltpu.VMEM((cuts * border, units), BF16),
             pltpu.SemaphoreType.DMA((9,)),
         ],
-        compiler_params=pltpu.CompilerParams(vmem_limit_bytes=held + (8 << 20)),
+        compiler_params=pltpu.CompilerParams(vmem_limit_bytes=2 * held + (8 << 20)),
         name="first_layer",
     )(*in_hbm(owners, neighbor_count, bcounts, features, w_neigh1, w_self1, degree, brows, edge_weight))
     sent = list(sent)
@@ -270,24 +285,22 @@
     pairs = [trade(a, 1) for a in pairs]
     owns = [trade(a, i + 2) for i, a in enumerate(owns)]
     slabs = slabs[:1] + [trade(a, 1) for a in slabs[1:]]
-    paired = [(a + b.astype(F32)).astype(BF16) for a, b in zip(local, pairs)]
+    paired = [(a.astype(F32) + b.astype(F32)).astype(BF16) for a, b in zip(local, pairs)]
     borders = [trade(a, 2 * i + 2) for i, a in enumerate(paired)]
     prepared = pl.pallas_call(
-        functools.partial(own_rows_kernel, cuts, reps, subs),
+        functools.partial(prepare_kernel, cuts, reps, subs),
         out_shape=[
-            shape((rows, units), F32),
-            shape((units, units), BF16),
+            shape((2 * units, units), BF16),
+            shape((1, units), F32),
             shape((1, units), F32),
             shape((border, rows), BF16),
             shape((rows, rows), F32),
             shape((rows, rows), BF16),
             shape((rows, rows), BF16),
         ],
-        in_specs=[vmem] * cuts + [hbm] * 9,
+        in_specs=[pl.BlockSpec(memory_space=pl.ANY)] + [hbm] * 9,
         out_specs=[vmem] * 7,
         scratch_shapes=[
-            pltpu.VMEM((units, units), BF16),
-            pltpu.VMEM((1, units), F32),
             *counts_held[1:],
             pltpu.VMEM(degree.shape, jnp.int32),
             pltpu.VMEM(edge_weight.shape[2:], BF16),
@@ -295,22 +308,22 @@
             pltpu.SemaphoreType.DMA((9,)),
         ],
         compiler_params=pltpu.CompilerParams(vmem_limit_bytes=24 << 20),
-        cost_estimate=pl.CostEstimate(flops=2 * rows * units * units, bytes_accessed=4 * units * units, transcendentals=0),
-        name="own_rows",
+        cost_estimate=pl.CostEstimate(flops=rows * rows * units, bytes_accessed=4 * units * units, transcendentals=0),
+        name="prepare",
     )(
-        *slabs,
-        *owns,
+        sent[-1],
         *in_hbm(neighbor_count, bcounts, w_self2, w_neigh2, bias1.reshape(1, units), bias2.reshape(1, units)),
         *in_hbm(degree, edge_weight, node_id),
     )
+    arrived = slabs + owns + borders
     payload = pl.pallas_call(
-        functools.partial(border_rows_kernel, cuts),
+        functools.partial(second_layer_kernel, cuts),
         out_shape=shape((rows, units + rows), BF16),
-        in_specs=[vmem] * (near + far // 2 + 7),
+        in_specs=[vmem] * (len(arrived) + 7),
         out_specs=vmem,
         compiler_params=pltpu.CompilerParams(vmem_limit_bytes=24 << 20),
-        name="border_rows",
-    )(*slabs, *borders, *prepared)
+        name="second_layer",
+    )(*arrived, *prepared)
     peers = cuts * reps
     moved = lax.all_to_all(
         payload.reshape(peers, rows // peers, units + rows), ("cuts", "rep"), split_axis=0, concat_axis=0, tiled=True

time: 41 us -> 40.1 us (0.978)
  Pallas kernels: 8.63 us -> 7.49 us
    pallas_call x1, Pallas kernels: 4.61 us -> 3.74 us  [body(): pl.pallas_call(functools.partial(first_layer_kernel, cuts), out_shape=[bo...]
  transfers between devices with their start and end apart: 5 -> 5, of which waited for: 3 -> 2; matrix products, arithmetic and copies ran while one was open for 0% -> 0% of each run, Pallas kernels for 4% -> 3%
where the time goes in v4:
time: 40.1 us; the launch traced here: 39.9 us
  blocking collectives  12.2 us (30%)
  starting transfers between devices  10.2 us (25%)
  waiting for transfers between devices  10 us (25%)
  Pallas kernels  7.49 us (19%)
    all_to_all x1, blocking collectives, body(): lax.all_to_all(payload.reshape(peers, rows // peers, units + rows), ('cut...  12.2 us
    ppermute x5, starting transfers between devices, body(): trade = lambda a, step: lax.ppermute(a, 'cuts', partner_pairs(step, cuts))  10.2 us
    ppermute x5, waiting for transfers between devices, body(): trade = lambda a, step: lax.ppermute(a, 'cuts', partner_pairs(step, cuts))  10 us
    pallas_call x1, Pallas kernels, body(): pl.pallas_call(functools.partial(first_layer_kernel, cuts), out_shape=[bo...  3.74 us
    pallas_call x1, Pallas kernels, body(): pl.pallas_call(placing_kernel, out_shape=shape((rows, units), BF16), in_s...  1.79 us
    pallas_call x1, Pallas kernels, body(): pl.pallas_call(functools.partial(prepare_kernel, cuts, reps, subs), out_s...  1.36 us
  transfers between devices with their start and end apart: 5, of which 2 were waited for; matrix products, arithmetic and copies ran while one was open for 0% of the time, Pallas kernels for 3%

profile of v4, /device:TPU:0, one launch (start us, length us, event | category | flops | bytes accessed | tf_op | source)
XLA Modules:
  0.0 39.9 jit_solution(13927971421109265195)
XLA Ops:
  0.0 3.7 %first_layer.1 = (bf16[96,512]{1,0:T(8,128)(2,1)S(1)}, bf16[128,512]{1,0:T(8,128)(2,1)S(1)}, bf16[128,512]{1,0:T(8,128)(2,1)S(1)}, bf16[224,512]{1,0:T(8,128)(2,...) custom-call(s32[3,1,4]{2,1,0:T(1,128)} %bitcast.14, s32[1,4]{1,0:T(1,128)} %rest_0_.1, ...), custom_call_target="tpu_custom_call" | custom-call | tf_op jit(solution)/shard_map/first_layer/pallas_call | solution.py:250
  3.7 3.1 %collective-permute-start.3 = (bf16[96,512]{1,0:T(8,128)(2,1)S(1)}, bf16[96,512]{1,0:T(8,128)(2,1)S(1)}, u32[]{:S(2)}, u32[]{:S(2)}) collective-permute-start(bf16[96,512]{1,0:T(8,128)(2,1)S(1)} %get-tuple-element.23), channel_id=1, source_target_pairs={{0,4},{4,0},{8,12},{12,8},{1,5},{5,1},{9,13},{13,9},{2,6},{6,2},{1... | collective-permute-start | bytes 294920 | tf_op jit(solution)/shard_map/ppermute | solution.py:284
  6.8 2.6 %collective-permute-start.1 = (bf16[128,512]{1,0:T(8,128)(2,1)S(1)}, bf16[128,512]{1,0:T(8,128)(2,1)S(1)}, u32[]{:S(2)}, u32[]{:S(2)}) collective-permute-start(bf16[128,512]{1,0:T(8,128)(2,1)S(1)} %get-tuple-element.20), channel_id=1, source_target_pairs={{0,8},{4,12},{8,0},{12,4},{1,9},{5,13},{9,1},{13,5},{2,10},{6,14},... | collective-permute-start | bytes 393224 | tf_op jit(solution)/shard_map/ppermute | solution.py:284
  9.5 0.0 collective-permute-start.2
  9.5 0.9 %collective-permute-start = (bf16[224,512]{1,0:T(8,128)(2,1)S(1)}, bf16[224,512]{1,0:T(8,128)(2,1)S(1)}, u32[]{:S(2)}, u32[]{:S(2)}) collective-permute-start(bf16[224,512]{1,0:T(8,128)(2,1)S(1)} %get-tuple-element.19), channel_id=1, source_target_pairs={{0,4},{4,0},{8,12},{12,8},{1,5},{5,1},{9,13},{13,9},{2,6},{6,2},{1... | collective-permute-start | bytes 688136 | tf_op jit(solution)/shard_map/ppermute | solution.py:284
  10.3 0.0 collective-permute-done.3
  10.4 3.6 %collective-permute-start.4 = (bf16[96,512]{1,0:T(8,128)(2,1)S(1)}, bf16[96,512]{1,0:T(8,128)(2,1)S(1)}, u32[]{:S(2)}, u32[]{:S(2)}) collective-permute-start(bf16[96,512]{1,0:T(8,128)(2,1)S(1)} %add_convert_fusion), channel_id=1, source_target_pairs={{0,8},{4,12},{8,0},{12,4},{1,9},{5,13},{9,1},{13,5},{2,10},{6,14},... | collective-permute-start | bytes 294920 | tf_op jit(solution)/shard_map/ppermute | solution.py:284
  13.9 1.4 %prepare.1 = (bf16[1024,512]{1,0:T(8,128)(2,1)S(1)}, f32[1,512]{1,0:T(1,128)S(1)}, f32[1,512]{1,0:T(1,128)S(1)}, bf16[96,128]{1,0:T(8,128)(2,1)S(1)}, f32[128,12...) custom-call(bf16[96,512]{1,0:T(8,128)(2,1)S(1)} %get-tuple-element.22.after_ref, ...), custom_call_target="tpu_custom_call" | custom-call | flops 8388608 | bytes 1048576 | tf_op jit(solution)/shard_map/prepare/pallas_call | solution.py:290
  15.3 4.2 %collective-permute-done.1.rest_2_ = bf16[128,512]{1,0:T(8,128)(2,1)S(1)} collective-permute-done((bf16[128,512]{1,0:T(8,128)(2,1)S(1)}, bf16[128,512]{1,0:T(8,128)(2,1)S(1)}, u32[]{:S(2)}, u32[]{:S(2)}) %collective-permute-start.1) | collective-permute-done | bytes 131104 | tf_op jit(solution)/shard_map/ppermute | solution.py:284
  19.5 0.0 collective-permute-done.2.rest_3_
  19.5 5.9 %collective-permute-done.4.rest_4_ = bf16[96,512]{1,0:T(8,128)(2,1)S(1)} collective-permute-done((bf16[96,512]{1,0:T(8,128)(2,1)S(1)}, bf16[96,512]{1,0:T(8,128)(2,1)S(1)}, u32[]{:S(2)}, u32[]{:S(2)}) %collective-permute-start.4) | collective-permute-done | bytes 98336 | tf_op jit(solution)/shard_map/ppermute | solution.py:284
  25.3 0.0 collective-permute-done.rest_1_
  25.4 0.6 %second_layer.1 = bf16[128,640]{1,0:T(8,128)(2,1)S(1)} custom-call(bf16[224,512]{1,0:T(8,128)(2,1)S(1)} %get-tuple-element.18.rest_0_, bf16[224,512]{1,0:T(8,128)(2,1)S(1)} %collective-permute-done.rest_1_, bf16[128,512]{1,0:T(8,128)(2,1)S(1)} %collective-permute-done.1.rest_2_, bf16[128,512]{1,0:T(8,128)(2,1)S(1)} %collective-permute-done.2.rest_3_, ...), custom_call_target="tpu_custom_call" | custom-call | tf_op jit(solution)/shard_map/second_layer/pallas_call | solution.py:319
  26.0 12.2 %all_to_all.5 = bf16[8,16,640]{2,1,0:T(8,128)(2,1)} all-to-all(bf16[8,16,640]{2,1,0:T(8,128)(2,1)S(1)} %bitcast.7), channel_id=1, replica_groups=mesh['groups'=2,'cuts'=4,'rep'=2,'sub'=2] {'cuts','rep'}, dimensions={0} | all-to-all | bytes 327680 | tf_op jit(solution)/shard_map/all_to_all | solution.py:328
  38.1 1.8 %placing.1 = bf16[128,512]{1,0:T(8,128)(2,1)} custom-call(bf16[128,640]{1,0:T(8,128)(2,1)} %bitcast.8), custom_call_target="tpu_custom_call" | custom-call | tf_op jit(solution)/shard_map/placing/pallas_call | solution.py:331
  (1 shorter events, 0.0 us)
Async XLA Ops:
  3.7 6.6 %collective-permute-start.3 = (bf16[96,512]{1,0:T(8,128)(2,1)S(1)}, bf16[96,512]{1,0:T(8,128)(2,1)S(1)}, u32[]{:S(2)}, u32[]{:S(2)}) collective-permute-start(bf16[96,512]{1,0:T(8,128)(2,1)S(1)} %get-tuple-element.23), channel_id=1, source_target_pairs={{0,4},{4,0},{8,12},{12,8},{1,5},{5,1},{9,13},{13,9},{2,6},{6,2},{1... | collective-permute-start | bytes 294920 | tf_op jit(solution)/shard_map/ppermute | solution.py:284
  6.8 12.6 %collective-permute-start.1 = (bf16[128,512]{1,0:T(8,128)(2,1)S(1)}, bf16[128,512]{1,0:T(8,128)(2,1)S(1)}, u32[]{:S(2)}, u32[]{:S(2)}) collective-permute-start(bf16[128,512]{1,0:T(8,128)(2,1)S(1)} %get-tuple-element.20), channel_id=1, source_target_pairs={{0,8},{4,12},{8,0},{12,4},{1,9},{5,13},{9,1},{13,5},{2,10},{6,14},... | collective-permute-start | bytes 393224 | tf_op jit(solution)/shard_map/ppermute | solution.py:284
  9.5 10.0 %collective-permute-start.2 = (bf16[128,512]{1,0:T(8,128)(2,1)S(1)}, bf16[128,512]{1,0:T(8,128)(2,1)S(1)}, u32[]{:S(2)}, u32[]{:S(2)}) collective-permute-start(bf16[128,512]{1,0:T(8,128)(2,1)S(1)} %get-tuple-element.21), channel_id=1, source_target_pairs={{0,12},{4,8},{8,4},{12,0},{1,13},{5,9},{9,5},{13,1},{2,14},{6,10},... | collective-permute-start | bytes 393224 | tf_op jit(solution)/shard_map/ppermute | solution.py:284
  9.5 15.9 %collective-permute-start = (bf16[224,512]{1,0:T(8,128)(2,1)S(1)}, bf16[224,512]{1,0:T(8,128)(2,1)S(1)}, u32[]{:S(2)}, u32[]{:S(2)}) collective-permute-start(bf16[224,512]{1,0:T(8,128)(2,1)S(1)} %get-tuple-element.19), channel_id=1, source_target_pairs={{0,4},{4,0},{8,12},{12,8},{1,5},{5,1},{9,13},{13,9},{2,6},{6,2},{1... | collective-permute-start | bytes 688136 | tf_op jit(solution)/shard_map/ppermute | solution.py:284
  10.4 15.0 %collective-permute-start.4 = (bf16[96,512]{1,0:T(8,128)(2,1)S(1)}, bf16[96,512]{1,0:T(8,128)(2,1)S(1)}, u32[]{:S(2)}, u32[]{:S(2)}) collective-permute-start(bf16[96,512]{1,0:T(8,128)(2,1)S(1)} %add_convert_fusion), channel_id=1, source_target_pairs={{0,8},{4,12},{8,0},{12,4},{1,9},{5,13},{9,1},{13,5},{2,10},{6,14},... | collective-permute-start | bytes 294920 | tf_op jit(solution)/shard_map/ppermute | solution.py:284

commit v5 on v4

--- a/solution.py
+++ b/solution.py
@@ -11,6 +11,11 @@
 BF16 = jnp.bfloat16
 VMEM = pltpu.VMEM
 SMEM = pltpu.SMEM
+DIRECT = 112
+
+
+def direct_rows(rows):
+    return rows * DIRECT // 128
 
 
 def partner_pairs(step, total):
@@ -54,10 +59,6 @@
     for copy in copies:
         copy.start()
     return copies
-
-
-def part_of(ref, owner, size):
-    return ref[pl.ds(pl.multiple_of(owner * size, size), size), :]
 
 
 def first_layer_kernel(
@@ -130,15 +131,25 @@
             fill_picks(first)
         at = slice(first * neigh * cap, (first + span) * neigh * cap)
         border_v[at, :] = jnp.dot(pick_v[...], sums_v[...], preferred_element_type=F32).astype(BF16)
+    direct = direct_rows(rows)
+    border = neigh * cap
+
+    def own_at(owner, first, size):
+        return pl.ds(pl.multiple_of(owner * rows + first, 16), size)
+
+    def paired_part(out_ref, owner):
+        out_ref[: rows - direct, :] = sums_v[own_at(owner, direct, rows - direct), :]
+        out_ref[rows - direct :, :] = border_v[pl.ds(pl.multiple_of(owner * border, border), border), :]
+
     for i, out_ref in enumerate(border_refs):
-        out_ref[...] = part_of(border_v, me ^ (2 * i + 3), neigh * cap)
+        paired_part(out_ref, me ^ (2 * i + 3))
     for i, out_ref in enumerate(own_refs):
-        out_ref[...] = part_of(sums_v, me ^ (i + 2), rows)
+        out_ref[...] = sums_v[own_at(me ^ (i + 2), 0, direct), :]
     for step, out_ref in enumerate(slab_refs):
-        out_ref[:rows, :] = part_of(sums_v, me ^ step, rows)
-        out_ref[rows:, :] = part_of(border_v, me ^ step, neigh * cap)
+        out_ref[:direct, :] = sums_v[own_at(me ^ step, 0, direct), :]
+        paired_part(out_ref.at[pl.ds(direct, rows - direct + border)], me ^ step)
     for i, out_ref in enumerate(local_refs):
-        out_ref[...] = part_of(border_v, me ^ (2 * i + 2), neigh * cap)
+        paired_part(out_ref, me ^ (2 * i + 2))
 
 
 def hidden_rows(parts, b1_ref):
@@ -196,8 +207,11 @@
     w_ref, b1_ref, b2_ref, live_ref, scale_ref, chosen_ref, slots_ref, out_ref = rest[near + far + far // 2 :]
     rows = chosen_ref.shape[0]
     units = w_ref.shape[1]
-    own = hidden_rows([slab[:rows, :] for slab in slab_refs] + [part[...] for part in own_refs], b1_ref)
-    border = hidden_rows([slab[rows:, :] for slab in slab_refs] + [part[...] for part in border_refs], b1_ref)
+    direct = direct_rows(rows)
+    first = hidden_rows([slab[:direct, :] for slab in slab_refs] + [part[...] for part in own_refs], b1_ref)
+    others = hidden_rows([slab[direct:, :] for slab in slab_refs] + [part[...] for part in border_refs], b1_ref)
+    own = jnp.concatenate([first, others[: rows - direct]], axis=0)
+    border = others[rows - direct :]
     summed = contract_first(live_ref[...], border)
     mean = (summed * scale_ref[:, :1]).astype(BF16)
     z = jnp.dot(jnp.concatenate([own, mean], axis=1), w_ref[...], preferred_element_type=F32) + b2_ref[...]
@@ -239,7 +253,8 @@
     hbm = pl.BlockSpec(memory_space=pltpu.HBM)
     shape = jax.ShapeDtypeStruct
     slab = shape((rows + border, units), BF16)
-    own_slab, border_slab = shape((rows, units), BF16), shape((border, units), BF16)
+    direct = direct_rows(rows)
+    own_slab, border_slab = shape((direct, units), BF16), shape((rows - direct + border, units), BF16)
     near, far = min(2, cuts), cuts - min(2, cuts)
     owners = neighbor_owners.transpose(2, 0, 1)
     bcounts = boundary_count.transpose(2, 0, 1)
@@ -334,7 +349,7 @@
         in_specs=[vmem],
         out_specs=vmem,
         name="placing",
-    )(moved.reshape(rows, units + rows))
+    )(pltpu.with_memory_space_constraint(moved.reshape(rows, units + rows), pltpu.VMEM))
 
 
 def solution(mesh):

time: 40.1 us -> 38.4 us (0.958)
  Pallas kernels: 7.49 us -> 6.58 us
  waiting for transfers between devices: 10 us -> 9.33 us
    pallas_call x1, Pallas kernels: 1.79 us -> 0.87 us  [body(): pl.pallas_call(placing_kernel, out_shape=shape((rows, units), BF16), in_s...]
    ppermute x5, waiting for transfers between devices: 10 us -> 9.33 us  [body(): trade = lambda a, step: lax.ppermute(a, 'cuts', partner_pairs(step, cuts))]
  transfers between devices with their start and end apart: 5 -> 5, of which waited for: 2 -> 2; matrix products, arithmetic and copies ran while one was open for 0% -> 0% of each run, Pallas kernels for 3% -> 4%
where the time goes in v5:
time: 38.4 us; the launch traced here: 38.2 us
  blocking collectives  12 us (31%)
  starting transfers between devices  10.2 us (27%)
  waiting for transfers between devices  9.33 us (24%)
  Pallas kernels  6.58 us (17%)
    all_to_all x1, blocking collectives, body(): lax.all_to_all(payload.reshape(peers, rows // peers, units + rows), ('cut...  12 us
    ppermute x5, starting transfers between devices, body(): trade = lambda a, step: lax.ppermute(a, 'cuts', partner_pairs(step, cuts))  10.2 us
    ppermute x5, waiting for transfers between devices, body(): trade = lambda a, step: lax.ppermute(a, 'cuts', partner_pairs(step, cuts))  9.33 us
    pallas_call x1, Pallas kernels, body(): pl.pallas_call(functools.partial(first_layer_kernel, cuts), out_shape=[bo...  3.74 us
    pallas_call x1, Pallas kernels, body(): pl.pallas_call(functools.partial(prepare_kernel, cuts, reps, subs), out_s...  1.36 us
    pallas_call x1, Pallas kernels, body(): pl.pallas_call(placing_kernel, out_shape=shape((rows, units), BF16), in_s...  0.87 us
  transfers between devices with their start and end apart: 5, of which 2 were waited for; matrix products, arithmetic and copies ran while one was open for 0% of the time, Pallas kernels for 4%

profile of v5, /device:TPU:0, one launch (start us, length us, event | category | flops | bytes accessed | tf_op | source)
XLA Modules:
  0.0 38.2 jit_solution(12063991810595762324)
XLA Ops:
  0.0 3.7 %first_layer.1 = (bf16[112,512]{1,0:T(8,128)(2,1)S(1)}, bf16[112,512]{1,0:T(8,128)(2,1)S(1)}, bf16[112,512]{1,0:T(8,128)(2,1)S(1)}, bf16[224,512]{1,0:T(8,128)(2...) custom-call(s32[3,1,4]{2,1,0:T(1,128)} %bitcast.14, s32[1,4]{1,0:T(1,128)} %rest_0_.1, ...), custom_call_target="tpu_custom_call" | custom-call | tf_op jit(solution)/shard_map/first_layer/pallas_call | solution.py:265
  3.7 3.1 %collective-permute-start.3 = (bf16[112,512]{1,0:T(8,128)(2,1)S(1)}, bf16[112,512]{1,0:T(8,128)(2,1)S(1)}, u32[]{:S(2)}, u32[]{:S(2)}) collective-permute-start(bf16[112,512]{1,0:T(8,128)(2,1)S(1)} %get-tuple-element.23), channel_id=1, source_target_pairs={{0,4},{4,0},{8,12},{12,8},{1,5},{5,1},{9,13},{13,9},{2,6},{6,2},{1... | collective-permute-start | bytes 344072 | tf_op jit(solution)/shard_map/ppermute | solution.py:299
  6.8 2.6 %collective-permute-start.1 = (bf16[112,512]{1,0:T(8,128)(2,1)S(1)}, bf16[112,512]{1,0:T(8,128)(2,1)S(1)}, u32[]{:S(2)}, u32[]{:S(2)}) collective-permute-start(bf16[112,512]{1,0:T(8,128)(2,1)S(1)} %get-tuple-element.20), channel_id=1, source_target_pairs={{0,8},{4,12},{8,0},{12,4},{1,9},{5,13},{9,1},{13,5},{2,10},{6,14},... | collective-permute-start | bytes 344072 | tf_op jit(solution)/shard_map/ppermute | solution.py:299
  9.5 0.0 collective-permute-start.2
  9.5 0.9 %collective-permute-start = (bf16[224,512]{1,0:T(8,128)(2,1)S(1)}, bf16[224,512]{1,0:T(8,128)(2,1)S(1)}, u32[]{:S(2)}, u32[]{:S(2)}) collective-permute-start(bf16[224,512]{1,0:T(8,128)(2,1)S(1)} %get-tuple-element.19), channel_id=1, source_target_pairs={{0,4},{4,0},{8,12},{12,8},{1,5},{5,1},{9,13},{13,9},{2,6},{6,2},{1... | collective-permute-start | bytes 688136 | tf_op jit(solution)/shard_map/ppermute | solution.py:299
  10.3 0.0 collective-permute-done.3
  10.4 3.6 %collective-permute-start.4 = (bf16[112,512]{1,0:T(8,128)(2,1)S(1)}, bf16[112,512]{1,0:T(8,128)(2,1)S(1)}, u32[]{:S(2)}, u32[]{:S(2)}) collective-permute-start(bf16[112,512]{1,0:T(8,128)(2,1)S(1)} %add_convert_fusion), channel_id=1, source_target_pairs={{0,8},{4,12},{8,0},{12,4},{1,9},{5,13},{9,1},{13,5},{2,10},{6,14},... | collective-permute-start | bytes 344072 | tf_op jit(solution)/shard_map/ppermute | solution.py:299
  14.0 1.4 %prepare.1 = (bf16[1024,512]{1,0:T(8,128)(2,1)S(1)}, f32[1,512]{1,0:T(1,128)S(1)}, f32[1,512]{1,0:T(1,128)S(1)}, bf16[96,128]{1,0:T(8,128)(2,1)S(1)}, f32[128,12...) custom-call(bf16[112,512]{1,0:T(8,128)(2,1)S(1)} %get-tuple-element.22.after_ref, ...), custom_call_target="tpu_custom_call" | custom-call | flops 8388608 | bytes 1048576 | tf_op jit(solution)/shard_map/prepare/pallas_call | solution.py:305
  15.4 3.2 %collective-permute-done.1.rest_2_ = bf16[112,512]{1,0:T(8,128)(2,1)S(1)} collective-permute-done((bf16[112,512]{1,0:T(8,128)(2,1)S(1)}, bf16[112,512]{1,0:T(8,128)(2,1)S(1)}, u32[]{:S(2)}, u32[]{:S(2)}) %collective-permute-start.1) | collective-permute-done | bytes 114720 | tf_op jit(solution)/shard_map/ppermute | solution.py:299
  18.6 0.0 collective-permute-done.2.rest_3_
  18.6 6.1 %collective-permute-done.4.rest_4_ = bf16[112,512]{1,0:T(8,128)(2,1)S(1)} collective-permute-done((bf16[112,512]{1,0:T(8,128)(2,1)S(1)}, bf16[112,512]{1,0:T(8,128)(2,1)S(1)}, u32[]{:S(2)}, u32[]{:S(2)}) %collective-permute-start.4) | collective-permute-done | bytes 114720 | tf_op jit(solution)/shard_map/ppermute | solution.py:299
  24.7 0.0 collective-permute-done.rest_1_
  24.7 0.6 %second_layer.1 = bf16[128,640]{1,0:T(8,128)(2,1)S(1)} custom-call(bf16[224,512]{1,0:T(8,128)(2,1)S(1)} %get-tuple-element.18.rest_0_, bf16[224,512]{1,0:T(8,128)(2,1)S(1)} %collective-permute-done.rest_1_, bf16[112,512]{1,0:T(8,128)(2,1)S(1)} %collective-permute-done.1.rest_2_, bf16[112,512]{1,0:T(8,128)(2,1)S(1)} %collective-permute-done.2.rest_3_, ...), custom_call_target="tpu_custom_call" | custom-call | tf_op jit(solution)/shard_map/second_layer/pallas_call | solution.py:334
  25.3 12.0 %all_to_all.5 = bf16[8,16,640]{2,1,0:T(8,128)(2,1)S(1)} all-to-all(bf16[8,16,640]{2,1,0:T(8,128)(2,1)S(1)} %bitcast.7), channel_id=1, replica_groups=mesh['groups'=2,'cuts'=4,'rep'=2,'sub'=2] {'cuts','rep'}, dimensions={0} | all-to-all | bytes 327680 | tf_op jit(solution)/shard_map/all_to_all | solution.py:343
  37.3 0.9 %placing.1 = bf16[128,512]{1,0:T(8,128)(2,1)} custom-call(bf16[128,640]{1,0:T(8,128)(2,1)S(1)} %bitcast.8), custom_call_target="tpu_custom_call" | custom-call | tf_op jit(solution)/shard_map/placing/pallas_call | solution.py:346
  (1 shorter events, 0.0 us)
Async XLA Ops:
  3.7 6.6 %collective-permute-start.3 = (bf16[112,512]{1,0:T(8,128)(2,1)S(1)}, bf16[112,512]{1,0:T(8,128)(2,1)S(1)}, u32[]{:S(2)}, u32[]{:S(2)}) collective-permute-start(bf16[112,512]{1,0:T(8,128)(2,1)S(1)} %get-tuple-element.23), channel_id=1, source_target_pairs={{0,4},{4,0},{8,12},{12,8},{1,5},{5,1},{9,13},{13,9},{2,6},{6,2},{1... | collective-permute-start | bytes 344072 | tf_op jit(solution)/shard_map/ppermute | solution.py:299
  6.8 11.7 %collective-permute-start.1 = (bf16[112,512]{1,0:T(8,128)(2,1)S(1)}, bf16[112,512]{1,0:T(8,128)(2,1)S(1)}, u32[]{:S(2)}, u32[]{:S(2)}) collective-permute-start(bf16[112,512]{1,0:T(8,128)(2,1)S(1)} %get-tuple-element.20), channel_id=1, source_target_pairs={{0,8},{4,12},{8,0},{12,4},{1,9},{5,13},{9,1},{13,5},{2,10},{6,14},... | collective-permute-start | bytes 344072 | tf_op jit(solution)/shard_map/ppermute | solution.py:299
  9.5 9.1 %collective-permute-start.2 = (bf16[112,512]{1,0:T(8,128)(2,1)S(1)}, bf16[112,512]{1,0:T(8,128)(2,1)S(1)}, u32[]{:S(2)}, u32[]{:S(2)}) collective-permute-start(bf16[112,512]{1,0:T(8,128)(2,1)S(1)} %get-tuple-element.21), channel_id=1, source_target_pairs={{0,12},{4,8},{8,4},{12,0},{1,13},{5,9},{9,5},{13,1},{2,14},{6,10},... | collective-permute-start | bytes 344072 | tf_op jit(solution)/shard_map/ppermute | solution.py:299
  9.5 15.2 %collective-permute-start = (bf16[224,512]{1,0:T(8,128)(2,1)S(1)}, bf16[224,512]{1,0:T(8,128)(2,1)S(1)}, u32[]{:S(2)}, u32[]{:S(2)}) collective-permute-start(bf16[224,512]{1,0:T(8,128)(2,1)S(1)} %get-tuple-element.19), channel_id=1, source_target_pairs={{0,4},{4,0},{8,12},{12,8},{1,5},{5,1},{9,13},{13,9},{2,6},{6,2},{1... | collective-permute-start | bytes 688136 | tf_op jit(solution)/shard_map/ppermute | solution.py:299
  10.4 14.3 %collective-permute-start.4 = (bf16[112,512]{1,0:T(8,128)(2,1)S(1)}, bf16[112,512]{1,0:T(8,128)(2,1)S(1)}, u32[]{:S(2)}, u32[]{:S(2)}) collective-permute-start(bf16[112,512]{1,0:T(8,128)(2,1)S(1)} %add_convert_fusion), channel_id=1, source_target_pairs={{0,8},{4,12},{8,0},{12,4},{1,9},{5,13},{9,1},{13,5},{2,10},{6,14},... | collective-permute-start | bytes 344072 | tf_op jit(solution)/shard_map/ppermute | solution.py:299

commit v6 on v5

--- a/solution.py
+++ b/solution.py
@@ -11,11 +11,19 @@
 BF16 = jnp.bfloat16
 VMEM = pltpu.VMEM
 SMEM = pltpu.SMEM
-DIRECT = 112
+DIRECT = 80
 
 
 def direct_rows(rows):
     return rows * DIRECT // 128
+
+
+def pair_chunks(rows, border):
+    direct = direct_rows(rows)
+    units = (rows - direct + border) // 16
+    pieces = -(-units * 16 // direct)
+    ends = [16 * (units * i // pieces) for i in range(pieces + 1)]
+    return list(zip(ends[:-1], ends[1:]))
 
 
 def partner_pairs(step, total):
@@ -203,13 +211,18 @@
 
 def second_layer_kernel(cuts, *rest):
     near, far = min(2, cuts), cuts - min(2, cuts)
-    slab_refs, own_refs, border_refs = rest[:near], rest[near : near + far], rest[near + far : near + far + far // 2]
-    w_ref, b1_ref, b2_ref, live_ref, scale_ref, chosen_ref, slots_ref, out_ref = rest[near + far + far // 2 :]
+    slab_refs, own_refs, border_refs = rest[:near], rest[near : near + far], rest[near + far : -8]
+    w_ref, b1_ref, b2_ref, live_ref, scale_ref, chosen_ref, slots_ref, out_ref = rest[-8:]
     rows = chosen_ref.shape[0]
+    chunks = pair_chunks(rows, live_ref.shape[0])
     units = w_ref.shape[1]
     direct = direct_rows(rows)
     first = hidden_rows([slab[:direct, :] for slab in slab_refs] + [part[...] for part in own_refs], b1_ref)
-    others = hidden_rows([slab[direct:, :] for slab in slab_refs] + [part[...] for part in border_refs], b1_ref)
+    pieces = []
+    for i, (low, high) in enumerate(chunks):
+        parts = [slab[direct + low : direct + high, :] for slab in slab_refs]
+        pieces.append(hidden_rows(parts + [part[...] for part in border_refs[i :: len(chunks)]], b1_ref))
+    others = jnp.concatenate(pieces, axis=0)
     own = jnp.concatenate([first, others[: rows - direct]], axis=0)
     border = others[rows - direct :]
     summed = contract_first(live_ref[...], border)
@@ -299,9 +312,11 @@
     trade = lambda a, step: lax.ppermute(a, "cuts", partner_pairs(step, cuts))
     pairs = [trade(a, 1) for a in pairs]
     owns = [trade(a, i + 2) for i, a in enumerate(owns)]
-    slabs = slabs[:1] + [trade(a, 1) for a in slabs[1:]]
+    pairs, waiting = lax.optimization_barrier((pairs, slabs[1:]))
+    slabs = slabs[:1] + [trade(a, 1) for a in waiting]
     paired = [(a.astype(F32) + b.astype(F32)).astype(BF16) for a, b in zip(local, pairs)]
-    borders = [trade(a, 2 * i + 2) for i, a in enumerate(paired)]
+    cuts_of = pair_chunks(rows, border)
+    borders = [trade(a[low:high], 2 * i + 2) for i, a in enumerate(paired) for low, high in cuts_of]
     prepared = pl.pallas_call(
         functools.partial(prepare_kernel, cuts, reps, subs),
         out_shape=[

time: 38.4 us -> 37.7 us (0.982)
  waiting for transfers between devices: 9.33 us -> 6.93 us
  blocking collectives: 12 us -> 13.2 us
  starting transfers between devices: 10.2 us -> 10.7 us
    ppermute x5 -> x6, waiting for transfers between devices: 9.33 us -> 6.93 us  [body(): trade = lambda a, step: lax.ppermute(a, 'cuts', partner_pairs(step, cuts))]
    all_to_all x1, blocking collectives: 12 us -> 13.2 us  [body(): lax.all_to_all(payload.reshape(peers, rows // peers, units + rows), ('cut...]
    ppermute x5 -> x6, starting transfers between devices: 10.2 us -> 10.7 us  [body(): trade = lambda a, step: lax.ppermute(a, 'cuts', partner_pairs(step, cuts))]
  transfers between devices with their start and end apart: 5 -> 6, of which waited for: 2 -> 3; matrix products, arithmetic and copies ran while one was open for 0% -> 0% of each run, Pallas kernels for 4% -> 4%
where the time goes in v6:
time: 37.7 us; the launch traced here: 37.5 us
  blocking collectives  13.2 us (35%)
  starting transfers between devices  10.7 us (28%)
  waiting for transfers between devices  6.93 us (18%)
  Pallas kernels  6.58 us (17%)
    all_to_all x1, blocking collectives, body(): lax.all_to_all(payload.reshape(peers, rows // peers, units + rows), ('cut...  13.2 us
    ppermute x6, starting transfers between devices, body(): trade = lambda a, step: lax.ppermute(a, 'cuts', partner_pairs(step, cuts))  10.7 us
    ppermute x6, waiting for transfers between devices, body(): trade = lambda a, step: lax.ppermute(a, 'cuts', partner_pairs(step, cuts))  6.93 us
    pallas_call x1, Pallas kernels, body(): pl.pallas_call(functools.partial(first_layer_kernel, cuts), out_shape=[bo...  3.74 us
    pallas_call x1, Pallas kernels, body(): pl.pallas_call(functools.partial(prepare_kernel, cuts, reps, subs), out_s...  1.36 us
    pallas_call x1, Pallas kernels, body(): pl.pallas_call(placing_kernel, out_shape=shape((rows, units), BF16), in_s...  0.87 us
  transfers between devices with their start and end apart: 6, of which 3 were waited for; matrix products, arithmetic and copies ran while one was open for 0% of the time, Pallas kernels for 4%

profile of v6, /device:TPU:0, one launch (start us, length us, event | category | flops | bytes accessed | tf_op | source)
XLA Modules:
  0.0 37.5 jit_solution(12696206194106886633)
XLA Ops:
  0.0 3.7 %first_layer.1 = (bf16[144,512]{1,0:T(8,128)(2,1)S(1)}, bf16[80,512]{1,0:T(8,128)(2,1)S(1)}, bf16[80,512]{1,0:T(8,128)(2,1)S(1)}, bf16[224,512]{1,0:T(8,128)(2,1...) custom-call(s32[3,1,4]{2,1,0:T(1,128)} %bitcast.14, s32[1,4]{1,0:T(1,128)} %rest_0_.1, ...), custom_call_target="tpu_custom_call" | custom-call | tf_op jit(solution)/shard_map/first_layer/pallas_call | solution.py:278
  3.7 3.1 %collective-permute-start = (bf16[144,512]{1,0:T(8,128)(2,1)S(1)}, bf16[144,512]{1,0:T(8,128)(2,1)S(1)}, u32[]{:S(2)}, u32[]{:S(2)}) collective-permute-start(bf16[144,512]{1,0:T(8,128)(2,1)S(1)} %get-tuple-element.21), channel_id=1, source_target_pairs={{0,4},{4,0},{8,12},{12,8},{1,5},{5,1},{9,13},{13,9},{2,6},{6,2},{1... | collective-permute-start | bytes 442376 | tf_op jit(solution)/shard_map/ppermute | solution.py:312
  6.8 2.6 %collective-permute-start.2 = (bf16[80,512]{1,0:T(8,128)(2,1)S(1)}, bf16[80,512]{1,0:T(8,128)(2,1)S(1)}, u32[]{:S(2)}, u32[]{:S(2)}) collective-permute-start(bf16[80,512]{1,0:T(8,128)(2,1)S(1)} %get-tuple-element.24), channel_id=1, source_target_pairs={{0,8},{4,12},{8,0},{12,4},{1,9},{5,13},{9,1},{13,5},{2,10},{6,14},... | collective-permute-start | bytes 245768 | tf_op jit(solution)/shard_map/ppermute | solution.py:312
  9.5 0.0 collective-permute-start.3
  9.5 2.3 %collective-permute-done = bf16[144,512]{1,0:T(8,128)(2,1)S(1)} collective-permute-done((bf16[144,512]{1,0:T(8,128)(2,1)S(1)}, bf16[144,512]{1,0:T(8,128)(2,1)S(1)}, u32[]{:S(2)}, u32[]{:S(2)}) %collective-permute-start) | collective-permute-done | bytes 147488 | tf_op jit(solution)/shard_map/ppermute | solution.py:312
  11.8 1.4 %collective-permute-start.1 = (bf16[224,512]{1,0:T(8,128)(2,1)S(1)}, bf16[224,512]{1,0:T(8,128)(2,1)S(1)}, u32[]{:S(2)}, u32[]{:S(2)}) collective-permute-start(bf16[224,512]{1,0:T(8,128)(2,1)S(1)} %get-tuple-element.23), channel_id=1, source_target_pairs={{0,4},{4,0},{8,12},{12,8},{1,5},{5,1},{9,13},{13,9},{2,6},{6,2},{1... | collective-permute-start | bytes 688136 | tf_op jit(solution)/shard_map/ppermute | solution.py:312
  13.3 3.5 %collective-permute-start.5 = (bf16[80,512]{1,0:T(8,128)(2,1)S(1)}, bf16[80,512]{1,0:T(8,128)(2,1)S(1)}, u32[]{:S(2)}, u32[]{:S(2)}) collective-permute-start(bf16[80,512]{1,0:T(8,128)(2,1)S(1)} %slice.9), channel_id=1, source_target_pairs={{0,8},{4,12},{8,0},{12,4},{1,9},{5,13},{9,1},{13,5},{2,10},{6,14},... | collective-permute-start | bytes 245768 | tf_op jit(solution)/shard_map/ppermute | solution.py:312
  16.8 0.1 collective-permute-start.4
  16.9 1.4 %prepare.1 = (bf16[1024,512]{1,0:T(8,128)(2,1)S(1)}, f32[1,512]{1,0:T(1,128)S(1)}, f32[1,512]{1,0:T(1,128)S(1)}, bf16[96,128]{1,0:T(8,128)(2,1)S(1)}, f32[128,12...) custom-call(bf16[144,512]{1,0:T(8,128)(2,1)S(1)} %get-tuple-element.26.after_ref, ...), custom_call_target="tpu_custom_call" | custom-call | flops 8388608 | bytes 1048576 | tf_op jit(solution)/shard_map/prepare/pallas_call | solution.py:320
  18.3 0.0 collective-permute-done.2.rest_2_
  18.3 0.0 collective-permute-done.3.rest_3_
  18.3 4.5 %collective-permute-done.4.rest_4_ = bf16[64,512]{1,0:T(8,128)(2,1)S(1)} collective-permute-done((bf16[64,512]{1,0:T(8,128)(2,1)S(1)}, bf16[64,512]{1,0:T(8,128)(2,1)S(1)}, u32[]{:S(2)}, u32[]{:S(2)}) %collective-permute-start.4) | collective-permute-done | bytes 65568 | tf_op jit(solution)/shard_map/ppermute | solution.py:312
  22.8 0.0 collective-permute-done.5.rest_5_
  22.8 0.1 collective-permute-done.1.rest_1_
  22.9 0.6 %second_layer.1 = bf16[128,640]{1,0:T(8,128)(2,1)S(1)} custom-call(bf16[224,512]{1,0:T(8,128)(2,1)S(1)} %get-tuple-element.20.rest_0_, bf16[224,512]{1,0:T(8,128)(2,1)S(1)} %collective-permute-done.1.rest_1_, bf16[80,512]{1,0:T(8,128)(2,1)S(1)} %collective-permute-done.2.rest_2_, bf16[80,512]{1,0:T(8,128)(2,1)S(1)} %collective-permute-done.3.rest_3_, ...), custom_call_target="tpu_custom_call" | custom-call | tf_op jit(solution)/shard_map/second_layer/pallas_call | solution.py:349
  23.5 13.2 %all_to_all.5 = bf16[8,16,640]{2,1,0:T(8,128)(2,1)S(1)} all-to-all(bf16[8,16,640]{2,1,0:T(8,128)(2,1)S(1)} %bitcast.7), channel_id=1, replica_groups=mesh['groups'=2,'cuts'=4,'rep'=2,'sub'=2] {'cuts','rep'}, dimensions={0} | all-to-all | bytes 327680 | tf_op jit(solution)/shard_map/all_to_all | solution.py:358
  36.6 0.9 %placing.1 = bf16[128,512]{1,0:T(8,128)(2,1)} custom-call(bf16[128,640]{1,0:T(8,128)(2,1)S(1)} %bitcast.8), custom_call_target="tpu_custom_call" | custom-call | tf_op jit(solution)/shard_map/placing/pallas_call | solution.py:361
  (3 shorter events, 0.0 us)
Async XLA Ops:
  3.7 8.1 %collective-permute-start = (bf16[144,512]{1,0:T(8,128)(2,1)S(1)}, bf16[144,512]{1,0:T(8,128)(2,1)S(1)}, u32[]{:S(2)}, u32[]{:S(2)}) collective-permute-start(bf16[144,512]{1,0:T(8,128)(2,1)S(1)} %get-tuple-element.21), channel_id=1, source_target_pairs={{0,4},{4,0},{8,12},{12,8},{1,5},{5,1},{9,13},{13,9},{2,6},{6,2},{1... | collective-permute-start | bytes 442376 | tf_op jit(solution)/shard_map/ppermute | solution.py:312
  6.8 11.4 %collective-permute-start.2 = (bf16[80,512]{1,0:T(8,128)(2,1)S(1)}, bf16[80,512]{1,0:T(8,128)(2,1)S(1)}, u32[]{:S(2)}, u32[]{:S(2)}) collective-permute-start(bf16[80,512]{1,0:T(8,128)(2,1)S(1)} %get-tuple-element.24), channel_id=1, source_target_pairs={{0,8},{4,12},{8,0},{12,4},{1,9},{5,13},{9,1},{13,5},{2,10},{6,14},... | collective-permute-start | bytes 245768 | tf_op jit(solution)/shard_map/ppermute | solution.py:312
  9.5 8.8 %collective-permute-start.3 = (bf16[80,512]{1,0:T(8,128)(2,1)S(1)}, bf16[80,512]{1,0:T(8,128)(2,1)S(1)}, u32[]{:S(2)}, u32[]{:S(2)}) collective-permute-start(bf16[80,512]{1,0:T(8,128)(2,1)S(1)} %get-tuple-element.25), channel_id=1, source_target_pairs={{0,12},{4,8},{8,4},{12,0},{1,13},{5,9},{9,5},{13,1},{2,14},{6,10},... | collective-permute-start | bytes 245768 | tf_op jit(solution)/shard_map/ppermute | solution.py:312
  11.8 11.1 %collective-permute-start.1 = (bf16[224,512]{1,0:T(8,128)(2,1)S(1)}, bf16[224,512]{1,0:T(8,128)(2,1)S(1)}, u32[]{:S(2)}, u32[]{:S(2)}) collective-permute-start(bf16[224,512]{1,0:T(8,128)(2,1)S(1)} %get-tuple-element.23), channel_id=1, source_target_pairs={{0,4},{4,0},{8,12},{12,8},{1,5},{5,1},{9,13},{13,9},{2,6},{6,2},{1... | collective-permute-start | bytes 688136 | tf_op jit(solution)/shard_map/ppermute | solution.py:312
  13.3 9.4 %collective-permute-start.5 = (bf16[80,512]{1,0:T(8,128)(2,1)S(1)}, bf16[80,512]{1,0:T(8,128)(2,1)S(1)}, u32[]{:S(2)}, u32[]{:S(2)}) collective-permute-start(bf16[80,512]{1,0:T(8,128)(2,1)S(1)} %slice.9), channel_id=1, source_target_pairs={{0,8},{4,12},{8,0},{12,4},{1,9},{5,13},{9,1},{13,5},{2,10},{6,14},... | collective-permute-start | bytes 245768 | tf_op jit(solution)/shard_map/ppermute | solution.py:312
  16.8 6.0 %collective-permute-start.4 = (bf16[64,512]{1,0:T(8,128)(2,1)S(1)}, bf16[64,512]{1,0:T(8,128)(2,1)S(1)}, u32[]{:S(2)}, u32[]{:S(2)}) collective-permute-start(bf16[64,512]{1,0:T(8,128)(2,1)S(1)} %slice.8), channel_id=1, source_target_pairs={{0,8},{4,12},{8,0},{12,4},{1,9},{5,13},{9,1},{13,5},{2,10},{6,14},... | collective-permute-start | bytes 196616 | tf_op jit(solution)/shard_map/ppermute | solution.py:312

commit v7 on v4

--- a/solution.py
+++ b/solution.py
@@ -11,6 +11,12 @@
 BF16 = jnp.bfloat16
 VMEM = pltpu.VMEM
 SMEM = pltpu.SMEM
+
+
+def pair_chunks(rows, border):
+    pieces = -(-rows // border)
+    ends = [rows * i // pieces // 16 * 16 for i in range(pieces)] + [rows]
+    return list(zip(ends[:-1], ends[1:]))
 
 
 def partner_pairs(step, total):
@@ -56,23 +62,27 @@
     return copies
 
 
-def part_of(ref, owner, size):
-    return ref[pl.ds(pl.multiple_of(owner * size, size), size), :]
+def fill_picks(pick_ref, brow_ref, owners_ref, first, rows):
+    _, neigh, _, cap = brow_ref.shape
+    total = pick_ref.shape[1]
+    lane = lax.broadcasted_iota(jnp.int32, (cap, total), 1)
+    eye = (
+        lax.broadcasted_iota(jnp.int32, (cap, cap), 0) == lax.broadcasted_iota(jnp.int32, (cap, cap), 1)
+    ).astype(F32)
+    for k in range(neigh):
+        columns = contract_last(eye, brow_ref[0, k].astype(F32)).astype(jnp.int32)
+        for u in range(pick_ref.shape[0] // (neigh * cap)):
+            target = columns[:, first + u : first + u + 1] + owners_ref[k, 0, first + u] * rows
+            at = u * neigh * cap + k * cap
+            pick_ref[at : at + cap, :] = (lane == target).astype(F32).astype(BF16)
 
 
 def first_layer_kernel(
     cuts, owners_hbm, count_hbm, bcount_hbm, x_hbm, wn_hbm, ws_hbm, deg_hbm, brow_hbm, ew_hbm, *rest
 ):
-    near, far = min(2, cuts), cuts - min(2, cuts)
-    border_refs, own_refs, slab_refs, local_refs = (
-        rest[: far // 2],
-        rest[far // 2 : far // 2 + far],
-        rest[far // 2 + far : far // 2 + far + near],
-        rest[far // 2 + far + near : 2 * far + near],
-    )
-    rest = rest[2 * far + near :]
-    owners_ref, count_ref, bcount_ref, brow_v, deg_v, x_v, wn_v, ws_v, ew_v, pick_v, adj_v, *rest = rest
-    scale_v, y_v, sums_v, border_v, sems = rest
+    far = cuts - min(2, cuts)
+    own_refs, sums_ref, pick_ref, rest = rest[:far], rest[far], rest[far + 1], rest[far + 2 :]
+    owners_ref, count_ref, bcount_ref, brow_v, deg_v, x_v, wn_v, ws_v, ew_v, adj_v, scale_v, y_v, sems = rest
     pairs = (
         (brow_hbm, brow_v),
         (owners_hbm, owners_ref),
@@ -86,32 +96,18 @@
     )
     brow_in, owners_in, *counts_in, deg_in, ew_in, x_in, wn_in, ws_in = start_all(pairs, sems)
     _, _, neigh, cap, rows = ew_v.shape
-    total = cuts * rows
     me = lax.axis_index("cuts")
-    lane = lax.broadcasted_iota(jnp.int32, (cap, total), 1)
-    eye = (
-        lax.broadcasted_iota(jnp.int32, (cap, cap), 0) == lax.broadcasted_iota(jnp.int32, (cap, cap), 1)
-    ).astype(F32)
     span = min(cuts, 4)
-
-    def fill_picks(first):
-        for k in range(neigh):
-            columns = contract_last(eye, brow_v[0, k].astype(F32)).astype(jnp.int32)
-            for u in range(span):
-                target = columns[:, first + u : first + u + 1] + owners_ref[k, 0, first + u] * rows
-                at = u * neigh * cap + k * cap
-                pick_v[at : at + cap, :] = (lane == target).astype(F32).astype(BF16)
-
     brow_in.wait()
     owners_in.wait()
     for first in range(0, cuts, span):
-        fill_picks(first)
+        fill_picks(pick_ref, brow_v, owners_ref, first, rows)
         if first == 0:
             for copy in (*counts_in, deg_in, ew_in):
                 copy.wait()
         for u in range(first, first + span):
             at = slice(u * rows, (u + 1) * rows)
-            picks = pick_v[(u - first) * neigh * cap : (u - first + 1) * neigh * cap, :]
+            picks = pick_ref[(u - first) * neigh * cap : (u - first + 1) * neigh * cap, :]
             adj_v[at, :] = contract_first(live_tile(ew_v[0, u], count_ref, bcount_ref, u), picks).astype(BF16)
             scale_v[at, :] = as_column(1.0 / deg_v[:, at].astype(F32))
     x_in.wait()
@@ -124,21 +120,37 @@
         at = slice(first * rows, (first + span) * rows)
         selfs = jnp.dot(x_v[at, :], ws_v[...], preferred_element_type=F32)
         summed = jnp.dot(adj_v[at, :], y_v[...], preferred_element_type=F32)
-        sums_v[at, :] = (selfs + summed * scale_v[at, :]).astype(BF16)
+        sums_ref[at, :] = (selfs + summed * scale_v[at, :]).astype(BF16)
+    for i, out_ref in enumerate(own_refs):
+        out_ref[...] = sums_ref[pl.ds(pl.multiple_of((me ^ (i + 2)) * rows, rows), rows), :]
+
+
+def border_kernel(cuts, rows, cap, sums_ref, pick_ref, *rest):
+    near, far = min(2, cuts), cuts - min(2, cuts)
+    span = min(cuts, 4)
+    border = pick_ref.shape[0] // span
+    if span < cuts:
+        brow_hbm, owners_hbm, *rest = rest
+        brow_v, owners_v, pick_v, sems = rest[-4:]
+        for copy in start_all(((brow_hbm, brow_v), (owners_hbm, owners_v)), sems):
+            copy.wait()
+    far_refs, slab_refs, border_v = rest[:far], rest[far : far + near], rest[far + near]
+    me = lax.axis_index("cuts")
     for first in range(0, cuts, span):
         if span < cuts:
-            fill_picks(first)
-        at = slice(first * neigh * cap, (first + span) * neigh * cap)
-        border_v[at, :] = jnp.dot(pick_v[...], sums_v[...], preferred_element_type=F32).astype(BF16)
-    for i, out_ref in enumerate(border_refs):
-        out_ref[...] = part_of(border_v, me ^ (2 * i + 3), neigh * cap)
-    for i, out_ref in enumerate(own_refs):
-        out_ref[...] = part_of(sums_v, me ^ (i + 2), rows)
+            fill_picks(pick_v, brow_v, owners_v, first, rows)
+        picks = pick_ref if span == cuts else pick_v
+        at = slice(first * border, (first + span) * border)
+        border_v[at, :] = jnp.dot(picks[...], sums_ref[...], preferred_element_type=F32).astype(BF16)
+
+    def border_of(owner):
+        return border_v[pl.ds(pl.multiple_of(owner * border, border), border), :]
+
+    for i, out_ref in enumerate(far_refs):
+        out_ref[...] = border_of(me ^ (i + 2))
     for step, out_ref in enumerate(slab_refs):
-        out_ref[:rows, :] = part_of(sums_v, me ^ step, rows)
-        out_ref[rows:, :] = part_of(border_v, me ^ step, neigh * cap)
-    for i, out_ref in enumerate(local_refs):
-        out_ref[...] = part_of(border_v, me ^ (2 * i + 2), neigh * cap)
+        out_ref[:rows, :] = sums_ref[pl.ds(pl.multiple_of((me ^ step) * rows, rows), rows), :]
+        out_ref[rows:, :] = border_of(me ^ step)
 
 
 def hidden_rows(parts, b1_ref):
@@ -192,12 +204,17 @@
 
 def second_layer_kernel(cuts, *rest):
     near, far = min(2, cuts), cuts - min(2, cuts)
-    slab_refs, own_refs, border_refs = rest[:near], rest[near : near + far], rest[near + far : near + far + far // 2]
-    w_ref, b1_ref, b2_ref, live_ref, scale_ref, chosen_ref, slots_ref, out_ref = rest[near + far + far // 2 :]
+    slab_refs, border_refs, own_refs = rest[:near], rest[near : near + far], rest[near + far : -8]
+    w_ref, b1_ref, b2_ref, live_ref, scale_ref, chosen_ref, slots_ref, out_ref = rest[-8:]
     rows = chosen_ref.shape[0]
     units = w_ref.shape[1]
-    own = hidden_rows([slab[:rows, :] for slab in slab_refs] + [part[...] for part in own_refs], b1_ref)
+    chunks = pair_chunks(rows, live_ref.shape[0])
     border = hidden_rows([slab[rows:, :] for slab in slab_refs] + [part[...] for part in border_refs], b1_ref)
+    pieces = []
+    for i, (low, high) in enumerate(chunks):
+        parts = [slab[low:high, :] for slab in slab_refs] + [part[...] for part in own_refs[i :: len(chunks)]]
+        pieces.append(hidden_rows(parts, b1_ref))
+    own = jnp.concatenate(pieces, axis=0)
     summed = contract_first(live_ref[...], border)
     mean = (summed * scale_ref[:, :1]).astype(BF16)
     z = jnp.dot(jnp.concatenate([own, mean], axis=1), w_ref[...], preferred_element_type=F32) + b2_ref[...]
@@ -245,16 +262,14 @@
     bcounts = boundary_count.transpose(2, 0, 1)
     brows = boundary_rows.transpose(0, 2, 1, 3)
     counts_held = [SMEM(a.shape, jnp.int32) for a in (owners, neighbor_count, bcounts)]
+    span = min(cuts, 4)
     held = total * width + 2 * width * units + total * total + 2 * total * units + 256 * total
-    held += min(cuts, 4) * border * total + cuts * border * (units + rows) + units * (near * (rows + border) + far * (rows + border))
-    sent = pl.pallas_call(
+    held += span * border * total + cuts * border * rows + far * rows * units
+    *owns, sums, pick = pl.pallas_call(
         functools.partial(first_layer_kernel, cuts),
-        out_shape=[border_slab] * (far // 2)
-        + [own_slab] * far
-        + [slab] * near
-        + [border_slab] * (far // 2),
+        out_shape=[own_slab] * far + [shape((total, units), BF16), shape((span * border, total), BF16)],
         in_specs=[hbm] * 9,
-        out_specs=[vmem] * (2 * far + near),
+        out_specs=[vmem] * (far + 2),
         scratch_shapes=[
             *counts_held,
             pltpu.VMEM(brows.shape, jnp.int32),
@@ -263,30 +278,41 @@
             pltpu.VMEM((width, units), BF16),
             pltpu.VMEM((width, units), BF16),
             pltpu.VMEM(edge_weight.shape, BF16),
-            pltpu.VMEM((min(cuts, 4) * border, total), BF16),
             pltpu.VMEM((total, total), BF16),
             pltpu.VMEM((total, 1), F32),
             pltpu.VMEM((total, units), BF16),
-            pltpu.VMEM((total, units), BF16),
-            pltpu.VMEM((cuts * border, units), BF16),
             pltpu.SemaphoreType.DMA((9,)),
         ],
         compiler_params=pltpu.CompilerParams(vmem_limit_bytes=2 * held + (8 << 20)),
         name="first_layer",
     )(*in_hbm(owners, neighbor_count, bcounts, features, w_neigh1, w_self1, degree, brows, edge_weight))
-    sent = list(sent)
-    pairs, owns, slabs, local = (
-        sent[: far // 2],
-        sent[far // 2 : far // 2 + far],
-        sent[far // 2 + far : far // 2 + far + near],
-        sent[far // 2 + far + near :],
-    )
+    rebuilt = span < cuts
+    held = total * units + 2 * span * border * total + cuts * border * units + units * cuts * (rows + border)
+    *borders, first_slab, second_slab = pl.pallas_call(
+        functools.partial(border_kernel, cuts, rows, cap),
+        out_shape=[border_slab] * far + [slab] * near,
+        in_specs=[vmem] * 2 + [hbm] * (2 * rebuilt),
+        out_specs=[vmem] * cuts,
+        scratch_shapes=[pltpu.VMEM((cuts * border, units), BF16)]
+        + [
+            pltpu.VMEM(brows.shape, jnp.int32),
+            counts_held[0],
+            pltpu.VMEM((span * border, total), BF16),
+            pltpu.SemaphoreType.DMA((2,)),
+        ]
+        * rebuilt,
+        compiler_params=pltpu.CompilerParams(vmem_limit_bytes=2 * held + (8 << 20)),
+        cost_estimate=pl.CostEstimate(flops=2 * cuts * border * total * units, bytes_accessed=0, transcendentals=0),
+        name="border",
+    )(sums, pick, *in_hbm(*(brows, owners)[: 2 * rebuilt]))
     trade = lambda a, step: lax.ppermute(a, "cuts", partner_pairs(step, cuts))
-    pairs = [trade(a, 1) for a in pairs]
-    owns = [trade(a, i + 2) for i, a in enumerate(owns)]
-    slabs = slabs[:1] + [trade(a, 1) for a in slabs[1:]]
-    paired = [(a.astype(F32) + b.astype(F32)).astype(BF16) for a, b in zip(local, pairs)]
-    borders = [trade(a, 2 * i + 2) for i, a in enumerate(paired)]
+    pairs = [trade(a, 1) for a in owns[1::2]]
+    pairs, waiting, odd = lax.optimization_barrier((pairs, second_slab, borders[1::2]))
+    borders = [trade(odd[i // 2] if i % 2 else a, i + 2) for i, a in enumerate(borders)]
+    slabs = [first_slab, trade(waiting, 1)]
+    paired = [(a.astype(F32) + b.astype(F32)).astype(BF16) for a, b in zip(owns[::2], pairs)]
+    chunks = pair_chunks(rows, border)
+    owns = [trade(a[low:high], 2 * i + 2) for i, a in enumerate(paired) for low, high in chunks]
     prepared = pl.pallas_call(
         functools.partial(prepare_kernel, cuts, reps, subs),
         out_shape=[
@@ -311,11 +337,11 @@
         cost_estimate=pl.CostEstimate(flops=rows * rows * units, bytes_accessed=4 * units * units, transcendentals=0),
         name="prepare",
     )(
-        sent[-1],
+        sums,
         *in_hbm(neighbor_count, bcounts, w_self2, w_neigh2, bias1.reshape(1, units), bias2.reshape(1, units)),
         *in_hbm(degree, edge_weight, node_id),
     )
-    arrived = slabs + owns + borders
+    arrived = slabs + borders + owns
     payload = pl.pallas_call(
         functools.partial(second_layer_kernel, cuts),
         out_shape=shape((rows, units + rows), BF16),
@@ -334,7 +360,7 @@
         in_specs=[vmem],
         out_specs=vmem,
         name="placing",
-    )(moved.reshape(rows, units + rows))
+    )(pltpu.with_memory_space_constraint(moved.reshape(rows, units + rows), pltpu.VMEM))
 
 
 def solution(mesh):

time: 40.1 us -> 37.4 us (0.933)
  waiting for transfers between devices: 10 us -> 5.73 us
  starting transfers between devices: 10.2 us -> 13.8 us
  blocking collectives: 12.2 us -> 10.9 us
  Pallas kernels: 7.49 us -> 6.66 us
    ppermute x5 -> x6, waiting for transfers between devices: 10 us -> 5.73 us  [body(): trade = lambda a, step: lax.ppermute(a, 'cuts', partner_pairs(step, cuts))]
    ppermute x5 -> x6, starting transfers between devices: 10.2 us -> 13.8 us  [body(): trade = lambda a, step: lax.ppermute(a, 'cuts', partner_pairs(step, cuts))]
    all_to_all x1, blocking collectives: 12.2 us -> 10.9 us  [body(): lax.all_to_all(payload.reshape(peers, rows // peers, units + rows), ('cut...]
    pallas_call x1, Pallas kernels: 1.79 us -> 0.87 us  [body(): pl.pallas_call(placing_kernel, out_shape=shape((rows, units), BF16), in_s...]
    pallas_call x1 -> x2, Pallas kernels: 3.74 us -> 3.8 us  [the longest x1 3.41 us: body(): pl.pallas_call(functools.partial(first_layer_kernel, cuts), out_shape=[ow...]
  transfers between devices with their start and end apart: 5 -> 6, of which waited for: 2 -> 4; matrix products, arithmetic and copies ran while one was open for 0% -> 0% of each run, Pallas kernels for 3% -> 5%
where the time goes in v7:
time: 37.4 us; the launch traced here: 37.2 us
  starting transfers between devices  13.8 us (37%)
  blocking collectives  10.9 us (29%)
  Pallas kernels  6.66 us (18%)
  waiting for transfers between devices  5.73 us (15%)
    ppermute x6, starting transfers between devices, body(): trade = lambda a, step: lax.ppermute(a, 'cuts', partner_pairs(step, cuts))  13.8 us
    all_to_all x1, blocking collectives, body(): lax.all_to_all(payload.reshape(peers, rows // peers, units + rows), ('cut...  10.9 us
    ppermute x6, waiting for transfers between devices, body(): trade = lambda a, step: lax.ppermute(a, 'cuts', partner_pairs(step, cuts))  5.73 us
    pallas_call x1, Pallas kernels, body(): pl.pallas_call(functools.partial(first_layer_kernel, cuts), out_shape=[ow...  3.41 us
    pallas_call x1, Pallas kernels, body(): pl.pallas_call(functools.partial(prepare_kernel, cuts, reps, subs), out_s...  1.36 us
    pallas_call x1, Pallas kernels, body(): pl.pallas_call(placing_kernel, out_shape=shape((rows, units), BF16), in_s...  0.87 us
  transfers between devices with their start and end apart: 6, of which 4 were waited for; matrix products, arithmetic and copies ran while one was open for 0% of the time, Pallas kernels for 5%

profile of v7, /device:TPU:0, one launch (start us, length us, event | category | flops | bytes accessed | tf_op | source)
XLA Modules:
  0.0 37.2 jit_solution(7333589152347500627)
XLA Ops:
  0.0 3.4 %first_layer.1 = (bf16[128,512]{1,0:T(8,128)(2,1)S(1)}, bf16[128,512]{1,0:T(8,128)(2,1)S(1)}, bf16[512,512]{1,0:T(8,128)(2,1)S(1)}, bf16[384,512]{1,0:T(8,128)(2,1)S(1)}) custom-call(s32[3,1,4]{2,1,0:T(1,128)} %bitcast.14, s32[1,4]{1,0:T(1,128)} %rest_0_.1, s32[3,1,4]{2,1,0:T(1,128)} %bitcast.9, bf16[512,1024]{1,0:T(8,128)(2,1)} %x_hbm.1, ...), custom_call_target="tpu_custom_call" | custom-call | tf_op jit(solution)/shard_map/first_layer/pallas_call | solution.py:268
  3.4 3.1 %collective-permute-start = (bf16[128,512]{1,0:T(8,128)(2,1)S(1)}, bf16[128,512]{1,0:T(8,128)(2,1)S(1)}, u32[]{:S(2)}, u32[]{:S(2)}) collective-permute-start(bf16[128,512]{1,0:T(8,128)(2,1)S(1)} %get-tuple-element.26), channel_id=1, source_target_pairs={{0,4},{4,0},{8,12},{12,8},{1,5},{5,1},{9,13},{13,9},{2,6},{6,2},{1... | collective-permute-start | bytes 393224 | tf_op jit(solution)/shard_map/ppermute | solution.py:308
  6.5 0.4 %border.1 = (bf16[96,512]{1,0:T(8,128)(2,1)S(1)}, bf16[96,512]{1,0:T(8,128)(2,1)S(1)}, bf16[224,512]{1,0:T(8,128)(2,1)S(1)}, bf16[224,512]{1,0:T(8,128)(2,1)S(1)}) custom-call(bf16[512,512]{1,0:T(8,128)(2,1)S(1)} %get-tuple-element.23.sums_ref.after_ref, bf16[384,512]{1,0:T(8,128)(2,1)S(1)} %get-tuple-element.24.pick_ref), custom_call_target="tpu_custom_call" | custom-call | flops 201326592 | tf_op jit(solution)/shard_map/border/pallas_call | solution.py:291
  6.9 2.6 %collective-permute-start.2 = (bf16[96,512]{1,0:T(8,128)(2,1)S(1)}, bf16[96,512]{1,0:T(8,128)(2,1)S(1)}, u32[]{:S(2)}, u32[]{:S(2)}) collective-permute-start(bf16[96,512]{1,0:T(8,128)(2,1)S(1)} %get-tuple-element.30), channel_id=1, source_target_pairs={{0,8},{4,12},{8,0},{12,4},{1,9},{5,13},{9,1},{13,5},{2,10},{6,14},... | collective-permute-start | bytes 294920 | tf_op jit(solution)/shard_map/ppermute | solution.py:308
  9.6 0.4 %collective-permute-done = bf16[128,512]{1,0:T(8,128)(2,1)S(1)} collective-permute-done((bf16[128,512]{1,0:T(8,128)(2,1)S(1)}, bf16[128,512]{1,0:T(8,128)(2,1)S(1)}, u32[]{:S(2)}, u32[]{:S(2)}) %collective-permute-start) | collective-permute-done | bytes 131104 | tf_op jit(solution)/shard_map/ppermute | solution.py:308
  10.0 5.1 %collective-permute-start.3 = (bf16[96,512]{1,0:T(8,128)(2,1)S(1)}, bf16[96,512]{1,0:T(8,128)(2,1)S(1)}, u32[]{:S(2)}, u32[]{:S(2)}) collective-permute-start(bf16[96,512]{1,0:T(8,128)(2,1)S(1)} %get-tuple-element.31), channel_id=1, source_target_pairs={{0,12},{4,8},{8,4},{12,0},{1,13},{5,9},{9,5},{13,1},{2,14},{6,10},... | collective-permute-start | bytes 294920 | tf_op jit(solution)/shard_map/ppermute | solution.py:308
  15.1 0.0 collective-permute-start.1
  15.1 0.6 %collective-permute-start.5 = (bf16[64,512]{1,0:T(8,128)(2,1)S(1)}, bf16[64,512]{1,0:T(8,128)(2,1)S(1)}, u32[]{:S(2)}, u32[]{:S(2)}) collective-permute-start(bf16[64,512]{1,0:T(8,128)(2,1)S(1)} %get-tuple-element.41), channel_id=1, source_target_pairs={{0,8},{4,12},{8,0},{12,4},{1,9},{5,13},{9,1},{13,5},{2,10},{6,14},... | collective-permute-start | bytes 196616 | tf_op jit(solution)/shard_map/ppermute | solution.py:308
  15.8 2.4 %collective-permute-start.4 = (bf16[64,512]{1,0:T(8,128)(2,1)S(1)}, bf16[64,512]{1,0:T(8,128)(2,1)S(1)}, u32[]{:S(2)}, u32[]{:S(2)}) collective-permute-start(bf16[64,512]{1,0:T(8,128)(2,1)S(1)} %get-tuple-element.42), channel_id=1, source_target_pairs={{0,8},{4,12},{8,0},{12,4},{1,9},{5,13},{9,1},{13,5},{2,10},{6,14},... | collective-permute-start | bytes 196616 | tf_op jit(solution)/shard_map/ppermute | solution.py:308
  18.1 1.4 %prepare.1 = (bf16[1024,512]{1,0:T(8,128)(2,1)S(1)}, f32[1,512]{1,0:T(1,128)S(1)}, f32[1,512]{1,0:T(1,128)S(1)}, bf16[96,128]{1,0:T(8,128)(2,1)S(1)}, f32[128,12...) custom-call(bf16[512,512]{1,0:T(8,128)(2,1)S(1)} %get-tuple-element.23.sums_ref.after_ref, ...), custom_call_target="tpu_custom_call" | custom-call | flops 8388608 | bytes 1048576 | tf_op jit(solution)/shard_map/prepare/pallas_call | solution.py:316
  19.5 0.0 collective-permute-done.2.rest_2_
  19.5 3.4 %collective-permute-done.5.rest_5_ = bf16[64,512]{1,0:T(8,128)(2,1)S(1)} collective-permute-done((bf16[64,512]{1,0:T(8,128)(2,1)S(1)}, bf16[64,512]{1,0:T(8,128)(2,1)S(1)}, u32[]{:S(2)}, u32[]{:S(2)}) %collective-permute-start.5) | collective-permute-done | bytes 65568 | tf_op jit(solution)/shard_map/ppermute | solution.py:308
  23.0 0.7 %collective-permute-done.4.rest_4_ = bf16[64,512]{1,0:T(8,128)(2,1)S(1)} collective-permute-done((bf16[64,512]{1,0:T(8,128)(2,1)S(1)}, bf16[64,512]{1,0:T(8,128)(2,1)S(1)}, u32[]{:S(2)}, u32[]{:S(2)}) %collective-permute-start.4) | collective-permute-done | bytes 65568 | tf_op jit(solution)/shard_map/ppermute | solution.py:308
  23.7 0.0 collective-permute-done.3.rest_3_
  23.7 1.1 %collective-permute-done.1.rest_1_ = bf16[224,512]{1,0:T(8,128)(2,1)S(1)} collective-permute-done((bf16[224,512]{1,0:T(8,128)(2,1)S(1)}, bf16[224,512]{1,0:T(8,128)(2,1)S(1)}, u32[]{:S(2)}, u32[]{:S(2)}) %collective-permute-start.1) | collective-permute-done | bytes 229408 | tf_op jit(solution)/shard_map/ppermute | solution.py:308
  24.8 0.6 %second_layer.1 = bf16[128,640]{1,0:T(8,128)(2,1)S(1)} custom-call(bf16[224,512]{1,0:T(8,128)(2,1)S(1)} %get-tuple-element.25.rest_0_, bf16[224,512]{1,0:T(8,128)(2,1)S(1)} %collective-permute-done.1.rest_1_, bf16[96,512]{1,0:T(8,128)(2,1)S(1)} %collective-permute-done.2.rest_2_, bf16[96,512]{1,0:T(8,128)(2,1)S(1)} %collective-permute-done.3.rest_3_, ...), custom_call_target="tpu_custom_call" | custom-call | tf_op jit(solution)/shard_map/second_layer/pallas_call | solution.py:345
  25.4 10.9 %all_to_all.5 = bf16[8,16,640]{2,1,0:T(8,128)(2,1)S(1)} all-to-all(bf16[8,16,640]{2,1,0:T(8,128)(2,1)S(1)} %bitcast.7), channel_id=1, replica_groups=mesh['groups'=2,'cuts'=4,'rep'=2,'sub'=2] {'cuts','rep'}, dimensions={0} | all-to-all | bytes 327680 | tf_op jit(solution)/shard_map/all_to_all | solution.py:354
  36.4 0.9 %placing.1 = bf16[128,512]{1,0:T(8,128)(2,1)} custom-call(bf16[128,640]{1,0:T(8,128)(2,1)S(1)} %bitcast.8), custom_call_target="tpu_custom_call" | custom-call | tf_op jit(solution)/shard_map/placing/pallas_call | solution.py:357
  (2 shorter events, 0.0 us)
Async XLA Ops:
  3.4 6.6 %collective-permute-start = (bf16[128,512]{1,0:T(8,128)(2,1)S(1)}, bf16[128,512]{1,0:T(8,128)(2,1)S(1)}, u32[]{:S(2)}, u32[]{:S(2)}) collective-permute-start(bf16[128,512]{1,0:T(8,128)(2,1)S(1)} %get-tuple-element.26), channel_id=1, source_target_pairs={{0,4},{4,0},{8,12},{12,8},{1,5},{5,1},{9,13},{13,9},{2,6},{6,2},{1... | collective-permute-start | bytes 393224 | tf_op jit(solution)/shard_map/ppermute | solution.py:308
  6.9 12.6 %collective-permute-start.2 = (bf16[96,512]{1,0:T(8,128)(2,1)S(1)}, bf16[96,512]{1,0:T(8,128)(2,1)S(1)}, u32[]{:S(2)}, u32[]{:S(2)}) collective-permute-start(bf16[96,512]{1,0:T(8,128)(2,1)S(1)} %get-tuple-element.30), channel_id=1, source_target_pairs={{0,8},{4,12},{8,0},{12,4},{1,9},{5,13},{9,1},{13,5},{2,10},{6,14},... | collective-permute-start | bytes 294920 | tf_op jit(solution)/shard_map/ppermute | solution.py:308
  10.0 13.7 %collective-permute-start.3 = (bf16[96,512]{1,0:T(8,128)(2,1)S(1)}, bf16[96,512]{1,0:T(8,128)(2,1)S(1)}, u32[]{:S(2)}, u32[]{:S(2)}) collective-permute-start(bf16[96,512]{1,0:T(8,128)(2,1)S(1)} %get-tuple-element.31), channel_id=1, source_target_pairs={{0,12},{4,8},{8,4},{12,0},{1,13},{5,9},{9,5},{13,1},{2,14},{6,10},... | collective-permute-start | bytes 294920 | tf_op jit(solution)/shard_map/ppermute | solution.py:308
  15.1 9.7 %collective-permute-start.1 = (bf16[224,512]{1,0:T(8,128)(2,1)S(1)}, bf16[224,512]{1,0:T(8,128)(2,1)S(1)}, u32[]{:S(2)}, u32[]{:S(2)}) collective-permute-start(bf16[224,512]{1,0:T(8,128)(2,1)S(1)} %get-tuple-element.29), channel_id=1, source_target_pairs={{0,4},{4,0},{8,12},{12,8},{1,5},{5,1},{9,13},{13,9},{2,6},{6,2},{1... | collective-permute-start | bytes 688136 | tf_op jit(solution)/shard_map/ppermute | solution.py:308
  15.1 7.8 %collective-permute-start.5 = (bf16[64,512]{1,0:T(8,128)(2,1)S(1)}, bf16[64,512]{1,0:T(8,128)(2,1)S(1)}, u32[]{:S(2)}, u32[]{:S(2)}) collective-permute-start(bf16[64,512]{1,0:T(8,128)(2,1)S(1)} %get-tuple-element.41), channel_id=1, source_target_pairs={{0,8},{4,12},{8,0},{12,4},{1,9},{5,13},{9,1},{13,5},{2,10},{6,14},... | collective-permute-start | bytes 196616 | tf_op jit(solution)/shard_map/ppermute | solution.py:308
  15.8 7.9 %collective-permute-start.4 = (bf16[64,512]{1,0:T(8,128)(2,1)S(1)}, bf16[64,512]{1,0:T(8,128)(2,1)S(1)}, u32[]{:S(2)}, u32[]{:S(2)}) collective-permute-start(bf16[64,512]{1,0:T(8,128)(2,1)S(1)} %get-tuple-element.42), channel_id=1, source_target_pairs={{0,8},{4,12},{8,0},{12,4},{1,9},{5,13},{9,1},{13,5},{2,10},{6,14},... | collective-permute-start | bytes 196616 | tf_op jit(solution)/shard_map/ppermute | solution.py:308

commit v8 on v6

--- a/solution.py
+++ b/solution.py
@@ -11,7 +11,8 @@
 BF16 = jnp.bfloat16
 VMEM = pltpu.VMEM
 SMEM = pltpu.SMEM
-DIRECT = 80
+DIRECT = 64
+WEIGHT = 20_000_000_000
 
 
 def direct_rows(rows):
@@ -21,7 +22,7 @@
 def pair_chunks(rows, border):
     direct = direct_rows(rows)
     units = (rows - direct + border) // 16
-    pieces = -(-units * 16 // direct)
+    pieces = 1
     ends = [16 * (units * i // pieces) for i in range(pieces + 1)]
     return list(zip(ends[:-1], ends[1:]))
 
@@ -338,10 +339,10 @@
             pltpu.SemaphoreType.DMA((9,)),
         ],
         compiler_params=pltpu.CompilerParams(vmem_limit_bytes=24 << 20),
-        cost_estimate=pl.CostEstimate(flops=rows * rows * units, bytes_accessed=4 * units * units, transcendentals=0),
+        cost_estimate=pl.CostEstimate(flops=WEIGHT, bytes_accessed=4 * units * units, transcendentals=0),
         name="prepare",
     )(
-        sent[-1],
+        owns[0] if far else sent[-1],
         *in_hbm(neighbor_count, bcounts, w_self2, w_neigh2, bias1.reshape(1, units), bias2.reshape(1, units)),
         *in_hbm(degree, edge_weight, node_id),
     )

time: 37.7 us -> 37.4 us (level)
  blocking collectives: 13.2 us -> 11.1 us
  starting transfers between devices: 10.7 us -> 11.8 us
  waiting for transfers between devices: 6.93 us -> 7.6 us
    all_to_all x1, blocking collectives: 13.2 us -> 11.1 us  [body(): lax.all_to_all(payload.reshape(peers, rows // peers, units + rows), ('cut...]
    ppermute x6 -> x5, starting transfers between devices: 10.7 us -> 11.8 us  [body(): trade = lambda a, step: lax.ppermute(a, 'cuts', partner_pairs(step, cuts))]
    ppermute x6 -> x5, waiting for transfers between devices: 6.93 us -> 7.6 us  [body(): trade = lambda a, step: lax.ppermute(a, 'cuts', partner_pairs(step, cuts))]
  transfers between devices with their start and end apart: 6 -> 5, of which waited for: 3 -> 3; matrix products, arithmetic and copies ran while one was open for 0% -> 0% of each run, Pallas kernels for 4% -> 4%
where the time goes in v8:
time: 37.4 us; the launch traced here: 37.2 us
  starting transfers between devices  11.8 us (32%)
  blocking collectives  11.1 us (30%)
  waiting for transfers between devices  7.6 us (20%)
  Pallas kernels  6.58 us (18%)
    ppermute x5, starting transfers between devices, body(): trade = lambda a, step: lax.ppermute(a, 'cuts', partner_pairs(step, cuts))  11.8 us
    all_to_all x1, blocking collectives, body(): lax.all_to_all(payload.reshape(peers, rows // peers, units + rows), ('cut...  11.1 us
    ppermute x5, waiting for transfers between devices, body(): trade = lambda a, step: lax.ppermute(a, 'cuts', partner_pairs(step, cuts))  7.6 us
    pallas_call x1, Pallas kernels, body(): pl.pallas_call(functools.partial(first_layer_kernel, cuts), out_shape=[bo...  3.74 us
    pallas_call x1, Pallas kernels, body(): pl.pallas_call(functools.partial(prepare_kernel, cuts, reps, subs), out_s...  1.36 us
    pallas_call x1, Pallas kernels, body(): pl.pallas_call(placing_kernel, out_shape=shape((rows, units), BF16), in_s...  0.87 us
  transfers between devices with their start and end apart: 5, of which 3 were waited for; matrix products, arithmetic and copies ran while one was open for 0% of the time, Pallas kernels for 4%

profile of v8, /device:TPU:0, one launch (start us, length us, event | category | flops | bytes accessed | tf_op | source)
XLA Modules:
  0.0 37.2 jit_solution(11368328189257062553)
XLA Ops:
  0.0 3.7 %first_layer.1 = (bf16[160,512]{1,0:T(8,128)(2,1)S(1)}, bf16[64,512]{1,0:T(8,128)(2,1)S(1)}, bf16[64,512]{1,0:T(8,128)(2,1)S(1)}, bf16[224,512]{1,0:T(8,128)(2,1...) custom-call(s32[3,1,4]{2,1,0:T(1,128)} %bitcast.10, s32[1,4]{1,0:T(1,128)} %rest_0_.1, ...), custom_call_target="tpu_custom_call" | custom-call | tf_op jit(solution)/shard_map/first_layer/pallas_call | solution.py:279
  3.7 3.1 %collective-permute-start = (bf16[160,512]{1,0:T(8,128)(2,1)S(1)}, bf16[160,512]{1,0:T(8,128)(2,1)S(1)}, u32[]{:S(2)}, u32[]{:S(2)}) collective-permute-start(bf16[160,512]{1,0:T(8,128)(2,1)S(1)} %get-tuple-element.21), channel_id=1, source_target_pairs={{0,4},{4,0},{8,12},{12,8},{1,5},{5,1},{9,13},{13,9},{2,6},{6,2},{1... | collective-permute-start | bytes 491528 | tf_op jit(solution)/shard_map/ppermute | solution.py:313
  6.8 2.6 %collective-permute-start.2 = (bf16[64,512]{1,0:T(8,128)(2,1)S(1)}, bf16[64,512]{1,0:T(8,128)(2,1)S(1)}, u32[]{:S(2)}, u32[]{:S(2)}) collective-permute-start(bf16[64,512]{1,0:T(8,128)(2,1)S(1)} %get-tuple-element.24), channel_id=1, source_target_pairs={{0,8},{4,12},{8,0},{12,4},{1,9},{5,13},{9,1},{13,5},{2,10},{6,14},... | collective-permute-start | bytes 196616 | tf_op jit(solution)/shard_map/ppermute | solution.py:313
  9.5 0.0 collective-permute-start.3
  9.5 2.7 %collective-permute-done = bf16[160,512]{1,0:T(8,128)(2,1)S(1)} collective-permute-done((bf16[160,512]{1,0:T(8,128)(2,1)S(1)}, bf16[160,512]{1,0:T(8,128)(2,1)S(1)}, u32[]{:S(2)}, u32[]{:S(2)}) %collective-permute-start) | collective-permute-done | bytes 163872 | tf_op jit(solution)/shard_map/ppermute | solution.py:313
  12.2 3.0 %collective-permute-start.4 = (bf16[160,512]{1,0:T(8,128)(2,1)S(1)}, bf16[160,512]{1,0:T(8,128)(2,1)S(1)}, u32[]{:S(2)}, u32[]{:S(2)}) collective-permute-start(bf16[160,512]{1,0:T(8,128)(2,1)S(1)} %add_convert_fusion), channel_id=1, source_target_pairs={{0,8},{4,12},{8,0},{12,4},{1,9},{5,13},{9,1},{13,5},{2,10},{6,14},... | collective-permute-start | bytes 491528 | tf_op jit(solution)/shard_map/ppermute | solution.py:313
  15.2 3.2 %collective-permute-start.1 = (bf16[224,512]{1,0:T(8,128)(2,1)S(1)}, bf16[224,512]{1,0:T(8,128)(2,1)S(1)}, u32[]{:S(2)}, u32[]{:S(2)}) collective-permute-start(bf16[224,512]{1,0:T(8,128)(2,1)S(1)} %get-tuple-element.23), channel_id=1, source_target_pairs={{0,4},{4,0},{8,12},{12,8},{1,5},{5,1},{9,13},{13,9},{2,6},{6,2},{1... | collective-permute-start | bytes 688136 | tf_op jit(solution)/shard_map/ppermute | solution.py:313
  18.3 0.0 collective-permute-done.2.after_ref.rest_2_
  18.3 1.4 %prepare.1 = (bf16[1024,512]{1,0:T(8,128)(2,1)S(1)}, f32[1,512]{1,0:T(1,128)S(1)}, f32[1,512]{1,0:T(1,128)S(1)}, bf16[96,128]{1,0:T(8,128)(2,1)S(1)}, f32[128,12...) custom-call(bf16[64,512]{1,0:T(8,128)(2,1)S(1)} %collective-permute-done.2.after_ref.rest_2_, ...), custom_call_target="tpu_custom_call" | custom-call | flops 20000000000 | bytes 1048576 | tf_op jit(solution)/shard_map/prepare/pallas_call | solution.py:321
  19.7 0.0 collective-permute-done.3.rest_3_
  19.7 3.6 %collective-permute-done.4.rest_4_ = bf16[160,512]{1,0:T(8,128)(2,1)S(1)} collective-permute-done((bf16[160,512]{1,0:T(8,128)(2,1)S(1)}, bf16[160,512]{1,0:T(8,128)(2,1)S(1)}, u32[]{:S(2)}, u32[]{:S(2)}) %collective-permute-start.4) | collective-permute-done | bytes 163872 | tf_op jit(solution)/shard_map/ppermute | solution.py:313
  23.3 1.3 %collective-permute-done.1.rest_1_ = bf16[224,512]{1,0:T(8,128)(2,1)S(1)} collective-permute-done((bf16[224,512]{1,0:T(8,128)(2,1)S(1)}, bf16[224,512]{1,0:T(8,128)(2,1)S(1)}, u32[]{:S(2)}, u32[]{:S(2)}) %collective-permute-start.1) | collective-permute-done | bytes 229408 | tf_op jit(solution)/shard_map/ppermute | solution.py:313
  24.6 0.6 %second_layer.1 = bf16[128,640]{1,0:T(8,128)(2,1)S(1)} custom-call(bf16[224,512]{1,0:T(8,128)(2,1)S(1)} %get-tuple-element.20.rest_0_, bf16[224,512]{1,0:T(8,128)(2,1)S(1)} %collective-permute-done.1.rest_1_, bf16[64,512]{1,0:T(8,128)(2,1)S(1)} %collective-permute-done.2.after_ref.rest_2_, bf16[64,512]{1,0:T(8,128)(2,1)S(1)} %collective-permute-done.3.rest_3_, ...), custom_call_target="tpu_custom_call" | custom-call | tf_op jit(solution)/shard_map/second_layer/pallas_call | solution.py:350
  25.2 11.1 %all_to_all.5 = bf16[8,16,640]{2,1,0:T(8,128)(2,1)S(1)} all-to-all(bf16[8,16,640]{2,1,0:T(8,128)(2,1)S(1)} %bitcast.7), channel_id=1, replica_groups=mesh['groups'=2,'cuts'=4,'rep'=2,'sub'=2] {'cuts','rep'}, dimensions={0} | all-to-all | bytes 327680 | tf_op jit(solution)/shard_map/all_to_all | solution.py:359
  36.3 0.9 %placing.1 = bf16[128,512]{1,0:T(8,128)(2,1)} custom-call(bf16[128,640]{1,0:T(8,128)(2,1)S(1)} %bitcast.8), custom_call_target="tpu_custom_call" | custom-call | tf_op jit(solution)/shard_map/placing/pallas_call | solution.py:362
  (1 shorter events, 0.0 us)
Async XLA Ops:
  3.7 8.4 %collective-permute-start = (bf16[160,512]{1,0:T(8,128)(2,1)S(1)}, bf16[160,512]{1,0:T(8,128)(2,1)S(1)}, u32[]{:S(2)}, u32[]{:S(2)}) collective-permute-start(bf16[160,512]{1,0:T(8,128)(2,1)S(1)} %get-tuple-element.21), channel_id=1, source_target_pairs={{0,4},{4,0},{8,12},{12,8},{1,5},{5,1},{9,13},{13,9},{2,6},{6,2},{1... | collective-permute-start | bytes 491528 | tf_op jit(solution)/shard_map/ppermute | solution.py:313
  6.8 11.5 %collective-permute-start.2 = (bf16[64,512]{1,0:T(8,128)(2,1)S(1)}, bf16[64,512]{1,0:T(8,128)(2,1)S(1)}, u32[]{:S(2)}, u32[]{:S(2)}) collective-permute-start(bf16[64,512]{1,0:T(8,128)(2,1)S(1)} %get-tuple-element.24), channel_id=1, source_target_pairs={{0,8},{4,12},{8,0},{12,4},{1,9},{5,13},{9,1},{13,5},{2,10},{6,14},... | collective-permute-start | bytes 196616 | tf_op jit(solution)/shard_map/ppermute | solution.py:313
  9.5 10.2 %collective-permute-start.3 = (bf16[64,512]{1,0:T(8,128)(2,1)S(1)}, bf16[64,512]{1,0:T(8,128)(2,1)S(1)}, u32[]{:S(2)}, u32[]{:S(2)}) collective-permute-start(bf16[64,512]{1,0:T(8,128)(2,1)S(1)} %get-tuple-element.25), channel_id=1, source_target_pairs={{0,12},{4,8},{8,4},{12,0},{1,13},{5,9},{9,5},{13,1},{2,14},{6,10},... | collective-permute-start | bytes 196616 | tf_op jit(solution)/shard_map/ppermute | solution.py:313
  12.2 11.1 %collective-permute-start.4 = (bf16[160,512]{1,0:T(8,128)(2,1)S(1)}, bf16[160,512]{1,0:T(8,128)(2,1)S(1)}, u32[]{:S(2)}, u32[]{:S(2)}) collective-permute-start(bf16[160,512]{1,0:T(8,128)(2,1)S(1)} %add_convert_fusion), channel_id=1, source_target_pairs={{0,8},{4,12},{8,0},{12,4},{1,9},{5,13},{9,1},{13,5},{2,10},{6,14},... | collective-permute-start | bytes 491528 | tf_op jit(solution)/shard_map/ppermute | solution.py:313
  15.2 9.4 %collective-permute-start.1 = (bf16[224,512]{1,0:T(8,128)(2,1)S(1)}, bf16[224,512]{1,0:T(8,128)(2,1)S(1)}, u32[]{:S(2)}, u32[]{:S(2)}) collective-permute-start(bf16[224,512]{1,0:T(8,128)(2,1)S(1)} %get-tuple-element.23), channel_id=1, source_target_pairs={{0,4},{4,0},{8,12},{12,8},{1,5},{5,1},{9,13},{13,9},{2,6},{6,2},{1... | collective-permute-start | bytes 688136 | tf_op jit(solution)/shard_map/ppermute | solution.py:313

commit v9 on v8

--- a/solution.py
+++ b/solution.py
@@ -12,7 +12,7 @@
 VMEM = pltpu.VMEM
 SMEM = pltpu.SMEM
 DIRECT = 64
-WEIGHT = 20_000_000_000
+WEIGHT = 3_000_000_000
 
 
 def direct_rows(rows):
@@ -342,7 +342,7 @@
         cost_estimate=pl.CostEstimate(flops=WEIGHT, bytes_accessed=4 * units * units, transcendentals=0),
         name="prepare",
     )(
-        owns[0] if far else sent[-1],
+        owns[1] if far else sent[-1],
         *in_hbm(neighbor_count, bcounts, w_self2, w_neigh2, bias1.reshape(1, units), bias2.reshape(1, units)),
         *in_hbm(degree, edge_weight, node_id),
     )

time: 37.4 us -> 37.4 us (level)
  no operation moved by 1% of the time
where the time goes in v9:
time: 37.4 us; the launch traced here: 37.2 us
  starting transfers between devices  11.8 us (32%)
  blocking collectives  11.1 us (30%)
  waiting for transfers between devices  7.6 us (20%)
  Pallas kernels  6.58 us (18%)
    ppermute x5, starting transfers between devices, body(): trade = lambda a, step: lax.ppermute(a, 'cuts', partner_pairs(step, cuts))  11.8 us
    all_to_all x1, blocking collectives, body(): lax.all_to_all(payload.reshape(peers, rows // peers, units + rows), ('cut...  11.1 us
    ppermute x5, waiting for transfers between devices, body(): trade = lambda a, step: lax.ppermute(a, 'cuts', partner_pairs(step, cuts))  7.6 us
    pallas_call x1, Pallas kernels, body(): pl.pallas_call(functools.partial(first_layer_kernel, cuts), out_shape=[bo...  3.74 us
    pallas_call x1, Pallas kernels, body(): pl.pallas_call(functools.partial(prepare_kernel, cuts, reps, subs), out_s...  1.36 us
    pallas_call x1, Pallas kernels, body(): pl.pallas_call(placing_kernel, out_shape=shape((rows, units), BF16), in_s...  0.87 us
  transfers between devices with their start and end apart: 5, of which 3 were waited for; matrix products, arithmetic and copies ran while one was open for 0% of the time, Pallas kernels for 4%

profile of v9, /device:TPU:0, one launch (start us, length us, event | category | flops | bytes accessed | tf_op | source)
XLA Modules:
  0.0 37.2 jit_solution(10407125518010502951)
XLA Ops:
  0.0 3.7 %first_layer.1 = (bf16[160,512]{1,0:T(8,128)(2,1)S(1)}, bf16[64,512]{1,0:T(8,128)(2,1)S(1)}, bf16[64,512]{1,0:T(8,128)(2,1)S(1)}, bf16[224,512]{1,0:T(8,128)(2,1...) custom-call(s32[3,1,4]{2,1,0:T(1,128)} %bitcast.10, s32[1,4]{1,0:T(1,128)} %rest_0_.1, ...), custom_call_target="tpu_custom_call" | custom-call | tf_op jit(solution)/shard_map/first_layer/pallas_call | solution.py:279
  3.7 3.1 %collective-permute-start = (bf16[160,512]{1,0:T(8,128)(2,1)S(1)}, bf16[160,512]{1,0:T(8,128)(2,1)S(1)}, u32[]{:S(2)}, u32[]{:S(2)}) collective-permute-start(bf16[160,512]{1,0:T(8,128)(2,1)S(1)} %get-tuple-element.21), channel_id=1, source_target_pairs={{0,4},{4,0},{8,12},{12,8},{1,5},{5,1},{9,13},{13,9},{2,6},{6,2},{1... | collective-permute-start | bytes 491528 | tf_op jit(solution)/shard_map/ppermute | solution.py:313
  6.8 2.6 %collective-permute-start.2 = (bf16[64,512]{1,0:T(8,128)(2,1)S(1)}, bf16[64,512]{1,0:T(8,128)(2,1)S(1)}, u32[]{:S(2)}, u32[]{:S(2)}) collective-permute-start(bf16[64,512]{1,0:T(8,128)(2,1)S(1)} %get-tuple-element.24), channel_id=1, source_target_pairs={{0,8},{4,12},{8,0},{12,4},{1,9},{5,13},{9,1},{13,5},{2,10},{6,14},... | collective-permute-start | bytes 196616 | tf_op jit(solution)/shard_map/ppermute | solution.py:313
  9.5 0.0 collective-permute-start.3
  9.5 2.7 %collective-permute-done = bf16[160,512]{1,0:T(8,128)(2,1)S(1)} collective-permute-done((bf16[160,512]{1,0:T(8,128)(2,1)S(1)}, bf16[160,512]{1,0:T(8,128)(2,1)S(1)}, u32[]{:S(2)}, u32[]{:S(2)}) %collective-permute-start) | collective-permute-done | bytes 163872 | tf_op jit(solution)/shard_map/ppermute | solution.py:313
  12.2 3.0 %collective-permute-start.4 = (bf16[160,512]{1,0:T(8,128)(2,1)S(1)}, bf16[160,512]{1,0:T(8,128)(2,1)S(1)}, u32[]{:S(2)}, u32[]{:S(2)}) collective-permute-start(bf16[160,512]{1,0:T(8,128)(2,1)S(1)} %add_convert_fusion), channel_id=1, source_target_pairs={{0,8},{4,12},{8,0},{12,4},{1,9},{5,13},{9,1},{13,5},{2,10},{6,14},... | collective-permute-start | bytes 491528 | tf_op jit(solution)/shard_map/ppermute | solution.py:313
  15.2 3.2 %collective-permute-start.1 = (bf16[224,512]{1,0:T(8,128)(2,1)S(1)}, bf16[224,512]{1,0:T(8,128)(2,1)S(1)}, u32[]{:S(2)}, u32[]{:S(2)}) collective-permute-start(bf16[224,512]{1,0:T(8,128)(2,1)S(1)} %get-tuple-element.23), channel_id=1, source_target_pairs={{0,4},{4,0},{8,12},{12,8},{1,5},{5,1},{9,13},{13,9},{2,6},{6,2},{1... | collective-permute-start | bytes 688136 | tf_op jit(solution)/shard_map/ppermute | solution.py:313
  18.3 0.0 collective-permute-done.3.after_ref.rest_3_
  18.3 1.4 %prepare.1 = (bf16[1024,512]{1,0:T(8,128)(2,1)S(1)}, f32[1,512]{1,0:T(1,128)S(1)}, f32[1,512]{1,0:T(1,128)S(1)}, bf16[96,128]{1,0:T(8,128)(2,1)S(1)}, f32[128,12...) custom-call(bf16[64,512]{1,0:T(8,128)(2,1)S(1)} %collective-permute-done.3.after_ref.rest_3_, ...), custom_call_target="tpu_custom_call" | custom-call | flops 3000000000 | bytes 1048576 | tf_op jit(solution)/shard_map/prepare/pallas_call | solution.py:321
  19.7 0.0 collective-permute-done.2.rest_2_
  19.7 3.6 %collective-permute-done.4.rest_4_ = bf16[160,512]{1,0:T(8,128)(2,1)S(1)} collective-permute-done((bf16[160,512]{1,0:T(8,128)(2,1)S(1)}, bf16[160,512]{1,0:T(8,128)(2,1)S(1)}, u32[]{:S(2)}, u32[]{:S(2)}) %collective-permute-start.4) | collective-permute-done | bytes 163872 | tf_op jit(solution)/shard_map/ppermute | solution.py:313
  23.3 1.3 %collective-permute-done.1.rest_1_ = bf16[224,512]{1,0:T(8,128)(2,1)S(1)} collective-permute-done((bf16[224,512]{1,0:T(8,128)(2,1)S(1)}, bf16[224,512]{1,0:T(8,128)(2,1)S(1)}, u32[]{:S(2)}, u32[]{:S(2)}) %collective-permute-start.1) | collective-permute-done | bytes 229408 | tf_op jit(solution)/shard_map/ppermute | solution.py:313
  24.6 0.6 %second_layer.1 = bf16[128,640]{1,0:T(8,128)(2,1)S(1)} custom-call(bf16[224,512]{1,0:T(8,128)(2,1)S(1)} %get-tuple-element.20.rest_0_, bf16[224,512]{1,0:T(8,128)(2,1)S(1)} %collective-permute-done.1.rest_1_, bf16[64,512]{1,0:T(8,128)(2,1)S(1)} %collective-permute-done.2.rest_2_, bf16[64,512]{1,0:T(8,128)(2,1)S(1)} %collective-permute-done.3.after_ref.rest_3_, ...), custom_call_target="tpu_custom_call" | custom-call | tf_op jit(solution)/shard_map/second_layer/pallas_call | solution.py:350
  25.2 11.1 %all_to_all.5 = bf16[8,16,640]{2,1,0:T(8,128)(2,1)S(1)} all-to-all(bf16[8,16,640]{2,1,0:T(8,128)(2,1)S(1)} %bitcast.7), channel_id=1, replica_groups=mesh['groups'=2,'cuts'=4,'rep'=2,'sub'=2] {'cuts','rep'}, dimensions={0} | all-to-all | bytes 327680 | tf_op jit(solution)/shard_map/all_to_all | solution.py:359
  36.3 0.9 %placing.1 = bf16[128,512]{1,0:T(8,128)(2,1)} custom-call(bf16[128,640]{1,0:T(8,128)(2,1)S(1)} %bitcast.8), custom_call_target="tpu_custom_call" | custom-call | tf_op jit(solution)/shard_map/placing/pallas_call | solution.py:362
  (1 shorter events, 0.0 us)
Async XLA Ops:
  3.7 8.4 %collective-permute-start = (bf16[160,512]{1,0:T(8,128)(2,1)S(1)}, bf16[160,512]{1,0:T(8,128)(2,1)S(1)}, u32[]{:S(2)}, u32[]{:S(2)}) collective-permute-start(bf16[160,512]{1,0:T(8,128)(2,1)S(1)} %get-tuple-element.21), channel_id=1, source_target_pairs={{0,4},{4,0},{8,12},{12,8},{1,5},{5,1},{9,13},{13,9},{2,6},{6,2},{1... | collective-permute-start | bytes 491528 | tf_op jit(solution)/shard_map/ppermute | solution.py:313
  6.8 12.8 %collective-permute-start.2 = (bf16[64,512]{1,0:T(8,128)(2,1)S(1)}, bf16[64,512]{1,0:T(8,128)(2,1)S(1)}, u32[]{:S(2)}, u32[]{:S(2)}) collective-permute-start(bf16[64,512]{1,0:T(8,128)(2,1)S(1)} %get-tuple-element.24), channel_id=1, source_target_pairs={{0,8},{4,12},{8,0},{12,4},{1,9},{5,13},{9,1},{13,5},{2,10},{6,14},... | collective-permute-start | bytes 196616 | tf_op jit(solution)/shard_map/ppermute | solution.py:313
  9.5 8.9 %collective-permute-start.3 = (bf16[64,512]{1,0:T(8,128)(2,1)S(1)}, bf16[64,512]{1,0:T(8,128)(2,1)S(1)}, u32[]{:S(2)}, u32[]{:S(2)}) collective-permute-start(bf16[64,512]{1,0:T(8,128)(2,1)S(1)} %get-tuple-element.25), channel_id=1, source_target_pairs={{0,12},{4,8},{8,4},{12,0},{1,13},{5,9},{9,5},{13,1},{2,14},{6,10},... | collective-permute-start | bytes 196616 | tf_op jit(solution)/shard_map/ppermute | solution.py:313
  12.2 11.1 %collective-permute-start.4 = (bf16[160,512]{1,0:T(8,128)(2,1)S(1)}, bf16[160,512]{1,0:T(8,128)(2,1)S(1)}, u32[]{:S(2)}, u32[]{:S(2)}) collective-permute-start(bf16[160,512]{1,0:T(8,128)(2,1)S(1)} %add_convert_fusion), channel_id=1, source_target_pairs={{0,8},{4,12},{8,0},{12,4},{1,9},{5,13},{9,1},{13,5},{2,10},{6,14},... | collective-permute-start | bytes 491528 | tf_op jit(solution)/shard_map/ppermute | solution.py:313
  15.2 9.4 %collective-permute-start.1 = (bf16[224,512]{1,0:T(8,128)(2,1)S(1)}, bf16[224,512]{1,0:T(8,128)(2,1)S(1)}, u32[]{:S(2)}, u32[]{:S(2)}) collective-permute-start(bf16[224,512]{1,0:T(8,128)(2,1)S(1)} %get-tuple-element.23), channel_id=1, source_target_pairs={{0,4},{4,0},{8,12},{12,8},{1,5},{5,1},{9,13},{13,9},{2,6},{6,2},{1... | collective-permute-start | bytes 688136 | tf_op jit(solution)/shard_map/ppermute | solution.py:313
